TPU v7x, 32 devices: a whole 2x2x4 slice. The times are simulated.
32 devices in a mesh: seq: 8 (over z, x), fsdp: 4 (over y, core).
Axes of the slice: x: 2, y: 2, z: 4, core: 2. Of those that a mesh axis runs over, the one named last changes fastest.
Arguments:
- tokens: bfloat16 [4, 1024, 2560], P('fsdp', 'seq'), may hold values from -6 to 6
- w_x: bfloat16 [2560, 2560], P(('seq', 'fsdp')), may hold values from -0.125 to 0.125
- w_y: bfloat16 [2560, 2560], P(('seq', 'fsdp')), may hold values from -0.125 to 0.125
- w_out: bfloat16 [2560, 2560], P(('seq', 'fsdp')), may hold values from -0.3125 to 0.3125
- gate_w: bfloat16 [2, 256, 2560], P(None, None, ('seq', 'fsdp')), may hold values from -0.375 to 0.375
- gain_in: bfloat16 [2560], P(('seq', 'fsdp')), may hold values from 0.5 to 1.5
- gain_mlp: bfloat16 [2560], P(('seq', 'fsdp')), may hold values from 0.5 to 1.5
- conv_w: bfloat16 [4, 2560], P(None, ('seq', 'fsdp')), may hold values from -3 to 3
- gate_b: bfloat16 [2, 2560], P(None, ('seq', 'fsdp')), may hold values from -3 to 3
- rate: bfloat16 [2560], P(('seq', 'fsdp')), may hold values from 4.863739e-05 to 0.049804688
- w_gate: bfloat16 [2560, 7680], P('seq', 'fsdp'), may hold values from -0.125 to 0.125
- w_up: bfloat16 [2560, 7680], P('seq', 'fsdp'), may hold values from -0.125 to 0.125
- w_down: bfloat16 [7680, 2560], P('fsdp', 'seq'), may hold values from -0.125 to 0.125
- cotangent: bfloat16 [4, 1024, 2560], P('fsdp', 'seq'), may hold values from -6 to 6
Outputs:
- result: bfloat16 [4, 1024, 2560], P('fsdp', 'seq')
- tokens_grad: float32 [4, 1024, 2560], P('fsdp', 'seq')
- grad_w_x: float32 [2560, 2560], P(('seq', 'fsdp'))
- grad_w_y: float32 [2560, 2560], P(('seq', 'fsdp'))
- grad_w_out: float32 [2560, 2560], P(('seq', 'fsdp'))
- grad_gate_w: float32 [2, 256, 2560], P(None, None, ('seq', 'fsdp'))
- grad_gain_in: float32 [2560], P(('seq', 'fsdp'))
- grad_gain_mlp: float32 [2560], P(('seq', 'fsdp'))
- grad_conv_w: float32 [4, 2560], P(None, ('seq', 'fsdp'))
- grad_gate_b: float32 [2, 2560], P(None, ('seq', 'fsdp'))
- grad_rate: float32 [2560], P(('seq', 'fsdp'))
- grad_w_gate: float32 [2560, 7680], P('seq', 'fsdp')
- grad_w_up: float32 [2560, 7680], P('seq', 'fsdp')
- grad_w_down: float32 [7680, 2560], P('fsdp', 'seq')
All inputs are finite; a program needn't handle non-finite values.
Results may differ from a plain program's by a relative error of at most 0.03.
Values may be sent and summed in bfloat16 or wider, within the bound.
No kernel may reach another device: no remote copies, remote signals or barrier semaphores. Data moves between devices by JAX's collectives and lax.ppermute only.
A program may use at most 512 MiB of HBM per device.

v0:
```python
import jax
import jax.numpy as jnp
from jax import lax
from jax.sharding import PartitionSpec as P

HEADS = 10
HD = 256
WIDTH = 4


EPS = 1e-06
PRECISE = lax.Precision.HIGHEST


def passed_along(value, axis, by):
    devices = lax.axis_size(axis)
    pairs = [(i, i + by) for i in range(devices) if 0 <= i + by < devices]
    return lax.ppermute(value, axis, pairs)


def entering(value, axis, join, neutral, backward):
    count, mine = (lax.axis_size(axis), lax.axis_index(axis))
    pieces = jax.tree.map(lambda part: lax.all_gather(part, axis), value)
    if backward:
        pieces = jax.tree.map(lambda part: part[::-1], pieces)
        mine = count - 1 - mine
    total = jax.tree.map(
        lambda part, zero: jnp.full_like(part, 0) + jnp.asarray(zero, part.dtype), value, neutral
    )

    def step(position, total):
        longer = join(total, jax.tree.map(lambda part: part[position], pieces))
        return jax.tree.map(lambda new, old: jnp.where(position < mine, new, old), longer, total)

    return lax.fori_loop(0, count - 1, step, total)


def product(left, right):
    return jnp.dot(left, right, preferred_element_type=jnp.float32)


def rms_scale(values, gain_scale):
    return values * lax.rsqrt(jnp.mean(values * values, axis=-1, keepdims=True) + EPS) * gain_scale


def gelu_tanh(values):
    return jax.nn.gelu(values, approximate=True)


def gated_product(left, right):
    return gelu_tanh(left) * right


def affine_pair(earlier, latter):
    return (earlier[0] * latter[0], earlier[1] * latter[0] + latter[1])


def causal_conv(extended, conv_full, tok_count):
    conv_out = conv_full[0] * extended[WIDTH - 1 : WIDTH - 1 + tok_count]
    for tap_index in range(1, WIDTH):
        conv_out = (
            conv_out
            + conv_full[tap_index]
            * extended[WIDTH - 1 - tap_index : WIDTH - 1 - tap_index + tok_count]
        )
    return conv_out


def recurrence_inputs(conv_out, gate_full, bias_full, rate_full):
    tok_count = conv_out.shape[0]
    blocks = gate_full.reshape(2, HD, HEADS, HD)
    grouped = conv_out.reshape(tok_count, HEADS, HD)
    pre_a = (
        jnp.einsum("thi,ihj->thj", grouped, blocks[0], precision=PRECISE).reshape(tok_count, -1)
        + bias_full[0]
    )
    pre_x = (
        jnp.einsum("thi,ihj->thj", grouped, blocks[1], precision=PRECISE).reshape(tok_count, -1)
        + bias_full[1]
    )
    log_decay = -8.0 * jax.nn.sigmoid(pre_a) * rate_full
    decays = jnp.exp(log_decay)
    drives = jnp.sqrt(-jnp.expm1(2.0 * log_decay)) * jax.nn.sigmoid(pre_x) * conv_out
    return (decays, drives)


def fetch_recurrent(w_x, w_y, w_out, gate_w, gain_in, gain_mlp, conv_w, gate_b, rate):
    return (
        lax.all_gather(w_x, ("seq", "fsdp"), axis=0, tiled=True),
        lax.all_gather(w_y, ("seq", "fsdp"), axis=0, tiled=True),
        lax.all_gather(w_out, ("seq", "fsdp"), axis=0, tiled=True),
        lax.all_gather(gate_w, ("seq", "fsdp"), axis=2, tiled=True),
        lax.all_gather(gain_in, ("seq", "fsdp"), axis=0, tiled=True),
        lax.all_gather(gain_mlp, ("seq", "fsdp"), axis=0, tiled=True),
        lax.all_gather(conv_w, ("seq", "fsdp"), axis=1, tiled=True),
        lax.all_gather(gate_b, ("seq", "fsdp"), axis=1, tiled=True),
        lax.all_gather(rate, ("seq", "fsdp"), axis=0, tiled=True),
    )


def fetch_feedforward(w_gate, w_up, w_down):
    return (
        lax.all_gather(w_gate, "seq", axis=0, tiled=True),
        lax.all_gather(w_up, "seq", axis=0, tiled=True),
        lax.all_gather(w_down, "seq", axis=1, tiled=True),
    )


def split_owner(values, dim, seq_count, pair_count):
    shape = values.shape
    share = shape[dim] // (seq_count * pair_count)
    return values.reshape(shape[:dim] + (seq_count, pair_count, share) + shape[dim + 1 :])


def merge_owner(values, dim):
    shape = values.shape
    return values.reshape(shape[:dim] + (shape[dim + 2],) + shape[dim + 3 :])


def sum_recurrent(grads):
    seq_count = lax.axis_size("seq")
    pair_count = lax.axis_size("fsdp")
    dims = (0, 0, 0, 2, 0, 0, 1, 1, 0)
    split = tuple((split_owner(item, dim, seq_count, pair_count) for item, dim in zip(grads, dims)))
    paired = (
        lax.psum_scatter(split[0], "fsdp", scatter_dimension=1, tiled=True),
        lax.psum_scatter(split[1], "fsdp", scatter_dimension=1, tiled=True),
        lax.psum_scatter(split[2], "fsdp", scatter_dimension=1, tiled=True),
        lax.psum_scatter(split[3], "fsdp", scatter_dimension=3, tiled=True),
        lax.psum_scatter(split[4], "fsdp", scatter_dimension=1, tiled=True),
        lax.psum_scatter(split[5], "fsdp", scatter_dimension=1, tiled=True),
        lax.psum_scatter(split[6], "fsdp", scatter_dimension=2, tiled=True),
        lax.psum_scatter(split[7], "fsdp", scatter_dimension=2, tiled=True),
        lax.psum_scatter(split[8], "fsdp", scatter_dimension=1, tiled=True),
    )
    summed = (
        lax.psum_scatter(paired[0], "seq", scatter_dimension=0, tiled=True),
        lax.psum_scatter(paired[1], "seq", scatter_dimension=0, tiled=True),
        lax.psum_scatter(paired[2], "seq", scatter_dimension=0, tiled=True),
        lax.psum_scatter(paired[3], "seq", scatter_dimension=2, tiled=True),
        lax.psum_scatter(paired[4], "seq", scatter_dimension=0, tiled=True),
        lax.psum_scatter(paired[5], "seq", scatter_dimension=0, tiled=True),
        lax.psum_scatter(paired[6], "seq", scatter_dimension=1, tiled=True),
        lax.psum_scatter(paired[7], "seq", scatter_dimension=1, tiled=True),
        lax.psum_scatter(paired[8], "seq", scatter_dimension=0, tiled=True),
    )
    return tuple((merge_owner(item, dim) for item, dim in zip(summed, dims)))


def per_device(
    tokens,
    w_x,
    w_y,
    w_out,
    gate_w,
    gain_in,
    gain_mlp,
    conv_w,
    gate_b,
    rate,
    w_gate,
    w_up,
    w_down,
    cotangent,
):
    gathered = fetch_recurrent(w_x, w_y, w_out, gate_w, gain_in, gain_mlp, conv_w, gate_b, rate)
    full_x, full_y, full_out = (gathered[0], gathered[1], gathered[2])
    gate_f = gathered[3].astype(jnp.float32)
    gain_first = gathered[4].astype(jnp.float32)
    gain_second = gathered[5].astype(jnp.float32)
    conv_f = gathered[6].astype(jnp.float32)
    bias_f = gathered[7].astype(jnp.float32)
    rate_f = gathered[8].astype(jnp.float32)
    slice_gate, slice_up, slice_down = fetch_feedforward(w_gate, w_up, w_down)
    tok_rows = tokens[0].astype(jnp.float32)
    tok_count = tok_rows.shape[0]
    model_width = tok_rows.shape[1]
    width_r = full_x.shape[1]
    normed = rms_scale(tok_rows, gain_first).astype(jnp.bfloat16)
    branch_x = product(normed, full_x).astype(jnp.bfloat16)
    branch_y = product(normed, full_y)
    carried = passed_along(branch_x[tok_count - (WIDTH - 1) :], "seq", 1)
    extended = jnp.concatenate([carried, branch_x], axis=0).astype(jnp.float32)
    conv_out = causal_conv(extended, conv_f, tok_count)
    decays, drives = recurrence_inputs(conv_out, gate_f, bias_f, rate_f)
    cum_decay, local_state = lax.associative_scan(affine_pair, (decays, drives), axis=0)
    ones_r = jnp.ones((width_r,), jnp.float32)
    zeros_r = jnp.zeros((width_r,), jnp.float32)
    carry_in = entering(
        (cum_decay[-1], local_state[-1]), "seq", affine_pair, (ones_r, zeros_r), False
    )
    state_in = carry_in[1]
    states = local_state + cum_decay * state_in
    gate_y = gelu_tanh(branch_y)
    mixed_rows = (states * gate_y).astype(jnp.bfloat16)
    residual = tok_rows + product(mixed_rows, full_out)
    normed_mlp = rms_scale(residual, gain_second).astype(jnp.bfloat16)
    rows_all = lax.all_gather(normed_mlp[None], "fsdp", axis=0, tiled=True).reshape(-1, model_width)
    gate_pre = product(rows_all, slice_gate)
    up_proj = product(rows_all, slice_up)
    hidden = gated_product(gate_pre, up_proj).astype(jnp.bfloat16)
    mlp_out = lax.psum_scatter(product(hidden, slice_down), "fsdp", scatter_dimension=0, tiled=True)
    result = (residual + mlp_out).astype(jnp.bfloat16)[None]
    fresh = lax.optimization_barrier((w_x, w_y, w_out, w_gate, w_up, w_down, mlp_out))
    again = fetch_recurrent(
        fresh[0], fresh[1], fresh[2], gate_w, gain_in, gain_mlp, conv_w, gate_b, rate
    )
    full_x, full_y, full_out = (again[0], again[1], again[2])
    slice_gate, slice_up, slice_down = fetch_feedforward(fresh[3], fresh[4], fresh[5])
    grad_rows = cotangent[0].astype(jnp.float32)
    grad_all = lax.all_gather(cotangent, "fsdp", axis=0, tiled=True).reshape(-1, model_width)
    d_hidden = product(grad_all, slice_down.T)
    grad_down = product(hidden.T, grad_all)
    unused, mlp_pull = jax.vjp(gated_product, gate_pre, up_proj)
    d_gate_f, d_up_f = mlp_pull(d_hidden)
    d_gate = d_gate_f.astype(jnp.bfloat16)
    d_up = d_up_f.astype(jnp.bfloat16)
    grad_gate = product(rows_all.T, d_gate)
    grad_up = product(rows_all.T, d_up)
    feed_grads = (
        lax.psum_scatter(grad_gate, "seq", scatter_dimension=0, tiled=True),
        lax.psum_scatter(grad_up, "seq", scatter_dimension=0, tiled=True),
        lax.psum_scatter(grad_down, "seq", scatter_dimension=1, tiled=True),
    )
    d_normed_mlp = lax.psum_scatter(
        product(d_gate, slice_gate.T) + product(d_up, slice_up.T),
        "fsdp",
        scatter_dimension=0,
        tiled=True,
    )
    unused, second_pull = jax.vjp(rms_scale, residual, gain_second)
    d_res_norm, d_gain_mlp = second_pull(d_normed_mlp)
    d_residual = grad_rows + d_res_norm
    d_branch = d_residual.astype(jnp.bfloat16)
    grad_out = product(mixed_rows.T, d_branch)
    d_mixed = product(d_branch, full_out.T)
    d_states = d_mixed * gate_y
    unused, y_pull = jax.vjp(gelu_tanh, branch_y)
    d_branch_y = y_pull(d_mixed * states)[0].astype(jnp.bfloat16)
    flipped = decays[::-1]
    coeffs = jnp.concatenate([jnp.ones((1, width_r), jnp.float32), flipped[:-1]], axis=0)
    cum_back, local_back = lax.associative_scan(affine_pair, (coeffs, d_states[::-1]), axis=0)
    outgoing = (cum_back[-1] * flipped[-1], local_back[-1] * flipped[-1])
    carry_back = entering(outgoing, "seq", affine_pair, (ones_r, zeros_r), True)
    state_grad = (local_back + cum_back * carry_back[1])[::-1]
    before = jnp.concatenate([state_in[None], states[:-1]], axis=0)
    unused, gate_pull = jax.vjp(recurrence_inputs, conv_out, gate_f, bias_f, rate_f)
    d_conv, d_gate_w, d_bias, d_rate = gate_pull((state_grad * before, state_grad))

    def conv_only(ext_rows, taps):
        return causal_conv(ext_rows, taps, tok_count)

    unused, conv_pull = jax.vjp(conv_only, extended, conv_f)
    d_extended, grad_conv = conv_pull(d_conv)
    rim_back = passed_along(d_extended[: WIDTH - 1], "seq", -1)
    d_branch_x = (
        d_extended[WIDTH - 1 :] + jnp.pad(rim_back, ((tok_count - (WIDTH - 1), 0), (0, 0)))
    ).astype(jnp.bfloat16)
    grad_x = product(normed.T, d_branch_x)
    grad_y = product(normed.T, d_branch_y)
    d_normed = product(d_branch_x, full_x.T) + product(d_branch_y, full_y.T)
    unused, first_pull = jax.vjp(rms_scale, tok_rows, gain_first)
    d_tok, d_gain_in = first_pull(d_normed)
    tokens_grad = (d_residual + d_tok)[None]
    recurrent_grads = sum_recurrent(
        (grad_x, grad_y, grad_out, d_gate_w, d_gain_in, d_gain_mlp, grad_conv, d_bias, d_rate)
    )
    return (
        result,
        tokens_grad,
        recurrent_grads[0],
        recurrent_grads[1],
        recurrent_grads[2],
        recurrent_grads[3],
        recurrent_grads[4],
        recurrent_grads[5],
        recurrent_grads[6],
        recurrent_grads[7],
        recurrent_grads[8],
        feed_grads[0],
        feed_grads[1],
        feed_grads[2],
    )


def solution(mesh):
    placed = (
        P("fsdp", "seq", None),
        P(("seq", "fsdp"), None),
        P(("seq", "fsdp"), None),
        P(("seq", "fsdp"), None),
        P(None, None, ("seq", "fsdp")),
        P(("seq", "fsdp")),
        P(("seq", "fsdp")),
        P(None, ("seq", "fsdp")),
        P(None, ("seq", "fsdp")),
        P(("seq", "fsdp")),
        P("seq", "fsdp"),
        P("seq", "fsdp"),
        P("fsdp", "seq"),
        P("fsdp", "seq", None),
    )
    return jax.shard_map(
        per_device,
        mesh=mesh,
        in_specs=placed,
        out_specs=(
            P("fsdp", "seq", None),
            P("fsdp", "seq", None),
            P(("seq", "fsdp"), None),
            P(("seq", "fsdp"), None),
            P(("seq", "fsdp"), None),
            P(None, None, ("seq", "fsdp")),
            P(("seq", "fsdp")),
            P(("seq", "fsdp")),
            P(None, ("seq", "fsdp")),
            P(None, ("seq", "fsdp")),
            P(("seq", "fsdp")),
            P("seq", "fsdp"),
            P("seq", "fsdp"),
            P("fsdp", "seq"),
        ),
        check_vma=False,
    )
```

profile of v0, /device:TPU:0, one launch (start us, length us, event | category | flops | bytes accessed | tf_op | source)
XLA Modules:
  0.0 4647.7 jit_solution(8309483232184199007)
XLA Ops:
  11.7 43.5 all-reduce.89
  55.8 40.1 all-gather.2
  96.1 36.7 all-gather.1
  141.4 31.1 all-gather.25.cloned.1.call-done
  285.9 30.8 all-gather.4
  322.5 31.2 all-gather.3
  361.4 10.1 multiply_convert_fusion.2
  383.2 133.7 %all-gather.31.cloned.1.call-done = bf16[2560,1920]{1,0:T(8,128)(2,1)} async-done(((bf16[320,1920]{1,0:T(8,128)(2,1)}), bf16[2560,1920]{1,0:T(8,128)(2,1)}) %all-gather.31.cloned.1.call-update) | async-done | bytes 9830416 | tf_op jit(solution)/shard_map/all_gather | solution.py:103
  516.9 25.8 all-gather.51.cloned.1.call-done
  542.6 11.4 fusion.86
  554.0 133.7 %all-gather.33.cloned.1.call-done = bf16[2560,1920]{1,0:T(8,128)(2,1)} async-done(((bf16[320,1920]{1,0:T(8,128)(2,1)}), bf16[2560,1920]{1,0:T(8,128)(2,1)}) %all-gather.33.cloned.1.call-update) | async-done | bytes 9830416 | tf_op jit(solution)/shard_map/all_gather | solution.py:104
  687.7 12.2 multiply_convert_fusion
  700.0 131.0 %all-gather.35.cloned.1.call-done = bf16[1920,2560]{0,1:T(8,128)(2,1)} async-done(((bf16[1920,320]{0,1:T(8,128)(2,1)}), bf16[1920,2560]{0,1:T(8,128)(2,1)}) %all-gather.35.cloned.1.call-update) | async-done | bytes 9830416 | tf_op jit(solution)/shard_map/all_gather | solution.py:105
  831.0 10.3 fusion.87
  842.0 49.1 %reduce-scatter.18.cloned.1.call-done = f32[128,2560]{1,0:T(8,128)} async-done(((f32[512,2560]{1,0:T(8,128)}), f32[128,2560]{1,0:T(8,128)}) %reduce-scatter.18.cloned.1.call-update) | async-done | bytes 1310736 | tf_op jit(solution)/shard_map/reduce_scatter | solution.py:202
  892.4 25.7 all-gather.39.cloned.1.call-done
  918.1 145.3 %all-gather.37.cloned.1.call-done = bf16[1920,2560]{0,1:T(8,128)(2,1)} async-done(((bf16[1920,320]{0,1:T(8,128)(2,1)}), bf16[1920,2560]{0,1:T(8,128)(2,1)}) %all-gather.37.cloned.1.call-update) | async-done | bytes 9830416 | tf_op jit(solution)/shard_map/all_gather | solution.py:105
  1063.4 15.1 fusion.7
  1078.6 128.2 %all-gather.41.cloned.1.call-done = bf16[2560,1920]{1,0:T(8,128)(2,1)} async-done(((bf16[320,1920]{1,0:T(8,128)(2,1)}), bf16[2560,1920]{1,0:T(8,128)(2,1)}) %all-gather.41.cloned.1.call-update) | async-done | bytes 9830416 | tf_op jit(solution)/shard_map/all_gather | solution.py:103
  1206.8 10.4 fusion.88
  1217.1 133.1 %all-gather.43.cloned.1.call-done = bf16[2560,1920]{1,0:T(8,128)(2,1)} async-done(((bf16[320,1920]{1,0:T(8,128)(2,1)}), bf16[2560,1920]{1,0:T(8,128)(2,1)}) %all-gather.43.cloned.1.call-update) | async-done | bytes 9830416 | tf_op jit(solution)/shard_map/all_gather | solution.py:104
  1350.3 11.1 convolution_add_fusion
  1373.2 10.8 slice.585
  1384.0 9.9 slice.630
  1399.8 9.9 slice.580
  1416.8 95.6 %all-gather.45.cloned.1.call-done = bf16[2560,2560]{1,0:T(8,128)(2,1)} async-done(((bf16[80,2560]{1,0:T(8,128)(2,1)}), bf16[2560,2560]{1,0:T(8,128)(2,1)}) %all-gather.45.cloned.1.call-update) | async-done | bytes 13107216 | tf_op jit(solution)/shard_map/all_gather | solution.py:91
  1512.4 11.3 fusion.38
  1528.5 9.9 slice.577
  1608.4 30.7 all-gather.6
  1645.1 31.0 all-gather.5
  1687.6 10.9 rev.13
  1736.7 10.4 fusion.90
  1747.1 10.9 fusion.41
  1773.9 10.6 fusion.34
  1784.5 10.7 fusion.36
  1797.0 11.9 fusion.93
  1810.5 11.6 fusion.92
  1823.6 11.5 fusion.91
  1836.3 1332.0 %all-reduce.92.cloned.1.call-done = (f32[8,4,80,2560]{3,2,1,0:T(8,128)}, f32[8,4,80,2560]{3,2,1,0:T(8,128)}, f32[8,4,80,2560]{3,2,1,0:T(8,128)}, f32[2,256,8,4,80]{1,4,0,3,2:T(8,128)}) async-done(((f32[8,4,80,2560]{3,2,1,0:T(8,128)}, f32[8,4,80,2560]{3,2,1,0:T(8,128)}, f32[8,4,80,2560]{3,2,1,0:T(8,128)}, f32[2,256,8,4,80]{1,4,0,3,2:T(8,128)}), (f32[8,4,80,2560]{3,2,1,0:T(8,128)}, ...) | async-done | bytes 83886096
  3193.3 10.6 all-reduce.87
  3212.6 39.5 all-reduce.86
  3258.2 283.3 %reduce-scatter.38.cloned.1.call-done = f32[1920,320]{0,1:T(8,128)} async-done(((f32[1920,2560]{0,1:T(8,128)}), f32[1920,320]{0,1:T(8,128)}) %reduce-scatter.38.cloned.1.call-update) | async-done | bytes 2457616 | tf_op jit(solution)/shard_map/reduce_scatter | solution.py:223
  3541.6 328.3 %reduce-scatter.36.cloned.1.call-done = f32[320,1920]{1,0:T(8,128)} async-done(((f32[2560,1920]{1,0:T(8,128)}), f32[320,1920]{1,0:T(8,128)}) %reduce-scatter.36.cloned.1.call-update) | async-done | bytes 2457616 | tf_op jit(solution)/shard_map/reduce_scatter | solution.py:222
  3869.9 328.3 %reduce-scatter.34.cloned.1.call-done = f32[320,1920]{1,0:T(8,128)} async-done(((f32[2560,1920]{1,0:T(8,128)}), f32[320,1920]{1,0:T(8,128)}) %reduce-scatter.34.cloned.1.call-update) | async-done | bytes 2457616 | tf_op jit(solution)/shard_map/reduce_scatter | solution.py:221
  4198.2 67.3 %reduce-scatter.28.cloned.1.call-done = f32[2,256,1,1,80]{1,4,0,3,2:T(8,128)} async-done(((f32[2,256,8,1,80]{1,4,0,3,2:T(8,128)}), f32[2,256,1,1,80]{1,4,0,3,2:T(8,128)}) %reduce-scatter.28.cloned.1.call-update) | async-done | bytes 163856 | tf_op jit(solution)/shard_map/reduce_scatter | solution.py:140
  4265.6 124.9 %reduce-scatter.22.cloned.1.call-done = f32[1,1,80,2560]{3,2,1,0:T(8,128)} async-done(((f32[8,1,80,2560]{3,2,1,0:T(8,128)}), f32[1,1,80,2560]{3,2,1,0:T(8,128)}) %reduce-scatter.22.cloned.1.call-update) | async-done | bytes 819216 | tf_op jit(solution)/shard_map/reduce_scatter | solution.py:137
  4390.5 125.3 %reduce-scatter.26.cloned.1.call-done = f32[1,1,80,2560]{3,2,1,0:T(8,128)} async-done(((f32[8,1,80,2560]{3,2,1,0:T(8,128)}), f32[1,1,80,2560]{3,2,1,0:T(8,128)}) %reduce-scatter.26.cloned.1.call-update) | async-done | bytes 819216 | tf_op jit(solution)/shard_map/reduce_scatter | solution.py:139
  4515.8 124.8 %reduce-scatter.24.cloned.1.call-done = f32[1,1,80,2560]{3,2,1,0:T(8,128)} async-done(((f32[8,1,80,2560]{3,2,1,0:T(8,128)}), f32[1,1,80,2560]{3,2,1,0:T(8,128)}) %reduce-scatter.24.cloned.1.call-update) | async-done | bytes 819216 | tf_op jit(solution)/shard_map/reduce_scatter | solution.py:138
  (582 shorter events, 383.1 us)
Async XLA Ops:
  7.2 125.9 %all-gather.23.cloned.1.call-start = ((), (), s32[]{:S(2)}) async-start(), calls=%async_computation.11 | async-start | bytes 13516800 | tf_op jit(solution)/shard_map/all_gather | solution.py:89
  7.9 164.5 %all-gather.25.cloned.1.call-start = ((), (), s32[]{:S(2)}) async-start(), calls=%async_computation.12 | async-start | bytes 2703360 | tf_op jit(solution)/shard_map/all_gather | solution.py:92
  8.7 352.7 %all-gather.27.cloned.1.call-start = ((), (), s32[]{:S(2)}) async-start(), calls=%async_computation.13 | async-start | bytes 13516800 | tf_op jit(solution)/shard_map/all_gather | solution.py:90
  9.4 46.4 copy-start.76
  9.4 86.7 %copy-start.75 = (bf16[4,80]{1,0:T(4,128)(2,1)S(1)}, bf16[4,80]{1,0:T(4,128)(2,1)}, u32[]{:S(2)}) copy-start(bf16[4,80]{1,0:T(4,128)(2,1)} %param.25) | copy-start | bytes 1924
  9.5 364.2 %all-gather.29.cloned.1.call-start = ((), (), s32[]{:S(2)}) async-start(), calls=%async_computation.14 | async-start | bytes 13516800 | tf_op jit(solution)/shard_map/all_gather | solution.py:91
  10.0 506.8 %all-gather.31.cloned.1.call-start = ((), (), s32[]{:S(2)}) async-start(), calls=%async_computation.15 | async-start | bytes 11059200 | tf_op jit(solution)/shard_map/all_gather | solution.py:103
  10.6 532.0 %all-gather.51.cloned.1.call-start = ((), (), s32[]{:S(2)}) async-start(), calls=%async_computation.36 | async-start | bytes 3276800 | tf_op jit(solution)/shard_map/all_gather | solution.py:198
  10.9 128.8 %copy-start.73 = (f32[128]{0:T(128)}, f32[128]{0:T(128)S(1)}, u32[]{:S(2)}) copy-start(f32[128]{0:T(128)S(1)} %fusion.69) | copy-start | bytes 1540
  55.2 306.2 %copy-start.39 = (f32[2560]{0:T(1024)}, f32[2560]{0:T(1024)S(1)}, u32[]{:S(2)}) copy-start(f32[2560]{0:T(1024)S(1)} %convert_element_type.69) | copy-start | bytes 30724
  55.8 142.9 %copy-start.52 = (f32[2560]{0:T(1024)}, f32[2560]{0:T(1024)S(1)}, u32[]{:S(2)}) copy-start(f32[2560]{0:T(1024)S(1)} %broadcast_multiply_fusion.4) | copy-start | bytes 30724
  96.1 102.7 %copy-start.54 = (f32[2560]{0:T(1024)}, f32[2560]{0:T(1024)S(1)}, u32[]{:S(2)}) copy-start(f32[2560]{0:T(1024)S(1)} %get-tuple-element.264) | copy-start | bytes 30724
  96.1 102.6 %copy-start.56 = (f32[2560]{0:T(1024)}, f32[2560]{0:T(1024)S(1)}, u32[]{:S(2)}) copy-start(f32[2560]{0:T(1024)S(1)} %get-tuple-element.265) | copy-start | bytes 30724
  133.1 65.7 %copy-start.43 = (f32[2560]{0:T(1024)}, f32[2560]{0:T(1024)S(1)}, u32[]{:S(2)}) copy-start(f32[2560]{0:T(1024)S(1)} %get-tuple-element.260) | copy-start | bytes 30724
  133.1 65.7 %copy-start.45 = (f32[2560]{0:T(1024)}, f32[2560]{0:T(1024)S(1)}, u32[]{:S(2)}) copy-start(f32[2560]{0:T(1024)S(1)} %get-tuple-element.261) | copy-start | bytes 30724
  133.1 65.7 %copy-start.47 = (f32[2560]{0:T(1024)}, f32[2560]{0:T(1024)S(1)}, u32[]{:S(2)}) copy-start(f32[2560]{0:T(1024)S(1)} %get-tuple-element.262) | copy-start | bytes 30724
  133.1 65.7 %copy-start.49 = (f32[2560]{0:T(1024)}, f32[2560]{0:T(1024)S(1)}, u32[]{:S(2)}) copy-start(f32[2560]{0:T(1024)S(1)} %get-tuple-element.263) | copy-start | bytes 30724
  139.8 36.0 collective-permute-start
  381.6 306.1 %all-gather.33.cloned.1.call-start = ((), (), s32[]{:S(2)}) async-start(), calls=%async_computation.16 | async-start | bytes 11059200 | tf_op jit(solution)/shard_map/all_gather | solution.py:104
  382.4 448.6 %all-gather.35.cloned.1.call-start = ((), (), s32[]{:S(2)}) async-start(), calls=%async_computation.17 | async-start | bytes 11059200 | tf_op jit(solution)/shard_map/all_gather | solution.py:105
  383.1 507.9 %reduce-scatter.18.cloned.1.call-start = ((), (), s32[]{:S(2)}) async-start(), calls=%async_computation.18 | async-start | bytes 6553600 | tf_op jit(solution)/shard_map/reduce_scatter | solution.py:202
  841.3 76.8 %all-gather.39.cloned.1.call-start = ((), (), s32[]{:S(2)}) async-start(), calls=%async_computation.20 | async-start | bytes 3276800 | tf_op jit(solution)/shard_map/all_gather | solution.py:211
  841.9 221.5 %all-gather.37.cloned.1.call-start = ((), (), s32[]{:S(2)}) async-start(), calls=%async_computation.19 | async-start | bytes 11059200 | tf_op jit(solution)/shard_map/all_gather | solution.py:105
  891.1 315.7 %all-gather.41.cloned.1.call-start = ((), (), s32[]{:S(2)}) async-start(), calls=%async_computation.21 | async-start | bytes 11059200 | tf_op jit(solution)/shard_map/all_gather | solution.py:103
  891.6 458.6 %all-gather.43.cloned.1.call-start = ((), (), s32[]{:S(2)}) async-start(), calls=%async_computation.22 | async-start | bytes 11059200 | tf_op jit(solution)/shard_map/all_gather | solution.py:104
  892.4 518.8 %reduce-scatter.20.cloned.1.call-start = ((), (), s32[]{:S(2)}) async-start(), calls=%async_computation.23 | async-start | bytes 6553600 | tf_op jit(solution)/shard_map/reduce_scatter | solution.py:225
  1361.4 151.0 %all-gather.45.cloned.1.call-start = ((), (), s32[]{:S(2)}) async-start(), calls=%async_computation.24 | async-start | bytes 13516800 | tf_op jit(solution)/shard_map/all_gather | solution.py:91
  1362.0 374.7 %all-gather.49.cloned.1.call-start = ((), (), s32[]{:S(2)}) async-start(), calls=%async_computation.26 | async-start | bytes 13516800 | tf_op jit(solution)/shard_map/all_gather | solution.py:90
  1362.6 398.4 %all-gather.47.cloned.1.call-start = ((), (), s32[]{:S(2)}) async-start(), calls=%async_computation.25 | async-start | bytes 13516800 | tf_op jit(solution)/shard_map/all_gather | solution.py:89
  1409.7 1758.5 %all-reduce.92.cloned.1.call-start = ((), (), s32[]{:S(2)}) async-start(), calls=%async_computation.37 | async-start | bytes 167772160
  1687.5 10.9 copy-start.46
  1687.5 10.9 copy-start.48
  1687.5 11.0 copy-start.50
  1687.5 11.0 copy-start.53
  1687.5 11.0 copy-start.55
  1687.5 11.0 copy-start.57
  1687.5 11.0 copy-start.59
  1687.5 11.0 copy-start.60
  1727.1 33.9 collective-permute-start.1
  1795.2 1410.7 %reduce-scatter.32.cloned.1.call-start = ((), (), s32[]{:S(2)}) async-start(), calls=%async_computation.32 | async-start | bytes 40960 | tf_op jit(solution)/shard_map/reduce_scatter | solution.py:133
  1796.1 1415.8 %reduce-scatter.30.cloned.1.call-start = ((), (), s32[]{:S(2)}) async-start(), calls=%async_computation.31 | async-start | bytes 81920 | tf_op jit(solution)/shard_map/reduce_scatter | solution.py:132
  1797.0 1744.6 %reduce-scatter.38.cloned.1.call-start = ((), (), s32[]{:S(2)}) async-start(), calls=%async_computation.35 | async-start | bytes 22118400 | tf_op jit(solution)/shard_map/reduce_scatter | solution.py:223
  1808.9 2061.0 %reduce-scatter.36.cloned.1.call-start = ((), (), s32[]{:S(2)}) async-start(), calls=%async_computation.34 | async-start | bytes 22118400 | tf_op jit(solution)/shard_map/reduce_scatter | solution.py:222
  1822.1 2376.2 %reduce-scatter.34.cloned.1.call-start = ((), (), s32[]{:S(2)}) async-start(), calls=%async_computation.33 | async-start | bytes 22118400 | tf_op jit(solution)/shard_map/reduce_scatter | solution.py:221
  1835.1 2430.5 %reduce-scatter.28.cloned.1.call-start = ((), (), s32[]{:S(2)}) async-start(), calls=%async_computation.30 | async-start | bytes 1474560 | tf_op jit(solution)/shard_map/reduce_scatter | solution.py:140
  3171.4 1219.1 %reduce-scatter.22.cloned.1.call-start = ((), (), s32[]{:S(2)}) async-start(), calls=%async_computation.27 | async-start | bytes 7372800 | tf_op jit(solution)/shard_map/reduce_scatter | solution.py:137
  3178.1 1337.6 %reduce-scatter.26.cloned.1.call-start = ((), (), s32[]{:S(2)}) async-start(), calls=%async_computation.29 | async-start | bytes 7372800 | tf_op jit(solution)/shard_map/reduce_scatter | solution.py:139
  3184.8 1455.8 %reduce-scatter.24.cloned.1.call-start = ((), (), s32[]{:S(2)}) async-start(), calls=%async_computation.28 | async-start | bytes 7372800 | tf_op jit(solution)/shard_map/reduce_scatter | solution.py:138
  (67 other events, 226.6 us)
Sparse Core Ops, SparseCore 0:
  10.9 102.2 all-gather.22
  116.0 56.4 all-gather.24
  175.3 97.4 all-gather.26
  275.5 98.1 all-gather.28
  375.7 141.1 all-gather.30
  518.9 23.7 all-gather.50
  544.8 142.8 all-gather.32
  689.9 141.0 all-gather.34
  841.4 49.5 reduce-scatter.17
  892.5 25.5 all-gather.38
  920.6 142.8 all-gather.36
  1065.7 141.0 all-gather.40
  1209.2 141.0 all-gather.42
  1361.5 49.5 reduce-scatter.19
  1413.8 98.5 all-gather.44
  1515.1 96.7 all-gather.48
  1614.6 97.5 all-gather.46
  1795.3 1372.9 all-reduce.91
  3170.7 19.3 reduce-scatter.31
  3192.4 19.4 reduce-scatter.29
  3216.4 325.1 reduce-scatter.37
  3546.1 323.7 reduce-scatter.35
  3874.4 323.8 reduce-scatter.33
  4202.1 63.4 reduce-scatter.27
  4269.7 120.6 reduce-scatter.21
  4394.9 120.7 reduce-scatter.25
  4519.8 120.7 reduce-scatter.23
where the time goes:
time: 4660 us; the launch traced here: 4650 us
  waiting for transfers between devices  3760 us (81%)
  blocking collectives  294 us (6%)
  local copies, waits for them, and re-layouts  287 us (6%)
  matrix products  214 us (5%)
  other arithmetic  68.9 us (1%)
    unnamed x28, waiting for transfers between devices  1340 us
    reduce_scatter x1, waiting for transfers between devices, per_device(): lax.psum_scatter(grad_gate, 'seq', scatter_dimension=0, tiled=True)  328 us
    reduce_scatter x1, waiting for transfers between devices, per_device(): lax.psum_scatter(grad_up, 'seq', scatter_dimension=0, tiled=True)  328 us
    reduce_scatter x1, waiting for transfers between devices, per_device(): lax.psum_scatter(grad_down, 'seq', scatter_dimension=1, tiled=True)  283 us
    all_gather x2, waiting for transfers between devices, fetch_feedforward(): lax.all_gather(w_down, 'seq', axis=1, tiled=True)  276 us
    all_gather x2, waiting for transfers between devices, fetch_feedforward(): lax.all_gather(w_up, 'seq', axis=0, tiled=True)  267 us
    all_gather x2, waiting for transfers between devices, fetch_feedforward(): lax.all_gather(w_gate, 'seq', axis=0, tiled=True)  262 us
    dot_general x18, matrix products, product(): return jnp.dot(left, right, preferred_element_type=jnp.float32)  193 us
  transfers between devices with their start and end apart: 29, of which 22 were waited for; matrix products, arithmetic and copies ran while one was open for 11% of the time, Pallas kernels for 0%

commit v1 on v0

v1 whole, which is shorter than its diff:
```python
import functools

import jax
import jax.numpy as jnp
from jax import lax
from jax.experimental import pallas as pl
from jax.experimental.pallas import tpu as pltpu
from jax.sharding import Mesh
from jax.sharding import PartitionSpec as P

HEADS = 10
HD = 256
WIDTH = 4
HALO = 16
EPS = 1e-06
BF = jnp.bfloat16
F32 = jnp.float32


def swap(value, axis):
    return lax.ppermute(value, axis, [(0, 1), (1, 0)])


def shifted(value, axes, by, count, wrap=False):
    pairs = [(i, (i + by) % count) for i in range(count) if wrap or 0 <= i + by < count]
    return lax.ppermute(value, axes, pairs)


def pick(flag, first, second):
    return jnp.where(flag, first, second)


def cycle(length):
    return [z * 2 for z in range(length)] + [z * 2 + 1 for z in reversed(range(length))]


def around(length):
    walk = cycle(length)
    count = len(walk)
    forth = [(walk[i], walk[(i + 1) % count]) for i in range(count)]
    back = [(j, i) for i, j in forth]
    return walk, forth, back


def place_in(walk, index):
    inverse = [0] * len(walk)
    for position, linear in enumerate(walk):
        inverse[linear] = position
    return jnp.asarray(inverse, jnp.int32)[index]


def after(value, other):
    return lax.optimization_barrier((value, other))[0]


def dot(left, right, dims):
    return lax.dot_general(left, right, (dims, ((), ())), preferred_element_type=F32)


def product(left, right):
    return dot(left, right, ((1,), (0,)))


def product_t(left, right):
    return dot(left, right, ((1,), (1,)))


def t_product(left, right):
    return dot(left, right, ((0,), (0,)))


def rms_scale(values, gain_scale):
    return values * lax.rsqrt(jnp.mean(values * values, axis=-1, keepdims=True) + EPS) * gain_scale


def gelu_tanh(values):
    return jax.nn.gelu(values, approximate=True)


def gated_product(left, right):
    return gelu_tanh(left) * right


def gelu_both(v):
    inner = 0.7978845608028654 * (v + 0.044715 * v * v * v)
    th = jnp.tanh(inner)
    value = 0.5 * v * (1.0 + th)
    slope = 0.5 * (1.0 + th) + 0.5 * v * (1.0 - th * th) * 0.7978845608028654 * (1.0 + 0.134145 * v * v)
    return value, slope


def minus_expm1(v):
    series = jnp.full_like(v, 1.0)
    for n in range(11, 1, -1):
        series = 1.0 + series * v * (1.0 / n)
    return jnp.where(v > -1.0, -v * series, 1.0 - jnp.exp(v))


def two_parts(v):
    high = v.astype(BF)
    return high, (v - high.astype(F32)).astype(BF)


def wide_dot(left, right, dims):
    high, low = two_parts(left)
    return dot(high, right, dims) + dot(low, right, dims)


def moved(values, by, fill, rows):
    count = values.shape[0]
    rolled = pltpu.roll(values, by % count, 0)
    inside = rows >= by if by > 0 else rows < count + by
    return jnp.where(inside, rolled, fill)


def scan_rows(decay, drive, rows, backward):
    step = 1
    while step < decay.shape[0]:
        by = -step if backward else step
        drive = drive + decay * moved(drive, by, 0.0, rows)
        decay = decay * moved(decay, by, 1.0, rows)
        step *= 2
    return decay, drive


def conv_taps(rows_ref, halo_ref):
    rows = rows_ref[0].astype(F32)
    extended = jnp.concatenate([halo_ref[0].astype(F32), rows], axis=0)
    count = rows.shape[0]
    return [rows] + [extended[HALO - k : HALO - k + count] for k in range(1, WIDTH)]


def gates(conv_out, gate_ref, prm_ref):
    nt = ((1,), (1,))
    high, low = two_parts(conv_out)
    pre_a = dot(high, gate_ref[0], nt) + dot(low, gate_ref[0], nt) + prm_ref[4:5, :]
    pre_x = dot(high, gate_ref[1], nt) + dot(low, gate_ref[1], nt) + prm_ref[5:6, :]
    sig_a = jax.nn.sigmoid(pre_a)
    sig_x = jax.nn.sigmoid(pre_x)
    log_decay = -8.0 * sig_a * prm_ref[6:7, :]
    return sig_a, sig_x, jnp.exp(log_decay), jnp.sqrt(minus_expm1(2.0 * log_decay))


def forward_kernel(rows_ref, halo_ref, prm_ref, gate_ref, decay_ref, local_ref, cum_ref):
    taps = conv_taps(rows_ref, halo_ref)
    conv_out = sum(prm_ref[k : k + 1, :] * taps[k] for k in range(WIDTH))
    sig_a, sig_x, decays, root = gates(conv_out, gate_ref, prm_ref)
    drives = root * sig_x * conv_out
    decay_ref[0] = decays
    rows = lax.broadcasted_iota(jnp.int32, decays.shape, 0)
    cum, local = scan_rows(decays, drives, rows, False)
    cum_ref[0] = cum
    local_ref[0] = local


def back_scan_kernel(d_mixed_ref, branch_y_ref, states_ref, decay_ref, d_y_ref, local_ref, cum_ref):
    value, slope = gelu_both(branch_y_ref[0])
    d_mixed = d_mixed_ref[0]
    d_y_ref[0] = (d_mixed * states_ref[0] * slope).astype(BF)
    rows = lax.broadcasted_iota(jnp.int32, d_mixed.shape, 0)
    coeffs = moved(decay_ref[0], -1, 1.0, rows)
    cum, local = scan_rows(coeffs, d_mixed * value, rows, True)
    cum_ref[0] = cum
    local_ref[0] = local


def backward_kernel(
    rows_ref, halo_ref, prm_ref, gate_ref, local_ref, cum_ref, ends_ref, states_ref,
    d_conv_ref, d_gate_ref, d_prm_ref,
):
    taps = conv_taps(rows_ref, halo_ref)
    conv_out = sum(prm_ref[k : k + 1, :] * taps[k] for k in range(WIDTH))
    sig_a, sig_x, decays, root = gates(conv_out, gate_ref, prm_ref)
    rows = lax.broadcasted_iota(jnp.int32, decays.shape, 0)
    grad = local_ref[0] + cum_ref[0] * ends_ref[0, 0:1, :]
    before = jnp.where(rows >= 1, pltpu.roll(states_ref[0], 1, 0), ends_ref[0, 1:2, :])
    d_log = grad * before * decays - grad * sig_x * conv_out * (decays * decays / root)
    d_pre_a = d_log * (-8.0 * prm_ref[6:7, :]) * sig_a * (1.0 - sig_a)
    d_pre_x = grad * root * conv_out * sig_x * (1.0 - sig_x)
    nn, tn = ((1,), (0,)), ((0,), (0,))
    a_high, a_low = two_parts(d_pre_a)
    x_high, x_low = two_parts(d_pre_x)
    c_high, c_low = two_parts(conv_out)
    d_conv = grad * root * sig_x
    d_conv = d_conv + (dot(a_high, gate_ref[0], nn) + dot(a_low, gate_ref[0], nn))
    d_conv = d_conv + (dot(x_high, gate_ref[1], nn) + dot(x_low, gate_ref[1], nn))
    d_conv_ref[0] = d_conv
    d_gate_a = dot(a_high, c_high, tn) + dot(a_low, c_high, tn) + dot(a_high, c_low, tn)
    d_gate_x = dot(x_high, c_high, tn) + dot(x_low, c_high, tn) + dot(x_high, c_low, tn)
    total = lambda v: jnp.sum(v, axis=0, keepdims=True)
    sums = [total(d_conv * taps[k]) for k in range(WIDTH)]
    sums += [total(d_pre_a), total(d_pre_x), total(d_log * (-8.0 * sig_a))]
    sums.append(jnp.zeros_like(sums[0]))
    d_prm = jnp.concatenate(sums, axis=0)
    first = pl.program_id(1) == 0

    @pl.when(first)
    def _():
        d_gate_ref[0] = d_gate_a
        d_gate_ref[1] = d_gate_x
        d_prm_ref[...] = d_prm

    @pl.when(jnp.logical_not(first))
    def _():
        d_gate_ref[0] += d_gate_a
        d_gate_ref[1] += d_gate_x
        d_prm_ref[...] += d_prm


def head_specs(tok):
    rows = pl.BlockSpec((1, tok, HD), lambda h, q: (q, 0, h))
    halo = pl.BlockSpec((1, HALO, HD), lambda h, q: (q, 0, h))
    prm = pl.BlockSpec((8, HD), lambda h, q: (0, h))
    gate = pl.BlockSpec((2, HD, HD), lambda h, q: (0, h, 0))
    ends = pl.BlockSpec((1, 8, HD), lambda h, q: (q, 0, h))
    return rows, halo, prm, gate, ends


PARAMS = dict(vmem_limit_bytes=40 * 1024 * 1024)


def forward_call(branch_x, halo, prm, gate):
    seqs, tok, half = branch_x.shape
    rows_s, halo_s, prm_s, gate_s, _ = head_specs(tok)
    out = jax.ShapeDtypeStruct(branch_x.shape, F32)
    return pl.pallas_call(
        forward_kernel,
        grid=(half // HD, seqs),
        in_specs=[rows_s, halo_s, prm_s, gate_s],
        out_specs=[rows_s] * 3,
        out_shape=[out] * 3,
        compiler_params=pltpu.CompilerParams(**PARAMS),
        name="recurrence_forward",
    )(branch_x, halo, prm, gate)


def back_scan_call(d_mixed, branch_y, states, decays):
    seqs, tok, half = d_mixed.shape
    rows_s = head_specs(tok)[0]
    out = jax.ShapeDtypeStruct(d_mixed.shape, F32)
    return pl.pallas_call(
        back_scan_kernel,
        grid=(half // HD, seqs),
        in_specs=[rows_s] * 4,
        out_specs=[rows_s] * 3,
        out_shape=[jax.ShapeDtypeStruct(d_mixed.shape, BF), out, out],
        compiler_params=pltpu.CompilerParams(**PARAMS),
        name="recurrence_back_scan",
    )(d_mixed, branch_y, states, decays)


def backward_call(branch_x, halo, prm, gate, local, cum, ends, states):
    seqs, tok, half = branch_x.shape
    rows_s, halo_s, prm_s, gate_s, ends_s = head_specs(tok)
    return pl.pallas_call(
        backward_kernel,
        grid=(half // HD, seqs),
        in_specs=[rows_s, halo_s, prm_s, gate_s, rows_s, rows_s, ends_s, rows_s],
        out_specs=[rows_s, gate_s, prm_s],
        out_shape=[
            jax.ShapeDtypeStruct(branch_x.shape, F32),
            jax.ShapeDtypeStruct(gate.shape, F32),
            jax.ShapeDtypeStruct(prm.shape, F32),
        ],
        compiler_params=pltpu.CompilerParams(**PARAMS),
        name="recurrence_backward",
    )(branch_x, halo, prm, gate, local, cum, ends, states)


def gather_small(value, zn, z, x, y, c):
    value = value[None]
    for axis, at in (("c", c), ("y", y), ("x", x)):
        other = swap(value, axis)
        value = pick(at == 0, jnp.concatenate([value, other]), jnp.concatenate([other, value]))
    whole = jnp.zeros((zn,) + value.shape, value.dtype)
    whole = lax.dynamic_update_slice_in_dim(whole, value[None], z, 0)
    for by in range(1, zn):
        came = shifted(value, "z", by, zn, True)
        whole = lax.dynamic_update_slice_in_dim(whole, came[None], lax.rem(z - by + zn, zn), 0)
    return whole.reshape((-1,) + value.shape[1:])


def sum_small(value, axes, zn):
    for axis in axes:
        value = value + swap(value, axis)
    return value + sum(shifted(value, "z", by, zn, True) for by in range(1, zn))


def carried(decay, drive, count, by):
    both = jnp.stack([decay, drive])
    state = jnp.zeros_like(drive)
    came = [shifted(both, ("z", "x"), by * far, count) for far in range(count - 1, 0, -1)]
    for part in came:
        state = part[0] * state + part[1]
    return state


def per_device(
    zn, fold,
    tokens, w_x, w_y, w_out, gate_w, gain_in, gain_mlp, conv_w, gate_b, rate,
    w_gate, w_up, w_down, cotangent,
):
    z, x, y, c = (lax.axis_index(axis) for axis in ("z", "x", "y", "c"))
    zh = zn // 2
    seq_count = 2 * zn
    tok, width = tokens.shape[1], tokens.shape[2]
    share = w_x.shape[0]
    wide_r = w_x.shape[1]
    half = wide_r // 2
    rows_ff, cols_ff = w_gate.shape
    walk, forth, back = around(zn)
    ring_count = len(walk)
    at_x = place_in(walk, z * 2 + x)
    walk_of = jnp.asarray(walk, jnp.int32)
    cw_from = [walk_of[lax.rem(at_x - k + ring_count, ring_count)] for k in range(ring_count)]
    ccw_from = [walk_of[lax.rem(at_x + k, ring_count)] for k in range(ring_count)]
    zx, zy = ("z", "x"), ("z", "y")

    spread = []
    for other in (0, 1):
        pairs = []
        for h in (0, 1):
            for zl in range(zh):
                for ys in (0, 1):
                    k = ys ^ other
                    pairs.append(((h * zh + zl) * 2 + ys, (k * zh + zl) * 2 + h))
        spread.append(pairs)
    gathered_back = [[(b, a) for a, b in pairs] for pairs in spread]

    tok_own = tokens[0]
    tok_pair = jnp.stack([tok_own, swap(tok_own, "y")])
    smalls = jnp.concatenate([gain_in[None], gain_mlp[None], conv_w, gate_b, rate[None]]).astype(F32)
    smalls = gather_small(smalls, zn, z, x, y, c)
    smalls = smalls.transpose(1, 0, 2).reshape(smalls.shape[1], -1)
    gain_first, gain_second = smalls[0], smalls[1]
    prm = jnp.pad(smalls[2:], ((0, 1), (0, 0)))
    prm = pick(y == 0, prm[:, :half], prm[:, half:])

    xy_first = jnp.concatenate([w_x[:, :half], w_y[:, :half]], axis=1)
    xy_second = jnp.concatenate([w_x[:, half:], w_y[:, half:]], axis=1)
    xy_own = pick(y == 0, xy_first, xy_second)
    xy_other = swap(pick(y == 0, xy_second, xy_first), "y")
    gate_t = gate_w.transpose(0, 2, 1)
    gate_pieces = [
        lax.ppermute(pick(y == 0, gate_t[k], gate_t[1 - k]), zy, spread[k]) for k in (0, 1)
    ]

    forth_part = jnp.concatenate([xy_own, gate_pieces[0]], axis=1)
    back_part = jnp.concatenate([xy_other, gate_pieces[1]], axis=1)
    full_xy = jnp.zeros((seq_count, 2, 2, share, wide_r), BF)
    gates_t = jnp.zeros((2, zh * 2, 2, 2, share, HD), BF)
    for k in range(ring_count):
        if k:
            forth_part = lax.ppermute(forth_part, zx, forth)
            back_part = lax.ppermute(back_part, zx, back)
        both = jnp.stack([forth_part, back_part])
        others = swap(both, "c")
        for core, parts in ((c, both), (1 - c, others)):
            for d, src in ((0, cw_from[k]), (1, ccw_from[k])):
                blk = parts[d]
                y_blk = y if d == 0 else 1 - y
                full_xy = lax.dynamic_update_slice(
                    full_xy, blk[None, None, None, :, :wide_r], (src, y_blk, core, 0, 0)
                )
                src_z, src_x = src // 2, lax.rem(src, 2)
                src_h, src_l = src_z // zh, lax.rem(src_z, zh)
                y_src = src_h if d == 0 else 1 - src_h
                gates_t = lax.dynamic_update_slice(
                    gates_t, blk[None, None, None, None, :, wide_r:],
                    (src_h, src_l * 2 + src_x, y_src, core, 0, 0),
                )
    full_xy = full_xy.reshape(-1, wide_r)
    gates_t = gates_t.reshape(2, half, HD)
    last = forth_part

    out_halves = [w_out[:, :half], w_out[:, half:]]
    out_parts = [
        lax.ppermute(pick(y == 0, out_halves[k], out_halves[1 - k]), zy, spread[k]) for k in (0, 1)
    ]
    forth_part, back_part = after(tuple(out_parts), last)
    full_out = jnp.zeros((2, zh * 2, 2, 2, share, half), BF)
    for k in range(ring_count):
        if k:
            forth_part = lax.ppermute(forth_part, zx, forth)
            back_part = lax.ppermute(back_part, zx, back)
        both = jnp.stack([forth_part, back_part])
        others = swap(both, "c")
        for core, parts in ((c, both), (1 - c, others)):
            for d, src in ((0, cw_from[k]), (1, ccw_from[k])):
                src_z, src_x = src // 2, lax.rem(src, 2)
                src_h, src_l = src_z // zh, lax.rem(src_z, zh)
                y_src = src_h if d == 0 else 1 - src_h
                full_out = lax.dynamic_update_slice(
                    full_out, parts[d][None, None, None, None],
                    (src_h, src_l * 2 + src_x, y_src, core, 0, 0),
                )
    full_out = full_out.reshape(2, half, half)
    full_out = jnp.concatenate([full_out[0], full_out[1]], axis=1)
    last = forth_part

    padded = zn * fold
    widen = lambda w: jnp.pad(w, ((0, 0), (0, padded - cols_ff)))
    ff_all = jnp.stack([widen(w_gate), widen(w_up), widen(w_down.T)])
    ff_all = ff_all.reshape(3, rows_ff, zn, fold).transpose(2, 1, 0, 3).reshape(zn, rows_ff, 3 * fold)
    ff_all = after(ff_all, last)
    w_gu = jnp.zeros((zn, 2, rows_ff, 2 * fold), BF)
    w_dt = jnp.zeros((zn, 2, rows_ff, fold), BF)

    def put_ff(w_gu, w_dt, piece, z_at):
        across = swap(piece, "x")
        for x_at, part in ((x, piece), (1 - x, across)):
            w_gu = lax.dynamic_update_slice(w_gu, part[None, None, :, : 2 * fold], (z_at, x_at, 0, 0))
            w_dt = lax.dynamic_update_slice(w_dt, part[None, None, :, 2 * fold :], (z_at, x_at, 0, 0))
        return w_gu, w_dt

    w_gu, w_dt = put_ff(w_gu, w_dt, lax.dynamic_index_in_dim(ff_all, z, 0, False), z)
    for far in range(1, zn):
        to = lax.rem(z + far, zn)
        came = shifted(lax.dynamic_index_in_dim(ff_all, to, 0, False), "z", far, zn, True)
        w_gu, w_dt = put_ff(w_gu, w_dt, came, lax.rem(z - far + zn, zn))
    w_gu = w_gu.reshape(-1, 2 * fold)
    w_dt = w_dt.reshape(-1, fold)

    cot = cotangent[0]
    cut = tok // 2

    def both_cores(part):
        return jnp.concatenate([part, swap(part, "c")])

    forth_part, back_part = after((cot[:cut], cot[cut:]), last)
    cot_steps = []
    for k in range(ring_count):
        if k:
            forth_part = lax.ppermute(forth_part, zy, forth)
            back_part = lax.ppermute(back_part, zy, back)
        cot_steps.append(both_cores(jnp.concatenate([forth_part, back_part])))

    tok_f = tok_pair.astype(F32)
    normed = rms_scale(tok_f, gain_first).astype(BF).reshape(2 * tok, width)
    branches = product(normed, full_xy)
    branch_x = branches[:, :half].astype(BF).reshape(2, tok, half)
    branch_y = branches[:, half:].reshape(2, tok, half)
    halo = shifted(branch_x[:, tok - HALO :], zx, 1, seq_count)
    decays, local, cum = forward_call(branch_x, halo, prm, gates_t)
    state_in = carried(cum[:, -1], local[:, -1], seq_count, 1)
    states = local + cum * state_in[:, None]
    mixed = (states * gelu_tanh(branch_y)).astype(BF).reshape(2 * tok, half)
    out_sum = product(mixed, full_out)
    residual = tok_own.astype(F32) + out_sum[:tok] + swap(out_sum[tok:].astype(BF), "y").astype(F32)
    normed_mlp = rms_scale(residual, gain_second).astype(BF)

    forth_part, back_part = normed_mlp[:cut], normed_mlp[cut:]
    row_steps, hidden_steps, d_gu_steps, out_steps = [], [], [], []
    first_sum, d_forth, d_back = None, None, None
    for k in range(ring_count):
        if k:
            forth_part = lax.ppermute(forth_part, zy, forth)
            back_part = lax.ppermute(back_part, zy, back)
        rows = both_cores(jnp.concatenate([forth_part, back_part]))
        gu = product(rows, w_gu)
        d_hidden = product(cot_steps[k], w_dt)
        gate_pre, up_proj = gu[:, :fold], gu[:, fold:]
        hidden, pull = jax.vjp(gated_product, gate_pre, up_proj)
        hidden = hidden.astype(BF)
        d_gu = jnp.concatenate([item.astype(BF) for item in pull(d_hidden)], axis=1)
        row_steps.append(rows)
        hidden_steps.append(hidden)
        d_gu_steps.append(d_gu)
        d_rows = product_t(d_gu, w_gu)
        d_own = d_rows[:tok] + swap(d_rows[tok:].astype(BF), "c").astype(F32)
        if k == 0:
            first_sum = d_own
        elif k == 1:
            d_forth, d_back = d_own[:cut].astype(BF), d_own[cut:].astype(BF)
        else:
            d_forth = (lax.ppermute(d_forth, zy, forth).astype(F32) + d_own[:cut]).astype(BF)
            d_back = (lax.ppermute(d_back, zy, back).astype(F32) + d_own[cut:]).astype(BF)
    d_forth = lax.ppermute(d_forth, zy, forth).astype(F32) + first_sum[:cut]
    d_back = lax.ppermute(d_back, zy, back).astype(F32) + first_sum[cut:]
    d_normed_mlp = jnp.concatenate([d_forth, d_back])

    rows_all = jnp.concatenate(row_steps)
    cot_all = jnp.concatenate(cot_steps)
    hidden_all = jnp.concatenate(hidden_steps)
    d_gu_all = jnp.concatenate(d_gu_steps)
    grad_gu = t_product(rows_all, d_gu_all).reshape(zn, 2, rows_ff, 2 * fold)
    grad_dt = t_product(cot_all, hidden_all).reshape(zn, 2, rows_ff, fold)

    grad_rows = cot.astype(F32)
    unused, second_pull = jax.vjp(rms_scale, residual, gain_second)
    d_res_norm, d_gain_mlp = second_pull(d_normed_mlp)
    d_residual = grad_rows + d_res_norm
    d_branch = d_residual.astype(BF)
    d_branch_pair = jnp.concatenate([d_branch, swap(d_branch, "y")])
    d_mixed = product_t(d_branch_pair, full_out).reshape(2, tok, half)
    grad_out = t_product(mixed, d_branch_pair)

    def ff_block(z_at, x_at):
        gu = lax.dynamic_slice(grad_gu, (z_at, x_at, 0, 0), (1, 1, rows_ff, 2 * fold))
        dt = lax.dynamic_slice(grad_dt, (z_at, x_at, 0, 0), (1, 1, rows_ff, fold))
        return jnp.concatenate([gu, dt], axis=-1)[0, 0]

    ff_grad = jnp.zeros((zn, rows_ff, 3 * fold), F32)
    for far in range(zn - 1, -1, -1):
        to = lax.rem(z + far, zn)
        piece = ff_block(to, x) + swap(ff_block(to, 1 - x).astype(BF), "x").astype(F32)
        if far:
            piece = shifted(piece.astype(BF), "z", far, zn, True).astype(F32)
        ff_grad = lax.dynamic_update_slice(ff_grad, piece[None], (lax.rem(z - far + zn, zn), 0, 0))
    ff_grad = ff_grad.reshape(zn, rows_ff, 3, fold).transpose(2, 1, 0, 3).reshape(3, rows_ff, padded)
    ff_grad = ff_grad[:, :, :cols_ff]

    def out_step(k):
        part = product_t(hidden_steps[k], w_dt)
        return part[:tok] + swap(part[tok:].astype(BF), "c").astype(F32)

    for k in range(1, ring_count):
        part = out_step(k)
        if k == 1:
            o_forth, o_back = part[:cut].astype(BF), part[cut:].astype(BF)
        else:
            o_forth = (lax.ppermute(o_forth, zy, forth).astype(F32) + part[:cut]).astype(BF)
            o_back = (lax.ppermute(o_back, zy, back).astype(F32) + part[cut:]).astype(BF)
    part = out_step(0)
    mlp_out = jnp.concatenate([
        lax.ppermute(o_forth, zy, forth).astype(F32) + part[:cut],
        lax.ppermute(o_back, zy, back).astype(F32) + part[cut:],
    ])
    result = (residual + mlp_out).astype(BF)[None]

    d_branch_y, local_back, cum_back = back_scan_call(d_mixed, branch_y, states, decays)
    leaving = decays[:, 0] * local_back[:, 0]
    carry_back = carried(cum[:, -1], leaving, seq_count, -1)
    ends = jnp.pad(jnp.stack([carry_back, state_in], axis=1), ((0, 0), (0, 6), (0, 0)))
    d_conv, d_gates, d_prm = backward_call(
        branch_x, halo, prm, gates_t, local_back, cum_back, ends, states
    )
    rim = shifted(d_conv[:, :8], zx, -1, seq_count)
    d_ext = jnp.concatenate([d_conv, rim], axis=1)
    d_branch_x = sum(prm[k] * d_ext[:, k : k + tok] for k in range(WIDTH)).astype(BF)
    d_branches = jnp.concatenate([d_branch_x, d_branch_y], axis=2).reshape(2 * tok, 2 * half)
    grad_xy = t_product(normed, d_branches)
    d_normed = product_t(d_branches, full_xy)
    d_normed = d_normed[:tok] + swap(d_normed[tok:].astype(BF), "y").astype(F32)
    unused, first_pull = jax.vjp(rms_scale, tok_own.astype(F32), gain_first)
    d_tok, d_gain_in = first_pull(d_normed)
    tokens_grad = (d_residual + d_tok)[None]

    def ring_sum(pieces_of):
        for k in range(1, ring_count):
            f, b = pieces_of(cw_from[k], 0), pieces_of(ccw_from[k], 1)
            if k > 1:
                f = f + lax.ppermute(forth_sum, zx, forth).astype(F32)
                b = b + lax.ppermute(back_sum, zx, back).astype(F32)
            forth_sum, back_sum = f.astype(BF), b.astype(BF)
        f, b = pieces_of(cw_from[0], 0), pieces_of(ccw_from[0], 1)
        return (
            f + lax.ppermute(forth_sum, zx, forth).astype(F32),
            b + lax.ppermute(back_sum, zx, back).astype(F32),
        )

    def over_cores(blocks, axis):
        keep = lax.dynamic_index_in_dim(blocks, c, axis, False)
        give = lax.dynamic_index_in_dim(blocks, 1 - c, axis, False)
        return keep + swap(give.astype(BF), "c").astype(F32)

    out_blocks = jnp.stack([grad_out[:, :half], grad_out[:, half:]])
    out_blocks = over_cores(out_blocks.reshape(2, zh * 2, 2, 2, share, half), 3)

    def out_piece(linear, direction, blocks=out_blocks):
        src_z, src_x = linear // 2, lax.rem(linear, 2)
        src_h, src_l = src_z // zh, lax.rem(src_z, zh)
        y_src = src_h if direction == 0 else 1 - src_h
        sizes = (1, 1, 1) + blocks.shape[3:]
        return lax.dynamic_slice(blocks, (src_h, src_l * 2 + src_x, y_src, 0, 0), sizes)[0, 0, 0]

    out_sums = ring_sum(out_piece)
    came = [lax.ppermute(out_sums[k].astype(BF), zy, gathered_back[k]).astype(F32) for k in (0, 1)]
    grad_w_out = jnp.concatenate(
        [pick(y == 0, came[0], came[1]), pick(y == 0, came[1], came[0])], axis=1
    )

    gate_blocks = over_cores(d_gates.reshape(2, zh * 2, 2, 2, share, HD), 3)
    xy_blocks = over_cores(grad_xy.reshape(seq_count, 2, 2, share, wide_r), 2)

    def xy_piece(linear, direction):
        y_blk = y if direction == 0 else 1 - y
        xy = lax.dynamic_slice(xy_blocks, (linear, y_blk, 0, 0), (1, 1, share, wide_r))[0, 0]
        return jnp.concatenate([xy, out_piece(linear, direction, gate_blocks)], axis=1)

    xy_sums = ring_sum(xy_piece)
    mine = xy_sums[0][:, :wide_r]
    across = swap(xy_sums[1][:, :wide_r].astype(BF), "y").astype(F32)
    low, high = pick(y == 0, mine, across), pick(y == 0, across, mine)
    grad_w_x = jnp.concatenate([low[:, :half], high[:, :half]], axis=1)
    grad_w_y = jnp.concatenate([low[:, half:], high[:, half:]], axis=1)
    came = [
        lax.ppermute(xy_sums[k][:, wide_r:].astype(BF), zy, gathered_back[k]).astype(F32)
        for k in (0, 1)
    ]
    grad_gate_w = jnp.stack([pick(y == 0, came[0], came[1]), pick(y == 0, came[1], came[0])])
    grad_gate_w = grad_gate_w.transpose(0, 2, 1)

    block = (z * 2 + x) * 4 + y * 2 + c
    small_sum = sum_small(d_prm, ("c", "x"), zn)
    other_half = swap(small_sum, "y")
    small_sum = jnp.concatenate(
        [pick(y == 0, small_sum, other_half), pick(y == 0, other_half, small_sum)], axis=1
    )
    own_small = lax.dynamic_slice(small_sum, (0, block * share), (8, share))
    gains = sum_small(jnp.stack([d_gain_in, d_gain_mlp]), ("c", "x", "y"), zn)
    own_gain = lax.dynamic_slice(gains, (0, block * share), (2, share))
    return (
        result,
        tokens_grad,
        grad_w_x,
        grad_w_y,
        grad_w_out,
        grad_gate_w,
        own_gain[0],
        own_gain[1],
        own_small[:WIDTH],
        own_small[WIDTH : WIDTH + 2],
        own_small[WIDTH + 2],
        ff_grad[0],
        ff_grad[1],
        ff_grad[2].T,
    )


def solution(mesh):
    seq_count, pair_count = mesh.shape["seq"], mesh.shape["fsdp"]
    zn = seq_count // 2
    grid = Mesh(mesh.devices.reshape(zn, 2, pair_count // 2, 2), ("z", "x", "y", "c"))
    seq, fsdp, both = ("z", "x"), ("y", "c"), ("z", "x", "y", "c")
    rows = P(fsdp, seq, None)
    by_row = P(both, None)
    by_col = P(None, both)
    placed = (
        rows, by_row, by_row, by_row, P(None, None, both), P(both), P(both), by_col, by_col, P(both),
        P(seq, fsdp), P(seq, fsdp), P(fsdp, seq), rows,
    )
    out_specs = (
        rows, rows, by_row, by_row, by_row, P(None, None, both), P(both), P(both), by_col, by_col,
        P(both), P(seq, fsdp), P(seq, fsdp), P(fsdp, seq),
    )

    def run(*args):
        hidden_share = args[10].shape[1] // pair_count
        lanes = 128
        fold = -(-hidden_share // (lanes * zn)) * lanes
        return jax.shard_map(
            functools.partial(per_device, zn, fold),
            mesh=grid, in_specs=placed, out_specs=out_specs, check_vma=False,
        )(*args)

    return run
```

time: 4660 us -> 1350 us (0.29)
  waiting for transfers between devices: 3760 us -> 429 us
  starting transfers between devices: 4.24 us -> 327 us
  blocking collectives: 294 us -> 0 us
  matrix products: 214 us -> 133 us
  other arithmetic: 68.9 us -> 119 us
    reduce_scatter x11 -> x0, waiting for transfers between devices: 1440 us -> none  [the longest x1 328 us: per_device(): lax.psum_scatter(grad_gate, 'seq', scatter_dimension=0, tiled=True)]
    unnamed x28 -> x0, waiting for transfers between devices: 1340 us -> none
    all_gather x15 -> x0, waiting for transfers between devices: 985 us -> none  [the longest x2 276 us: fetch_feedforward(): lax.all_gather(w_down, 'seq', axis=1, tiled=True)]
    ppermute x2 -> x225, waiting for transfers between devices: 0.01 us -> 429 us  [the longest x74 93 us: swap(): return lax.ppermute(value, axis, [(0, 1), (1, 0)])]
    ppermute x2 -> x225, starting transfers between devices: 3.17 us -> 327 us  [the longest x31 112 us: shifted(): return lax.ppermute(value, axes, pairs)]
    all_gather x6 -> x0, blocking collectives: 201 us -> none  [the longest x4 124 us: entering(): pieces = jax.tree.map(lambda part: lax.all_gather(part, axis), value)]
    slice x98 -> x40, local copies, waits for them, and re-layouts: 128 us -> 32.4 us  [the longest x1 10.2 us: per_device(): out_blocks = jnp.stack([grad_out[:, :half], grad_out[:, half:]])]
    unnamed x3 -> x0, blocking collectives: 93.5 us -> none
  transfers between devices with their start and end apart: 29 -> 225, of which waited for: 22 -> 94; matrix products, arithmetic and copies ran while one was open for 11% -> 36% of each run, Pallas kernels for 0% -> 2%
where the time goes in v1:
time: 1350 us; the launch traced here: 1340 us
  waiting for transfers between devices  429 us (32%)
  starting transfers between devices  327 us (24%)
  local copies, waits for them, and re-layouts  257 us (19%)
  matrix products  133 us (10%)
  other arithmetic  119 us (9%)
  between operations  47.6 us (4%)
  Pallas kernels  24.3 us (2%)
    dot_general x40, matrix products, dot(): lax.dot_general(left, right, (dims, ((), ())), preferred_element_type=F32)  133 us
    ppermute x31, starting transfers between devices, shifted(): return lax.ppermute(value, axes, pairs)  112 us
    ppermute x74, waiting for transfers between devices, swap(): return lax.ppermute(value, axis, [(0, 1), (1, 0)])  93 us
    ppermute x14, waiting for transfers between devices, per_device(): back_part = lax.ppermute(back_part, zy, back)  74 us
    unnamed x318, local copies, waits for them, and re-layouts  63.3 us
    ppermute x12, waiting for transfers between devices, ring_sum(): b = b + lax.ppermute(back_sum, zx, back).astype(F32)  60.2 us
    ppermute x74, starting transfers between devices, swap(): return lax.ppermute(value, axis, [(0, 1), (1, 0)])  41.8 us
    ppermute x14, starting transfers between devices, per_device(): forth_part = lax.ppermute(forth_part, zy, forth)  40.9 us
  transfers between devices with their start and end apart: 225, of which 94 were waited for; matrix products, arithmetic and copies ran while one was open for 36% of the time, Pallas kernels for 2%

profile of v1, /device:TPU:0, one launch (start us, length us, event | category | flops | bytes accessed | tf_op | source)
XLA Modules:
  0.0 1337.0 jit_solution(12835880245273319871)
XLA Ops:
  14.2 5.7 collective-permute-start.9
  61.1 6.2 broadcast_in_dim.315
  70.9 6.2 collective-permute-start.2
  114.4 6.5 collective-permute-start.5
  157.9 7.3 collective-permute-done.15
  190.3 6.8 collective-permute-done.21
  200.1 6.2 collective-permute-done.24
  253.6 5.1 collective-permute-done.49
  278.9 6.6 fusion.400
  290.3 8.1 recurrence_forward.1
  379.8 8.2 collective-permute-done.122
  399.4 40.5 %collective-permute-done.127 = bf16[64,2560]{1,0:T(8,128)(2,1)S(1)} collective-permute-done((bf16[64,2560]{1,0:T(8,128)(2,1)S(1)}, bf16[64,2560]{1,0:T(8,128)(2,1)S(1)}, u32[]{:S(2)}, u32[]{:S(2)}) %collective-permute-start.127) | collective-permute-done | bytes 327712 | tf_op jit(solution)/shard_map/ppermute | solution.py:435
  442.7 22.5 %collective-permute-start.131 = (bf16[64,2560]{1,0:T(8,128)(2,1)S(1)}, bf16[64,2560]{1,0:T(8,128)(2,1)S(1)}, u32[]{:S(2)}, u32[]{:S(2)}) collective-permute-start(bf16[64,2560]{1,0:T(8,128)(2,1)S(1)} %collective-permute-done.126), channel_id=1, source_target_pairs={{0,8},{8,16},{16,24},{24,26},{26,18},{18,10},{10,2},{2,0},{1,9},{9... | collective-permute-start | bytes 983048 | tf_op jit(solution)/shard_map/ppermute | solution.py:434
  475.0 5.1 collective-permute-done.66
  499.7 11.4 collective-permute-done.70
  511.2 20.9 %collective-permute-done.72 = bf16[320,1536]{1,0:T(8,128)(2,1)S(1)} collective-permute-done((bf16[320,1536]{1,0:T(8,128)(2,1)S(1)}, bf16[320,1536]{1,0:T(8,128)(2,1)S(1)}, u32[]{:S(2)}, u32[]{:S(2)}) %collective-permute-start.72) | collective-permute-done | bytes 983072 | tf_op jit(solution)/shard_map/ppermute | solution.py:21
  532.3 18.2 %collective-permute-done.74 = bf16[320,1536]{1,0:T(8,128)(2,1)S(1)} collective-permute-done((bf16[320,1536]{1,0:T(8,128)(2,1)S(1)}, bf16[320,1536]{1,0:T(8,128)(2,1)S(1)}, u32[]{:S(2)}, u32[]{:S(2)}) %collective-permute-start.74) | collective-permute-done | bytes 983072 | tf_op jit(solution)/shard_map/ppermute | solution.py:21
  748.9 5.8 collective-permute-done.155
  757.9 5.8 collective-permute-done.111
  775.6 9.5 fusion.412
  786.1 16.4 %fusion.411 = f32[2560,1024]{1,0:T(8,128)S(1)} fusion(bf16[2048,2560]{1,0:T(8,128)(2,1)} %constant_dynamic-update-slice_fusion.4, bf16[2048,1024]{1,0:T(8,128)(2,1)} %fusion.291), kind=kOutput, calls=%fused_computation.986 | convolution fusion | flops 10737418240 | bytes 25165824 | tf_op jit(solution)/shard_map/dot_general | solution.py:57
  841.6 5.9 collective-permute-done.145
  849.8 5.6 collective-permute-done.101
  857.6 5.9 collective-permute-done.150
  876.2 38.5 %collective-permute-done.224 = bf16[320,1536]{1,0:T(8,128)(2,1)S(1)} collective-permute-done((bf16[320,1536]{1,0:T(8,128)(2,1)S(1)}, bf16[320,1536]{1,0:T(8,128)(2,1)S(1)}, u32[]{:S(2)}, u32[]{:S(2)}) %collective-permute-start.224) | collective-permute-done | bytes 983072 | tf_op jit(solution)/shard_map/ppermute | solution.py:21
  941.6 7.7 fusion.151
  949.3 10.2 fusion.389
  962.2 5.4 fusion.9
  967.6 8.9 collective-permute-start.219
  976.6 5.7 collective-permute-start.221
  982.5 12.4 recurrence_backward.1
  1006.8 40.6 %collective-permute-start.215 = (f32[8,1280]{1,0:T(8,128)S(1)}, f32[8,1280]{1,0:T(8,128)S(1)}, u32[]{:S(2)}, u32[]{:S(2)}) collective-permute-start(f32[8,1280]{1,0:T(8,128)S(1)} %add.1745), channel_id=1, source_target_pairs={{0,16},{8,24},{16,0},{24,8},{1,17},{9,25},{17,1},{25,9},{2,18},{10... | collective-permute-start | bytes 122888 | tf_op jit(solution)/shard_map/ppermute | solution.py:26
  1049.3 10.5 fusion.410
  1059.8 6.7 fusion.409
  1066.5 5.4 collective-permute-start.223
  1074.0 8.4 fusion
  1092.4 5.6 collective-permute-done.223
  1128.3 11.7 copy.134
  1140.1 10.2 reshape.809
  1152.1 6.8 slice_bitcast_fusion
  1216.6 13.2 collective-permute-done.203
  1230.8 7.6 bitcast_add_fusion
  1248.6 5.2 dynamic-slice_bitcast_fusion.7
  1260.8 8.8 collective-permute-done.180
  1273.6 9.1 collective-permute-done.181
  1286.9 8.2 collective-permute-done.182
  1299.3 7.3 collective-permute-done.183
  1311.0 6.2 collective-permute-done.184
  (1158 shorter events, 782.5 us)
Async XLA Ops:
  2.8 67.3 %collective-permute-start.1 = (f32[1,9,80]{2,1,0:T(8,128)}, f32[1,9,80]{2,1,0:T(8,128)}, u32[]{:S(2)}, u32[]{:S(2)}) collective-permute-start(f32[1,9,80]{2,1,0:T(8,128)} %convert_element_type.642), channel_id=1, source_target_pairs={{0,1},{1,0},{2,3},{3,2},{4,5},{5,4},{6,7},{7,6},{8,9},{9,8},{10,11... | collective-permute-start | bytes 8648 | tf_op jit(solution)/shard_map/ppermute | solution.py:21
  3.2 136.8 %collective-permute-start = (bf16[128,2560]{1,0:T(8,128)(2,1)}, bf16[128,2560]{1,0:T(8,128)(2,1)}, u32[]{:S(2)}, u32[]{:S(2)}) collective-permute-start(bf16[128,2560]{1,0:T(8,128)(2,1)} %bitcast.867), channel_id=1, source_target_pairs={{0,2},{2,0},{1,3},{3,1},{4,6},{6,4},{5,7},{7,5},{8,10},{10,8},{9,1... | collective-permute-start | bytes 1966088 | tf_op jit(solution)/shard_map/ppermute | solution.py:21
  8.9 121.6 %collective-permute-start.7 = (bf16[80,2560]{1,0:T(8,128)(2,1)}, bf16[80,2560]{1,0:T(8,128)(2,1)}, u32[]{:S(2)}, u32[]{:S(2)}) collective-permute-start(bf16[80,2560]{1,0:T(8,128)(2,1)} %get-tuple-element.205), channel_id=1, source_target_pairs={{0,2},{2,0},{1,3},{3,1},{4,6},{6,4},{5,7},{7,5},{8,10},{10,8},{9,1... | collective-permute-start | bytes 1228808 | tf_op jit(solution)/shard_map/ppermute | solution.py:21
  14.2 94.0 %collective-permute-start.9 = (bf16[80,256]{1,0:T(8,128)(2,1)}, bf16[80,256]{1,0:T(8,128)(2,1)}, u32[]{:S(2)}, u32[]{:S(2)}) collective-permute-start(bf16[80,256]{1,0:T(8,128)(2,1)} %get-tuple-element.236), channel_id=1, source_target_pairs={{0,16},{2,0},{8,24},{10,8},{16,18},{18,2},{24,26},{26,10},{1,17},{... | collective-permute-start | bytes 122888 | tf_op jit(solution)/shard_map/ppermute | solution.py:345
  19.9 82.0 %collective-permute-start.8 = (bf16[80,256]{1,0:T(8,128)(2,1)}, bf16[80,256]{1,0:T(8,128)(2,1)}, u32[]{:S(2)}, u32[]{:S(2)}) collective-permute-start(bf16[80,256]{1,0:T(8,128)(2,1)} %get-tuple-element.235), channel_id=1, source_target_pairs={{0,0},{2,16},{8,8},{10,24},{16,2},{18,18},{24,10},{26,26},{1,1},{3... | collective-permute-start | bytes 122888 | tf_op jit(solution)/shard_map/ppermute | solution.py:345
  98.4 124.6 %collective-permute-start.40 = (bf16[80,1280]{1,0:T(8,128)(2,1)}, bf16[80,1280]{1,0:T(8,128)(2,1)}, u32[]{:S(2)}, u32[]{:S(2)}) collective-permute-start(bf16[80,1280]{1,0:T(8,128)(2,1)} %get-tuple-element.220), channel_id=1, source_target_pairs={{0,0},{2,16},{8,8},{10,24},{16,2},{18,18},{24,10},{26,26},{1,1},{3... | collective-permute-start | bytes 614408 | tf_op jit(solution)/shard_map/ppermute | solution.py:378
  101.9 121.2 %collective-permute-start.41 = (bf16[80,1280]{1,0:T(8,128)(2,1)}, bf16[80,1280]{1,0:T(8,128)(2,1)}, u32[]{:S(2)}, u32[]{:S(2)}) collective-permute-start(bf16[80,1280]{1,0:T(8,128)(2,1)} %get-tuple-element.219), channel_id=1, source_target_pairs={{0,16},{2,0},{8,24},{10,8},{16,18},{18,2},{24,26},{26,10},{1,17},{... | collective-permute-start | bytes 614408 | tf_op jit(solution)/shard_map/ppermute | solution.py:378
  219.7 48.7 %collective-permute-start.28 = (bf16[2,80,2816]{2,1,0:T(8,128)(2,1)S(1)}, bf16[2,80,2816]{2,1,0:T(8,128)(2,1)S(1)}, u32[]{:S(2)}, u32[]{:S(2)}) collective-permute-start(bf16[2,80,2816]{2,1,0:T(8,128)(2,1)S(1)} %pad_maximum_fusion.13), channel_id=1, source_target_pairs={{0,1},{1,0},{2,3},{3,2},{4,5},{5,4},{6,7},{7,6},{8,9},{9,8},{10,11... | collective-permute-start | bytes 2703368 | tf_op jit(solution)/shard_map/ppermute | solution.py:21
  317.7 37.0 %collective-permute-start.60 = (bf16[2,80,1280]{2,1,0:T(8,128)(2,1)}, bf16[2,80,1280]{2,1,0:T(8,128)(2,1)}, u32[]{:S(2)}, u32[]{:S(2)}) collective-permute-start(bf16[2,80,1280]{2,1,0:T(8,128)(2,1)} %pad_maximum_fusion.54), channel_id=1, source_target_pairs={{0,1},{1,0},{2,3},{3,2},{4,5},{5,4},{6,7},{7,6},{8,9},{9,8},{10,11... | collective-permute-start | bytes 1228808 | tf_op jit(solution)/shard_map/ppermute | solution.py:21
  332.1 60.1 %collective-permute-start.68 = (bf16[320,1536]{1,0:T(8,128)(2,1)}, bf16[320,1536]{1,0:T(8,128)(2,1)}, u32[]{:S(2)}, u32[]{:S(2)}) collective-permute-start(bf16[320,1536]{1,0:T(8,128)(2,1)} %bitcast.900), channel_id=1, source_target_pairs={{0,4},{4,0},{1,5},{5,1},{2,6},{6,2},{3,7},{7,3},{8,12},{12,8},{9,1... | collective-permute-start | bytes 2949128 | tf_op jit(solution)/shard_map/ppermute | solution.py:21
  354.8 43.7 %collective-permute-start.69 = (bf16[320,1536]{1,0:T(8,128)(2,1)}, bf16[320,1536]{1,0:T(8,128)(2,1)S(1)}, u32[]{:S(2)}, u32[]{:S(2)}) collective-permute-start(bf16[320,1536]{1,0:T(8,128)(2,1)} %bitcast.928), channel_id=1, source_target_pairs={{0,8},{8,16},{16,24},{24,0},{1,9},{9,17},{17,25},{25,1},{2,10},{10... | collective-permute-start | bytes 2949128 | tf_op jit(solution)/shard_map/ppermute | solution.py:26
  388.0 98.3 %collective-permute-start.71 = (bf16[320,1536]{1,0:T(8,128)(2,1)S(1)}, bf16[320,1536]{1,0:T(8,128)(2,1)S(1)}, u32[]{:S(2)}, u32[]{:S(2)}) collective-permute-start(bf16[320,1536]{1,0:T(8,128)(2,1)S(1)} %bitcast.927), channel_id=1, source_target_pairs={{0,16},{8,24},{16,0},{24,8},{1,17},{9,25},{17,1},{25,9},{2,18},{10... | collective-permute-start | bytes 2949128 | tf_op jit(solution)/shard_map/ppermute | solution.py:26
  388.6 99.3 %collective-permute-start.73 = (bf16[320,1536]{1,0:T(8,128)(2,1)S(1)}, bf16[320,1536]{1,0:T(8,128)(2,1)S(1)}, u32[]{:S(2)}, u32[]{:S(2)}) collective-permute-start(bf16[320,1536]{1,0:T(8,128)(2,1)S(1)} %bitcast.926), channel_id=1, source_target_pairs={{0,24},{8,0},{16,8},{24,16},{1,25},{9,1},{17,9},{25,17},{2,26},{10... | collective-permute-start | bytes 2949128 | tf_op jit(solution)/shard_map/ppermute | solution.py:26
  391.0 49.5 %collective-permute-start.64 = (bf16[128,2560]{1,0:T(8,128)(2,1)S(1)}, bf16[128,2560]{1,0:T(8,128)(2,1)S(1)}, u32[]{:S(2)}, u32[]{:S(2)}) collective-permute-start(bf16[128,2560]{1,0:T(8,128)(2,1)S(1)} %slice.2062), channel_id=1, source_target_pairs={{0,2},{2,0},{1,3},{3,1},{4,6},{6,4},{5,7},{7,5},{8,10},{10,8},{9,1... | collective-permute-start | bytes 1966088 | tf_op jit(solution)/shard_map/ppermute | solution.py:21
  392.1 47.8 %collective-permute-start.127 = (bf16[64,2560]{1,0:T(8,128)(2,1)S(1)}, bf16[64,2560]{1,0:T(8,128)(2,1)S(1)}, u32[]{:S(2)}, u32[]{:S(2)}) collective-permute-start(bf16[64,2560]{1,0:T(8,128)(2,1)S(1)} %collective-permute-done.122), channel_id=1, source_target_pairs={{8,0},{16,8},{24,16},{26,24},{18,26},{10,18},{2,10},{0,2},{9,1},{1... | collective-permute-start | bytes 983048 | tf_op jit(solution)/shard_map/ppermute | solution.py:435
  398.5 41.5 %collective-permute-start.126 = (bf16[64,2560]{1,0:T(8,128)(2,1)S(1)}, bf16[64,2560]{1,0:T(8,128)(2,1)S(1)}, u32[]{:S(2)}, u32[]{:S(2)}) collective-permute-start(bf16[64,2560]{1,0:T(8,128)(2,1)S(1)} %collective-permute-done.121), channel_id=1, source_target_pairs={{0,8},{8,16},{16,24},{24,26},{26,18},{18,10},{10,2},{2,0},{1,9},{9... | collective-permute-start | bytes 983048 | tf_op jit(solution)/shard_map/ppermute | solution.py:434
  440.0 41.8 %collective-permute-start.128 = (bf16[128,2560]{1,0:T(8,128)(2,1)S(1)}, bf16[128,2560]{1,0:T(8,128)(2,1)S(1)}, u32[]{:S(2)}, u32[]{:S(2)}) collective-permute-start(bf16[128,2560]{1,0:T(8,128)(2,1)S(1)} %pad_maximum_fusion.29), channel_id=1, source_target_pairs={{0,1},{1,0},{2,3},{3,2},{4,5},{5,4},{6,7},{7,6},{8,9},{9,8},{10,11... | collective-permute-start | bytes 1966088 | tf_op jit(solution)/shard_map/ppermute | solution.py:21
  487.9 44.2 %collective-permute-start.72 = (bf16[320,1536]{1,0:T(8,128)(2,1)S(1)}, bf16[320,1536]{1,0:T(8,128)(2,1)S(1)}, u32[]{:S(2)}, u32[]{:S(2)}) collective-permute-start(bf16[320,1536]{1,0:T(8,128)(2,1)S(1)} %collective-permute-done.71), channel_id=1, source_target_pairs={{0,4},{4,0},{1,5},{5,1},{2,6},{6,2},{3,7},{7,3},{8,12},{12,8},{9,1... | collective-permute-start | bytes 2949128 | tf_op jit(solution)/shard_map/ppermute | solution.py:21
  490.3 60.2 %collective-permute-start.74 = (bf16[320,1536]{1,0:T(8,128)(2,1)S(1)}, bf16[320,1536]{1,0:T(8,128)(2,1)S(1)}, u32[]{:S(2)}, u32[]{:S(2)}) collective-permute-start(bf16[320,1536]{1,0:T(8,128)(2,1)S(1)} %collective-permute-done.73), channel_id=1, source_target_pairs={{0,4},{4,0},{1,5},{5,1},{2,6},{6,2},{3,7},{7,3},{8,12},{12,8},{9,1... | collective-permute-start | bytes 2949128 | tf_op jit(solution)/shard_map/ppermute | solution.py:21
  499.1 67.4 %collective-permute-start.133 = (bf16[128,2560]{1,0:T(8,128)(2,1)S(1)}, bf16[128,2560]{1,0:T(8,128)(2,1)S(1)}, u32[]{:S(2)}, u32[]{:S(2)}) collective-permute-start(bf16[128,2560]{1,0:T(8,128)(2,1)S(1)} %pad_maximum_fusion.30), channel_id=1, source_target_pairs={{0,1},{1,0},{2,3},{3,2},{4,5},{5,4},{6,7},{7,6},{8,9},{9,8},{10,11... | collective-permute-start | bytes 1966088 | tf_op jit(solution)/shard_map/ppermute | solution.py:21
  499.6 71.6 %collective-permute-start.67 = (bf16[128,2560]{1,0:T(8,128)(2,1)S(1)}, bf16[128,2560]{1,0:T(8,128)(2,1)S(1)}, u32[]{:S(2)}, u32[]{:S(2)}) collective-permute-start(bf16[128,2560]{1,0:T(8,128)(2,1)S(1)} %pad_maximum_fusion.20), channel_id=1, source_target_pairs={{0,1},{1,0},{2,3},{3,2},{4,5},{5,4},{6,7},{7,6},{8,9},{9,8},{10,11... | collective-permute-start | bytes 1966088 | tf_op jit(solution)/shard_map/ppermute | solution.py:21
  511.1 77.0 %collective-permute-start.138 = (bf16[128,2560]{1,0:T(8,128)(2,1)S(1)}, bf16[128,2560]{1,0:T(8,128)(2,1)S(1)}, u32[]{:S(2)}, u32[]{:S(2)}) collective-permute-start(bf16[128,2560]{1,0:T(8,128)(2,1)S(1)} %pad_maximum_fusion.31), channel_id=1, source_target_pairs={{0,1},{1,0},{2,3},{3,2},{4,5},{5,4},{6,7},{7,6},{8,9},{9,8},{10,11... | collective-permute-start | bytes 1966088 | tf_op jit(solution)/shard_map/ppermute | solution.py:21
  571.3 45.2 %collective-permute-start.152 = (bf16[128,2560]{1,0:T(8,128)(2,1)S(1)}, bf16[128,2560]{1,0:T(8,128)(2,1)S(1)}, u32[]{:S(2)}, u32[]{:S(2)}) collective-permute-start(bf16[128,2560]{1,0:T(8,128)(2,1)S(1)} %slice.2046), channel_id=1, source_target_pairs={{0,1},{1,0},{2,3},{3,2},{4,5},{5,4},{6,7},{7,6},{8,9},{9,8},{10,11... | collective-permute-start | bytes 1966088 | tf_op jit(solution)/shard_map/ppermute | solution.py:21
  643.0 47.9 %collective-permute-start.94 = (bf16[128,2560]{1,0:T(8,128)(2,1)}, bf16[128,2560]{1,0:T(8,128)(2,1)S(1)}, u32[]{:S(2)}, u32[]{:S(2)}) collective-permute-start(bf16[128,2560]{1,0:T(8,128)(2,1)} %pad_maximum_fusion.24), channel_id=1, source_target_pairs={{0,1},{1,0},{2,3},{3,2},{4,5},{5,4},{6,7},{7,6},{8,9},{9,8},{10,11... | collective-permute-start | bytes 1966088 | tf_op jit(solution)/shard_map/ppermute | solution.py:21
  647.0 57.2 %collective-permute-start.129 = (bf16[128,2560]{1,0:T(8,128)(2,1)}, bf16[128,2560]{1,0:T(8,128)(2,1)}, u32[]{:S(2)}, u32[]{:S(2)}) collective-permute-start(bf16[128,2560]{1,0:T(8,128)(2,1)} %slice.2051), channel_id=1, source_target_pairs={{0,1},{1,0},{2,3},{3,2},{4,5},{5,4},{6,7},{7,6},{8,9},{9,8},{10,11... | collective-permute-start | bytes 1966088 | tf_op jit(solution)/shard_map/ppermute | solution.py:21
  686.0 45.4 %collective-permute-start.99 = (bf16[128,2560]{1,0:T(8,128)(2,1)}, bf16[128,2560]{1,0:T(8,128)(2,1)S(1)}, u32[]{:S(2)}, u32[]{:S(2)}) collective-permute-start(bf16[128,2560]{1,0:T(8,128)(2,1)} %pad_maximum_fusion.25), channel_id=1, source_target_pairs={{0,1},{1,0},{2,3},{3,2},{4,5},{5,4},{6,7},{7,6},{8,9},{9,8},{10,11... | collective-permute-start | bytes 1966088 | tf_op jit(solution)/shard_map/ppermute | solution.py:21
  689.9 54.9 %collective-permute-start.134 = (bf16[128,2560]{1,0:T(8,128)(2,1)}, bf16[128,2560]{1,0:T(8,128)(2,1)S(1)}, u32[]{:S(2)}, u32[]{:S(2)}) collective-permute-start(bf16[128,2560]{1,0:T(8,128)(2,1)} %slice.2050), channel_id=1, source_target_pairs={{0,1},{1,0},{2,3},{3,2},{4,5},{5,4},{6,7},{7,6},{8,9},{9,8},{10,11... | collective-permute-start | bytes 1966088 | tf_op jit(solution)/shard_map/ppermute | solution.py:21
  727.4 38.2 %collective-permute-start.104 = (bf16[128,2560]{1,0:T(8,128)(2,1)S(1)}, bf16[128,2560]{1,0:T(8,128)(2,1)S(1)}, u32[]{:S(2)}, u32[]{:S(2)}) collective-permute-start(bf16[128,2560]{1,0:T(8,128)(2,1)S(1)} %pad_maximum_fusion.26), channel_id=1, source_target_pairs={{0,1},{1,0},{2,3},{3,2},{4,5},{5,4},{6,7},{7,6},{8,9},{9,8},{10,11... | collective-permute-start | bytes 1966088 | tf_op jit(solution)/shard_map/ppermute | solution.py:21
  731.2 74.9 %collective-permute-start.139 = (bf16[128,2560]{1,0:T(8,128)(2,1)}, bf16[128,2560]{1,0:T(8,128)(2,1)}, u32[]{:S(2)}, u32[]{:S(2)}) collective-permute-start(bf16[128,2560]{1,0:T(8,128)(2,1)} %slice.2049), channel_id=1, source_target_pairs={{0,1},{1,0},{2,3},{3,2},{4,5},{5,4},{6,7},{7,6},{8,9},{9,8},{10,11... | collective-permute-start | bytes 1966088 | tf_op jit(solution)/shard_map/ppermute | solution.py:21
  745.8 62.7 %collective-permute-start.95 = (bf16[128,2560]{1,0:T(8,128)(2,1)S(1)}, bf16[128,2560]{1,0:T(8,128)(2,1)}, u32[]{:S(2)}, u32[]{:S(2)}) collective-permute-start(bf16[128,2560]{1,0:T(8,128)(2,1)S(1)} %slice.2057), channel_id=1, source_target_pairs={{0,1},{1,0},{2,3},{3,2},{4,5},{5,4},{6,7},{7,6},{8,9},{9,8},{10,11... | collective-permute-start | bytes 1966088 | tf_op jit(solution)/shard_map/ppermute | solution.py:21
  757.9 65.9 %collective-permute-start.144 = (bf16[128,2560]{1,0:T(8,128)(2,1)}, bf16[128,2560]{1,0:T(8,128)(2,1)}, u32[]{:S(2)}, u32[]{:S(2)}) collective-permute-start(bf16[128,2560]{1,0:T(8,128)(2,1)} %slice.2048), channel_id=1, source_target_pairs={{0,1},{1,0},{2,3},{3,2},{4,5},{5,4},{6,7},{7,6},{8,9},{9,8},{10,11... | collective-permute-start | bytes 1966088 | tf_op jit(solution)/shard_map/ppermute | solution.py:21
  763.7 50.1 %collective-permute-start.135 = (bf16[64,2560]{1,0:T(8,128)(2,1)}, bf16[64,2560]{1,0:T(8,128)(2,1)}, u32[]{:S(2)}, u32[]{:S(2)}) collective-permute-start(bf16[64,2560]{1,0:T(8,128)(2,1)} %get-tuple-element.164), channel_id=1, source_target_pairs={{0,8},{8,16},{16,24},{24,26},{26,18},{18,10},{10,2},{2,0},{1,9},{9... | collective-permute-start | bytes 983048 | tf_op jit(solution)/shard_map/ppermute | solution.py:476
  765.6 49.3 %collective-permute-start.156 = (bf16[64,2560]{1,0:T(8,128)(2,1)}, bf16[64,2560]{1,0:T(8,128)(2,1)}, u32[]{:S(2)}, u32[]{:S(2)}) collective-permute-start(bf16[64,2560]{1,0:T(8,128)(2,1)} %get-tuple-element.165), channel_id=1, source_target_pairs={{8,0},{16,8},{24,16},{26,24},{18,26},{10,18},{2,10},{0,2},{9,1},{1... | collective-permute-start | bytes 983048 | tf_op jit(solution)/shard_map/ppermute | solution.py:477
  830.6 85.7 %collective-permute-start.218 = (bf16[320,1536]{1,0:T(8,128)(2,1)S(1)}, bf16[320,1536]{1,0:T(8,128)(2,1)S(1)}, u32[]{:S(2)}, u32[]{:S(2)}) collective-permute-start(bf16[320,1536]{1,0:T(8,128)(2,1)S(1)} %maximum_bitcast_fusion.4), channel_id=1, source_target_pairs={{0,4},{4,0},{1,5},{5,1},{2,6},{6,2},{3,7},{7,3},{8,12},{12,8},{9,1... | collective-permute-start | bytes 2949128 | tf_op jit(solution)/shard_map/ppermute | solution.py:21
  835.2 82.3 %collective-permute-start.220 = (bf16[320,1536]{1,0:T(8,128)(2,1)S(1)}, bf16[320,1536]{1,0:T(8,128)(2,1)S(1)}, u32[]{:S(2)}, u32[]{:S(2)}) collective-permute-start(bf16[320,1536]{1,0:T(8,128)(2,1)S(1)} %maximum_bitcast_fusion.5), channel_id=1, source_target_pairs={{0,4},{4,0},{1,5},{5,1},{2,6},{6,2},{3,7},{7,3},{8,12},{12,8},{9,1... | collective-permute-start | bytes 2949128 | tf_op jit(solution)/shard_map/ppermute | solution.py:21
  837.3 84.6 %collective-permute-start.222 = (bf16[320,1536]{1,0:T(8,128)(2,1)}, bf16[320,1536]{1,0:T(8,128)(2,1)}, u32[]{:S(2)}, u32[]{:S(2)}) collective-permute-start(bf16[320,1536]{1,0:T(8,128)(2,1)} %maximum_bitcast_fusion.6), channel_id=1, source_target_pairs={{0,4},{4,0},{1,5},{5,1},{2,6},{6,2},{3,7},{7,3},{8,12},{12,8},{9,1... | collective-permute-start | bytes 2949128 | tf_op jit(solution)/shard_map/ppermute | solution.py:21
  870.7 44.1 %collective-permute-start.224 = (bf16[320,1536]{1,0:T(8,128)(2,1)S(1)}, bf16[320,1536]{1,0:T(8,128)(2,1)S(1)}, u32[]{:S(2)}, u32[]{:S(2)}) collective-permute-start(bf16[320,1536]{1,0:T(8,128)(2,1)S(1)} %maximum_bitcast_fusion.7), channel_id=1, source_target_pairs={{0,4},{4,0},{1,5},{5,1},{2,6},{6,2},{3,7},{7,3},{8,12},{12,8},{9,1... | collective-permute-start | bytes 2949128 | tf_op jit(solution)/shard_map/ppermute | solution.py:21
  874.3 50.7 %collective-permute-start.160 = (bf16[128,2560]{1,0:T(8,128)(2,1)S(1)}, bf16[128,2560]{1,0:T(8,128)(2,1)}, u32[]{:S(2)}, u32[]{:S(2)}) collective-permute-start(bf16[128,2560]{1,0:T(8,128)(2,1)S(1)} %get-tuple-element.68), channel_id=1, source_target_pairs={{0,2},{2,0},{1,3},{3,1},{4,6},{6,4},{5,7},{7,5},{8,10},{10,8},{9,1... | collective-permute-start | bytes 1966088 | tf_op jit(solution)/shard_map/ppermute | solution.py:21
  939.0 37.6 %collective-permute-start.164 = (f32[2,2,1280]{2,0,1:T(2,128)S(1)}, f32[2,2,1280]{2,0,1:T(2,128)S(1)}, u32[]{:S(2)}, u32[]{:S(2)}) collective-permute-start(f32[2,2,1280]{2,0,1:T(2,128)S(1)} %pad_maximum_fusion.64), channel_id=1, source_target_pairs={{16,0},{20,4},{24,8},{28,12},{17,1},{21,5},{25,9},{29,13},{18,2},{... | collective-permute-start | bytes 61448 | tf_op jit(solution)/shard_map/ppermute | solution.py:26
  940.3 42.0 %collective-permute-start.165 = (f32[2,2,1280]{2,0,1:T(2,128)S(1)}, f32[2,2,1280]{2,0,1:T(2,128)S(1)}, u32[]{:S(2)}, u32[]{:S(2)}) collective-permute-start(f32[2,2,1280]{2,0,1:T(2,128)S(1)} %pad_maximum_fusion.64), channel_id=1, source_target_pairs={{20,0},{24,4},{28,8},{21,1},{25,5},{29,9},{22,2},{26,6},{30,10},{2... | collective-permute-start | bytes 61448 | tf_op jit(solution)/shard_map/ppermute | solution.py:26
  967.6 117.5 %collective-permute-start.219 = (bf16[320,1536]{1,0:T(8,128)(2,1)}, bf16[320,1536]{1,0:T(8,128)(2,1)}, u32[]{:S(2)}, u32[]{:S(2)}) collective-permute-start(bf16[320,1536]{1,0:T(8,128)(2,1)} %fusion.13), channel_id=1, source_target_pairs={{0,24},{8,0},{16,8},{24,16},{1,25},{9,1},{17,9},{25,17},{2,26},{10... | collective-permute-start | bytes 2949128 | tf_op jit(solution)/shard_map/ppermute | solution.py:26
  976.6 112.2 %collective-permute-start.221 = (bf16[320,1536]{1,0:T(8,128)(2,1)}, bf16[320,1536]{1,0:T(8,128)(2,1)}, u32[]{:S(2)}, u32[]{:S(2)}) collective-permute-start(bf16[320,1536]{1,0:T(8,128)(2,1)} %fusion.15), channel_id=1, source_target_pairs={{0,16},{8,24},{16,0},{24,8},{1,17},{9,25},{17,1},{25,9},{2,18},{10... | collective-permute-start | bytes 2949128 | tf_op jit(solution)/shard_map/ppermute | solution.py:26
  1003.0 63.5 %collective-permute-start.216 = (f32[8,1280]{1,0:T(8,128)S(1)}, f32[8,1280]{1,0:T(8,128)S(1)}, u32[]{:S(2)}, u32[]{:S(2)}) collective-permute-start(f32[8,1280]{1,0:T(8,128)S(1)} %add.1745), channel_id=1, source_target_pairs={{0,24},{8,0},{16,8},{24,16},{1,25},{9,1},{17,9},{25,17},{2,26},{10... | collective-permute-start | bytes 122888 | tf_op jit(solution)/shard_map/ppermute | solution.py:26
  1006.5 65.3 %collective-permute-start.214 = (f32[8,1280]{1,0:T(8,128)S(1)}, f32[8,1280]{1,0:T(8,128)S(1)}, u32[]{:S(2)}, u32[]{:S(2)}) collective-permute-start(f32[8,1280]{1,0:T(8,128)S(1)} %add.1745), channel_id=1, source_target_pairs={{0,8},{8,16},{16,24},{24,0},{1,9},{9,17},{17,25},{25,1},{2,10},{10... | collective-permute-start | bytes 122888 | tf_op jit(solution)/shard_map/ppermute | solution.py:26
  1006.8 65.5 %collective-permute-start.215 = (f32[8,1280]{1,0:T(8,128)S(1)}, f32[8,1280]{1,0:T(8,128)S(1)}, u32[]{:S(2)}, u32[]{:S(2)}) collective-permute-start(f32[8,1280]{1,0:T(8,128)S(1)} %add.1745), channel_id=1, source_target_pairs={{0,16},{8,24},{16,0},{24,8},{1,17},{9,25},{17,1},{25,9},{2,18},{10... | collective-permute-start | bytes 122888 | tf_op jit(solution)/shard_map/ppermute | solution.py:26
  1083.3 76.9 %collective-permute-start.171 = (bf16[2,4,2,80,256]{4,3,2,1,0:T(8,128)(2,1)}, bf16[2,4,2,80,256]{4,3,2,1,0:T(8,128)(2,1)}, u32[]{:S(2)}, u32[]{:S(2)}) collective-permute-start(bf16[2,4,2,80,256]{4,3,2,1,0:T(8,128)(2,1)} %fusion.152), channel_id=1, source_target_pairs={{0,1},{1,0},{2,3},{3,2},{4,5},{5,4},{6,7},{7,6},{8,9},{9,8},{10,11... | collective-permute-start | bytes 1966088 | tf_op jit(solution)/shard_map/ppermute | solution.py:21
  1085.1 89.7 %collective-permute-start.169 = (bf16[128,2560]{1,0:T(8,128)(2,1)}, bf16[128,2560]{1,0:T(8,128)(2,1)S(1)}, u32[]{:S(2)}, u32[]{:S(2)}) collective-permute-start(bf16[128,2560]{1,0:T(8,128)(2,1)} %slice.2045), channel_id=1, source_target_pairs={{0,2},{2,0},{1,3},{3,1},{4,6},{6,4},{5,7},{7,5},{8,10},{10,8},{9,1... | collective-permute-start | bytes 1966088 | tf_op jit(solution)/shard_map/ppermute | solution.py:21
  1088.8 142.0 %collective-permute-start.170 = (bf16[8,2,80,2560]{3,2,1,0:T(8,128)(2,1)}, bf16[8,2,80,2560]{3,2,1,0:T(8,128)(2,1)}, u32[]{:S(2)}, u32[]{:S(2)}) collective-permute-start(bf16[8,2,80,2560]{3,2,1,0:T(8,128)(2,1)} %fusion), channel_id=1, source_target_pairs={{0,1},{1,0},{2,3},{3,2},{4,5},{5,4},{6,7},{7,6},{8,9},{9,8},{10,11... | collective-permute-start | bytes 19660808 | tf_op jit(solution)/shard_map/ppermute | solution.py:21
  (311 other events, 4717.1 us)

commit v2 on v0

--- a/solution.py
+++ b/solution.py
@@ -1,14 +1,975 @@
+import functools
+
 import jax
 import jax.numpy as jnp
 from jax import lax
+from jax.experimental import pallas as pl
+from jax.experimental.pallas import tpu as pltpu
+from jax.sharding import Mesh
 from jax.sharding import PartitionSpec as P
 
 HEADS = 10
 HD = 256
 WIDTH = 4
-
-
+HALO = 16
 EPS = 1e-06
+BF = jnp.bfloat16
+F32 = jnp.float32
+
+
+def swap(value, axis):
+    return lax.ppermute(value, axis, [(0, 1), (1, 0)])
+
+
+def shifted(value, axes, by, count, wrap=False):
+    pairs = [(i, (i + by) % count) for i in range(count) if wrap or 0 <= i + by < count]
+    return lax.ppermute(value, axes, pairs)
+
+
+def pick(flag, first, second):
+    return jnp.where(flag, first, second)
+
+
+def tick(*values):
+    return lax.optimization_barrier(values)
+
+
+def dot(left, right, dims):
+    return lax.dot_general(left, right, (dims, ((), ())), preferred_element_type=F32)
+
+
+def product(left, right):
+    return dot(left, right, ((1,), (0,)))
+
+
+def product_t(left, right):
+    return dot(left, right, ((1,), (1,)))
+
+
+def t_product(left, right):
+    return dot(left, right, ((0,), (0,)))
+
+
+def rms_scale(values, gain_scale):
+    return values * lax.rsqrt(jnp.mean(values * values, axis=-1, keepdims=True) + EPS) * gain_scale
+
+
+def gelu_tanh(values):
+    return jax.nn.gelu(values, approximate=True)
+
+
+def gated_product(left, right):
+    return gelu_tanh(left) * right
+
+
+def gelu_both(v):
+    inner = 0.7978845608028654 * (v + 0.044715 * v * v * v)
+    th = jnp.tanh(inner)
+    value = 0.5 * v * (1.0 + th)
+    slope = 0.5 * (1.0 + th) + 0.5 * v * (1.0 - th * th) * 0.7978845608028654 * (1.0 + 0.134145 * v * v)
+    return value, slope
+
+
+def minus_expm1(v):
+    series = jnp.full_like(v, 1.0)
+    for n in range(11, 1, -1):
+        series = 1.0 + series * v * (1.0 / n)
+    return jnp.where(v > -1.0, -v * series, 1.0 - jnp.exp(v))
+
+
+def two_parts(v):
+    high = v.astype(BF)
+    return high, (v - high.astype(F32)).astype(BF)
+
+
+def wide_dot(left, right, dims):
+    high, low = two_parts(left)
+    return dot(high, right, dims) + dot(low, right, dims)
+
+
+def moved(values, by, fill, rows):
+    count = values.shape[0]
+    rolled = pltpu.roll(values, by % count, 0)
+    inside = rows >= by if by > 0 else rows < count + by
+    return jnp.where(inside, rolled, fill)
+
+
+def scan_rows(decay, drive, rows, backward):
+    step = 1
+    while step < decay.shape[0]:
+        by = -step if backward else step
+        drive = drive + decay * moved(drive, by, 0.0, rows)
+        decay = decay * moved(decay, by, 1.0, rows)
+        step *= 2
+    return decay, drive
+
+
+def conv_taps(rows_ref, halo_ref):
+    rows = rows_ref[0].astype(F32)
+    extended = jnp.concatenate([halo_ref[0].astype(F32), rows], axis=0)
+    count = rows.shape[0]
+    return [rows] + [extended[HALO - k : HALO - k + count] for k in range(1, WIDTH)]
+
+
+def gates(conv_out, gate_ref, prm_ref):
+    nt = ((1,), (1,))
+    high, low = two_parts(conv_out)
+    pre_a = dot(high, gate_ref[0], nt) + dot(low, gate_ref[0], nt) + prm_ref[4:5, :]
+    pre_x = dot(high, gate_ref[1], nt) + dot(low, gate_ref[1], nt) + prm_ref[5:6, :]
+    sig_a = jax.nn.sigmoid(pre_a)
+    sig_x = jax.nn.sigmoid(pre_x)
+    log_decay = -8.0 * sig_a * prm_ref[6:7, :]
+    return sig_a, sig_x, jnp.exp(log_decay), jnp.sqrt(minus_expm1(2.0 * log_decay))
+
+
+def forward_kernel(rows_ref, halo_ref, prm_ref, gate_ref, decay_ref, local_ref, cum_ref):
+    taps = conv_taps(rows_ref, halo_ref)
+    conv_out = sum(prm_ref[k : k + 1, :] * taps[k] for k in range(WIDTH))
+    sig_a, sig_x, decays, root = gates(conv_out, gate_ref, prm_ref)
+    drives = root * sig_x * conv_out
+    decay_ref[0] = decays
+    rows = lax.broadcasted_iota(jnp.int32, decays.shape, 0)
+    cum, local = scan_rows(decays, drives, rows, False)
+    cum_ref[0] = cum
+    local_ref[0] = local
+
+
+def back_scan_kernel(d_mixed_ref, branch_y_ref, states_ref, decay_ref, d_y_ref, local_ref, cum_ref):
+    value, slope = gelu_both(branch_y_ref[0])
+    d_mixed = d_mixed_ref[0]
+    d_y_ref[0] = (d_mixed * states_ref[0] * slope).astype(BF)
+    rows = lax.broadcasted_iota(jnp.int32, d_mixed.shape, 0)
+    coeffs = moved(decay_ref[0], -1, 1.0, rows)
+    cum, local = scan_rows(coeffs, d_mixed * value, rows, True)
+    cum_ref[0] = cum
+    local_ref[0] = local
+
+
+def backward_kernel(
+    rows_ref, halo_ref, prm_ref, gate_ref, local_ref, cum_ref, ends_ref, states_ref,
+    d_conv_ref, d_gate_ref, d_prm_ref,
+):
+    taps = conv_taps(rows_ref, halo_ref)
+    conv_out = sum(prm_ref[k : k + 1, :] * taps[k] for k in range(WIDTH))
+    sig_a, sig_x, decays, root = gates(conv_out, gate_ref, prm_ref)
+    rows = lax.broadcasted_iota(jnp.int32, decays.shape, 0)
+    grad = local_ref[0] + cum_ref[0] * ends_ref[0, 0:1, :]
+    before = jnp.where(rows >= 1, pltpu.roll(states_ref[0], 1, 0), ends_ref[0, 1:2, :])
+    d_log = grad * before * decays - grad * sig_x * conv_out * (decays * decays / root)
+    d_pre_a = d_log * (-8.0 * prm_ref[6:7, :]) * sig_a * (1.0 - sig_a)
+    d_pre_x = grad * root * conv_out * sig_x * (1.0 - sig_x)
+    nn, tn = ((1,), (0,)), ((0,), (0,))
+    a_high, a_low = two_parts(d_pre_a)
+    x_high, x_low = two_parts(d_pre_x)
+    c_high, c_low = two_parts(conv_out)
+    d_conv = grad * root * sig_x
+    d_conv = d_conv + (dot(a_high, gate_ref[0], nn) + dot(a_low, gate_ref[0], nn))
+    d_conv = d_conv + (dot(x_high, gate_ref[1], nn) + dot(x_low, gate_ref[1], nn))
+    d_conv_ref[0] = d_conv
+    d_gate_a = dot(a_high, c_high, tn) + dot(a_low, c_high, tn) + dot(a_high, c_low, tn)
+    d_gate_x = dot(x_high, c_high, tn) + dot(x_low, c_high, tn) + dot(x_high, c_low, tn)
+    total = lambda v: jnp.sum(v, axis=0, keepdims=True)
+    sums = [total(d_conv * taps[k]) for k in range(WIDTH)]
+    sums += [total(d_pre_a), total(d_pre_x), total(d_log * (-8.0 * sig_a))]
+    sums.append(jnp.zeros_like(sums[0]))
+    d_prm = jnp.concatenate(sums, axis=0)
+    first = pl.program_id(1) == 0
+
+    @pl.when(first)
+    def _():
+        d_gate_ref[0] = d_gate_a
+        d_gate_ref[1] = d_gate_x
+        d_prm_ref[...] = d_prm
+
+    @pl.when(jnp.logical_not(first))
+    def _():
+        d_gate_ref[0] += d_gate_a
+        d_gate_ref[1] += d_gate_x
+        d_prm_ref[...] += d_prm
+
+
+def head_specs(tok):
+    rows = pl.BlockSpec((1, tok, HD), lambda h, q: (q, 0, h))
+    halo = pl.BlockSpec((1, HALO, HD), lambda h, q: (q, 0, h))
+    prm = pl.BlockSpec((8, HD), lambda h, q: (0, h))
+    gate = pl.BlockSpec((2, HD, HD), lambda h, q: (0, h, 0))
+    ends = pl.BlockSpec((1, 8, HD), lambda h, q: (q, 0, h))
+    return rows, halo, prm, gate, ends
+
+
+PARAMS = dict(vmem_limit_bytes=48 * 1024 * 1024)
+COST = pl.CostEstimate(flops=0, bytes_accessed=0, transcendentals=0)
+
+
+def forward_call(branch_x, halo, prm, gate):
+    seqs, tok, half = branch_x.shape
+    rows_s, halo_s, prm_s, gate_s, _ = head_specs(tok)
+    out = jax.ShapeDtypeStruct(branch_x.shape, F32)
+    return pl.pallas_call(
+        forward_kernel,
+        grid=(half // HD, seqs),
+        in_specs=[rows_s, halo_s, prm_s, gate_s],
+        out_specs=[rows_s] * 3,
+        out_shape=[out] * 3,
+        compiler_params=pltpu.CompilerParams(**PARAMS),
+        cost_estimate=COST,
+        name="recurrence_forward",
+    )(branch_x, halo, prm, gate)
+
+
+def back_scan_call(d_mixed, branch_y, states, decays):
+    seqs, tok, half = d_mixed.shape
+    rows_s = head_specs(tok)[0]
+    out = jax.ShapeDtypeStruct(d_mixed.shape, F32)
+    return pl.pallas_call(
+        back_scan_kernel,
+        grid=(half // HD, seqs),
+        in_specs=[rows_s] * 4,
+        out_specs=[rows_s] * 3,
+        out_shape=[jax.ShapeDtypeStruct(d_mixed.shape, BF), out, out],
+        compiler_params=pltpu.CompilerParams(**PARAMS),
+        cost_estimate=COST,
+        name="recurrence_back_scan",
+    )(d_mixed, branch_y, states, decays)
+
+
+def backward_call(branch_x, halo, prm, gate, local, cum, ends, states):
+    seqs, tok, half = branch_x.shape
+    rows_s, halo_s, prm_s, gate_s, ends_s = head_specs(tok)
+    return pl.pallas_call(
+        backward_kernel,
+        grid=(half // HD, seqs),
+        in_specs=[rows_s, halo_s, prm_s, gate_s, rows_s, rows_s, ends_s, rows_s],
+        out_specs=[rows_s, gate_s, prm_s],
+        out_shape=[
+            jax.ShapeDtypeStruct(branch_x.shape, F32),
+            jax.ShapeDtypeStruct(gate.shape, F32),
+            jax.ShapeDtypeStruct(prm.shape, F32),
+        ],
+        compiler_params=pltpu.CompilerParams(**PARAMS),
+        cost_estimate=COST,
+        name="recurrence_backward",
+    )(branch_x, halo, prm, gate, local, cum, ends, states)
+
+
+def place_kernel(plan, count_in, *refs):
+    index = {axis: lax.axis_index(axis) for axis in ("z", "x", "y", "c")}
+    for source, start, size, out, target in plan:
+        refs[count_in + out][target(index)] = refs[source][:, start : start + size]
+
+
+def place(plan, pieces, outs, name):
+    whole = pl.BlockSpec(memory_space=pltpu.VMEM)
+    return pl.pallas_call(
+        functools.partial(place_kernel, plan, len(pieces)),
+        in_specs=[whole] * len(pieces),
+        out_specs=[whole] * len(outs),
+        out_shape=[jax.ShapeDtypeStruct(shape, BF) for shape in outs],
+        cost_estimate=COST,
+        compiler_params=pltpu.CompilerParams(**PARAMS),
+        name=name,
+    )(*pieces)
+
+
+def rows_at(block, share, offset=None, size=None):
+    def target(index):
+        rows = pl.ds(pl.multiple_of(block(index) * share, 16), share)
+        if size is None:
+            return rows, slice(None)
+        return rows, pl.ds(offset(index), size)
+
+    return target
+
+
+def home_kernel(zn, fold, count, cols_ff, *refs):
+    lanes = 128
+    for far in range(count):
+        start = lax.rem(lax.axis_index("z") - far + zn, zn) * fold
+        for j in range(fold // lanes):
+            at = start + j * lanes
+
+            @pl.when(at < cols_ff)
+            def _(far=far, j=j, at=at):
+                dest = pl.ds(pl.multiple_of(at, lanes), lanes)
+                for n in range(3):
+                    col = n * fold + j * lanes
+                    refs[count + n][:, dest] = refs[far][:, col : col + lanes].astype(F32)
+
+
+def place_feed_forward_grads(pieces, rows_ff, cols_ff, fold, zn):
+    whole = pl.BlockSpec(memory_space=pltpu.VMEM)
+    return pl.pallas_call(
+        functools.partial(home_kernel, zn, fold, len(pieces), cols_ff),
+        in_specs=[whole] * len(pieces),
+        out_specs=[whole] * 3,
+        out_shape=[jax.ShapeDtypeStruct((rows_ff, cols_ff), F32)] * 3,
+        cost_estimate=COST,
+        compiler_params=pltpu.CompilerParams(**PARAMS),
+        name="place_feed_forward_grads",
+    )(*pieces)
+
+
+TN = ((0,), (0,))
+
+
+def split_blocks(whole_ref, keep_ref, give_ref, share, mine):
+    for j in range(4):
+        ours = pl.multiple_of((2 * j + mine) * share, 8)
+        theirs = pl.multiple_of((2 * j + 1 - mine) * share, 8)
+        keep_ref[0, j] = whole_ref[pl.ds(ours, share), :]
+        give_ref[0, j] = whole_ref[pl.ds(theirs, share), :].astype(BF)
+
+
+def yo_kernel(share, where_ref, normed_ref, mixed_ref, d_y_ref, d_out_ref, keep_ref, give_ref, whole_ref):
+    half = d_y_ref.shape[1]
+    whole_ref[:, :half] = dot(normed_ref[...], d_y_ref[...], TN)
+    whole_ref[:, half:] = dot(mixed_ref[...], d_out_ref[...], TN)
+    split_blocks(whole_ref, keep_ref, give_ref, share, where_ref[1])
+
+
+def xg_kernel(share, where_ref, normed_ref, d_gate_ref, d_x_ref, keep_ref, give_ref, whole_ref):
+    half = d_x_ref.shape[1]
+    whole_ref[:, :half] = dot(normed_ref[...], d_x_ref[...], TN)
+    whole_ref[:, half:] = d_gate_ref[0]
+    split_blocks(whole_ref, keep_ref, give_ref, share, where_ref[1])
+
+
+def term_call(kernel, where, specs, args, first, count, share, columns, name):
+    block = pl.BlockSpec((1, 4, share, columns), lambda n, where: (n, 0, 0, 0))
+    return pl.pallas_call(
+        functools.partial(kernel, share),
+        grid_spec=pltpu.PrefetchScalarGridSpec(
+            num_scalar_prefetch=1,
+            grid=(count,),
+            in_specs=specs,
+            out_specs=[block, block],
+            scratch_shapes=[pltpu.VMEM((8 * share, columns), F32)],
+        ),
+        out_shape=[
+            jax.ShapeDtypeStruct((count, 4, share, columns), F32),
+            jax.ShapeDtypeStruct((count, 4, share, columns), BF),
+        ],
+        cost_estimate=COST,
+        compiler_params=pltpu.CompilerParams(**PARAMS),
+        name=name,
+    )(where, *args)
+
+
+def ff_kernel(steps, fold, where_ref, *refs):
+    rows, cots, hidden, d_gu = (refs[n * steps : (n + 1) * steps] for n in range(4))
+    keep_ref, give_ref, whole_ref = refs[4 * steps :]
+    first = second = 0.0
+    for k in range(steps):
+        first = first + dot(rows[k][...], d_gu[k][...], TN)
+        second = second + dot(cots[k][...], hidden[k][...], TN)
+    whole_ref[:, : 2 * fold] = first
+    whole_ref[:, 2 * fold :] = second
+    size = keep_ref.shape[1]
+    mine = where_ref[2]
+    keep_ref[0] = whole_ref[pl.ds(pl.multiple_of(mine * size, 8), size), :]
+    give_ref[0] = whole_ref[pl.ds(pl.multiple_of((1 - mine) * size, 8), size), :].astype(BF)
+
+
+def ff_grads_call(where, rows, cots, hidden, d_gu, zn, rows_ff):
+    steps, fold = len(rows), hidden[0].shape[1]
+    count = rows[0].shape[0]
+    part = pl.BlockSpec((count, 2 * rows_ff), lambda far, where: (0, lax.rem(where[0] + far, zn)))
+    whole = lambda item: pl.BlockSpec(item.shape, lambda far, where: (0, 0))
+    block = pl.BlockSpec((1, rows_ff, 3 * fold), lambda far, where: (far, 0, 0))
+    shape = (zn, rows_ff, 3 * fold)
+    return pl.pallas_call(
+        functools.partial(ff_kernel, steps, fold),
+        grid_spec=pltpu.PrefetchScalarGridSpec(
+            num_scalar_prefetch=1,
+            grid=(zn,),
+            in_specs=[part] * (2 * steps) + [whole(item) for item in (*hidden, *d_gu)],
+            out_specs=[block, block],
+            scratch_shapes=[pltpu.VMEM((2 * rows_ff, 3 * fold), F32)],
+        ),
+        out_shape=[jax.ShapeDtypeStruct(shape, F32), jax.ShapeDtypeStruct(shape, BF)],
+        cost_estimate=COST,
+        compiler_params=pltpu.CompilerParams(**PARAMS),
+        name="feed_forward_grads",
+    )(where, *rows, *cots, *hidden, *d_gu)
+
+
+def carried(decay, drive, zn, x, by):
+    own = jnp.stack([decay, drive])
+    beside = swap(own, "x")
+    inner = x == 0 if by > 0 else x == 1
+    near, far = pick(inner, own, beside), pick(inner, beside, own)
+    pair = jnp.stack([near[0] * far[0], near[1] * far[0] + far[1]])
+    came = [shifted(pair, "z", by * dist, zn) for dist in range(zn - 1, 0, -1)]
+    state = jnp.zeros_like(drive)
+    for part in came:
+        state = part[0] * state + part[1]
+    return pick(inner, state, near[0] * state + near[1])
+
+
+def per_device(
+    zn, fold,
+    tokens, w_x, w_y, w_out, gate_w, gain_in, gain_mlp, conv_w, gate_b, rate,
+    w_gate, w_up, w_down, cotangent,
+):
+    z, x, y, c = (lax.axis_index(axis) for axis in ("z", "x", "y", "c"))
+    zh = zn // 2
+    seq_count = 2 * zn
+    tok, width = tokens.shape[1], tokens.shape[2]
+    share, wide_r = w_x.shape
+    half = wide_r // 2
+    rows_ff, cols_ff = w_gate.shape
+    zx, zy = ("z", "x"), ("z", "y")
+    z_of = [lax.rem(z - k + zn, zn) for k in range(zn)]
+    lanes = 128
+    every = range(zn)
+    hop = lambda value: shifted(value, "z", 1, zn, True)
+
+    spread = []
+    for other in (0, 1):
+        pairs = []
+        for h in (0, 1):
+            for zl in range(zh):
+                for ys in (0, 1):
+                    k = ys ^ other
+                    pairs.append(((h * zh + zl) * 2 + ys, (k * zh + zl) * 2 + h))
+        spread.append(pairs)
+    gathered_back = [[(b, a) for a, b in pairs] for pairs in spread]
+    own_half = lambda w: pick(y == 0, w[:, :half], w[:, half:])
+    other_half = lambda w: pick(y == 0, w[:, half:], w[:, :half])
+
+    def source(k, across, other):
+        def at(i):
+            flip = lambda value, on: 1 - value if on else value
+            return lax.rem(i["z"] - k + zn, zn), flip(i["x"], across), flip(i["c"], other)
+
+        return at
+
+    def by_rows(at, beside):
+        def block(i):
+            sz, sx, sc = at(i)
+            return ((sz * 2 + sx) * 2 + (1 - i["y"] if beside else i["y"])) * 2 + sc
+
+        return block
+
+    def by_spread(at, second):
+        def block(i):
+            sz, sx, sc = at(i)
+            sh = sz // zh
+            return ((lax.rem(sz, zh) * 2 + sx) * 2 + (1 - sh if second else sh)) * 2 + sc
+
+        return block
+
+    def gate_at(at, second):
+        rows = by_spread(at, second)
+
+        def target(i):
+            start = pl.multiple_of(rows(i) * share, 16)
+            return at(i)[0] // zh, pl.ds(start, share), slice(None)
+
+        return target
+
+    params = jnp.concatenate([gain_in[None], gain_mlp[None], conv_w, gate_b, rate[None]])
+    count_p = params.shape[0]
+    params = jnp.pad(params.T, ((0, 0), (0, lanes - count_p)))
+    gate_t = gate_w.transpose(0, 2, 1)
+    gate_pieces = [
+        lax.ppermute(pick(y == 0, gate_t[k], gate_t[1 - k]), zy, spread[k]) for k in (0, 1)
+    ]
+    wide_x = half + lanes
+    x_own = jnp.concatenate([own_half(w_x), params], axis=1)
+    x_other = swap(jnp.concatenate([other_half(w_x), params], axis=1), "y")
+    unit_x = jnp.concatenate([x_own, x_other, gate_pieces[0], gate_pieces[1]], axis=1)
+    tok_own, cot = tokens[0], cotangent[0]
+    cot_z, cot_y = [cot], {}
+    unit_x, w_y, w_out, tok_own, ff_raw = tick(unit_x, w_y, w_out, tok_own, (w_gate, w_up, w_down))
+
+    a_z, a_x, a_zc, a_xc = [unit_x], [], [], []
+    padded = zn * fold
+    widen = lambda w: jnp.pad(w, ((0, 0), (0, padded - cols_ff)))
+    ff_wide = [widen(ff_raw[0]), widen(ff_raw[1]), widen(ff_raw[2].T)]
+
+    def ff_piece(z_at):
+        return jnp.concatenate(
+            [lax.dynamic_slice_in_dim(w, z_at * fold, fold, 1) for w in ff_wide], axis=1
+        )
+
+    ff_units = [ff_piece(lax.rem(z + far, zn)) for far in every]
+    for k in range(1, zn):
+        a_z.append(hop(a_z[-1]))
+        a_x.append(swap(a_z[k - 1], "x"))
+        a_zc.append(swap(a_z[k - 1], "c"))
+        if k > 1:
+            a_xc.append(swap(a_x[k - 2], "c"))
+        if k == 1:
+            tok_other = swap(tok_own, "y")
+            a_z, a_x, w_y, w_out, tok_own = tick(a_z, a_x, w_y, w_out, tok_own)
+            y_other = swap(other_half(w_y), "y")
+            out_halves = [w_out[:, :half], w_out[:, half:]]
+            out_parts = [
+                lax.ppermute(pick(y == 0, out_halves[i], out_halves[1 - i]), zy, spread[i])
+                for i in (0, 1)
+            ]
+        elif k == 2:
+            a_z, a_x, tok_own, tok_other, y_other, out_parts = tick(
+                a_z, a_x, tok_own, tok_other, y_other, out_parts
+            )
+        else:
+            a_z, a_x = tick(a_z, a_x)
+    tok_f = jnp.stack([tok_own, tok_other]).astype(F32)
+    unit_yo = jnp.concatenate([own_half(w_y), y_other, out_parts[0], out_parts[1]], axis=1)
+    unit_yo, a_z = tick(unit_yo, a_z)
+
+    b_z, b_x, b_zc, b_xc = [unit_yo, hop(unit_yo)], [], [], []
+    a_x.append(swap(a_z[-1], "x"))
+    a_zc.append(swap(a_z[-1], "c"))
+    a_xc.append(swap(a_x[-2], "c"))
+    a_x, a_zc, a_xc, unit_yo, ff_units = tick(a_x, a_zc, a_xc, b_z[0], ff_units)
+    b_z[0] = unit_yo
+    a_xc.append(swap(a_x[-1], "c"))
+    b_x.append(swap(b_z[0], "x"))
+    placed, plan = [], []
+    for k in every:
+        for j, part in enumerate((a_z[k], a_zc[k], a_x[k], a_xc[k])):
+            at = source(k, j >= 2, j % 2)
+            n = len(placed)
+            placed.append(part)
+            for beside in (0, 1):
+                block = by_rows(at, beside)
+                plan.append((n, beside * wide_x, half, 0, rows_at(block, share)))
+                plan.append((n, beside * wide_x + half, lanes, 1, rows_at(block, share)))
+                plan.append((n, 2 * wide_x + beside * HD, HD, 2, gate_at(at, beside)))
+    full_x, full_p, gates_t = place(
+        plan, placed, [(width, half), (width, lanes), (2, half, HD)], "place_w_x"
+    )
+    smalls = full_p[:, :count_p].astype(F32).T
+    gain_first, gain_second = smalls[0], smalls[1]
+    prm = jnp.pad(smalls[2:], ((0, 1), (0, 0)))
+    prm = pick(y == 0, prm[:, :half], prm[:, half:])
+    normed = rms_scale(tok_f, gain_first).astype(BF).reshape(2 * tok, width)
+    branch_x = product(normed, full_x).astype(BF).reshape(2, tok, half)
+
+    branch_x, b_z = tick(branch_x, b_z)
+    b_z.append(hop(b_z[-1]))
+    b_x.append(swap(b_z[1], "x"))
+    b_zc += [swap(b_z[0], "c"), swap(b_z[1], "c")]
+    halo = shifted(branch_x[:, tok - HALO :], zx, 1, seq_count)
+    halo, b_z, b_x = tick(halo, b_z, b_x)
+    for k in range(3, zn):
+        b_z.append(hop(b_z[-1]))
+        b_x.append(swap(b_z[k - 1], "x"))
+        b_zc.append(swap(b_z[k - 1], "c"))
+        b_xc.append(swap(b_x[k - 3], "c"))
+        if k == 3:
+            decays, local, cum = tick(*forward_call(branch_x, halo, prm, gates_t))
+            state_in = carried(cum[:, -1], local[:, -1], zn, x, 1)
+            state_in, b_z, b_x = tick(state_in, b_z, b_x)
+        else:
+            b_z, b_x = tick(b_z, b_x)
+    turns = [
+        [(far, None) for far in range(1, zn) if far % 3 == 1],
+        [(far, 0) for far in range(1, zn) if far % 3 == 2],
+        [(far, 1) for far in range(1, zn) if far % 3 == 2],
+        [(far, None) for far in range(1, zn) if far % 3 == 0],
+    ]
+
+    def sent_along(blocks, turn):
+        sent = {}
+        for far, part in turns[turn]:
+            block = blocks[far]
+            cut = block.shape[1] // 2
+            if part is not None:
+                block = block[:, :cut] if part == 0 else block[:, cut:]
+            sent[far, part] = shifted(block, "z", far, zn, True)
+        return sent
+
+    def joined(came, fars):
+        return {
+            far: came[far, None] if (far, None) in came
+            else jnp.concatenate([came[far, 0], came[far, 1]], axis=1)
+            for far in fars
+        }
+
+    far_of = lambda turn: [far for far, _ in turns[turn]]
+    ff_units, b_z = tick(ff_units, b_z)
+    ff_came, ff_x = sent_along(ff_units, 0), {}
+    b_x.append(swap(b_z[-1], "x"))
+    b_zc.append(swap(b_z[-1], "c"))
+    b_xc += [swap(b_x[-3], "c"), swap(b_x[-2], "c")]
+    b_x, cot_z, cot_y, ff_units, ff_came = tick(b_x, cot_z, cot_y, ff_units, ff_came)
+
+    ff_came.update(sent_along(ff_units, 1))
+    ff_x[0] = swap(ff_units[0], "x")
+    cot_y[0] = swap(cot_z[0], "y")
+    b_xc.append(swap(b_x[-1], "c"))
+    placed, plan = [], []
+    for k in every:
+        for j, part in enumerate((b_z[k], b_zc[k], b_x[k], b_xc[k])):
+            at = source(k, j >= 2, j % 2)
+            n = len(placed)
+            placed.append(part)
+            column = lambda i, at=at: pl.multiple_of((at(i)[0] // zh) * half, lanes)
+            for beside in (0, 1):
+                plan.append((n, beside * half, half, 0, rows_at(by_rows(at, beside), share)))
+                plan.append(
+                    (n, (2 + beside) * half, half, 1, rows_at(by_spread(at, beside), share, column, half))
+                )
+    full_y, full_out = place(plan, placed, [(width, half), (half, width)], "place_w_y_w_out")
+    branch_y = product(normed, full_y).reshape(2, tok, half)
+    states = local + cum * state_in[:, None]
+    mixed = (states * gelu_tanh(branch_y)).astype(BF).reshape(2 * tok, half)
+    out_sum = product(mixed, full_out)
+    out_own, out_give = out_sum[:tok], out_sum[tok:].astype(BF)
+    out_own, out_give, ff_came, ff_x, ff_units, cot_z, cot_y = tick(
+        out_own, out_give, ff_came, ff_x, ff_units, cot_z, cot_y
+    )
+    out_came = swap(out_give, "y")
+    ff_came.update(sent_along(ff_units, 2))
+    ff_x.update({far: swap(piece, "x") for far, piece in joined(ff_came, far_of(0)).items()})
+    cot_z.append(hop(cot_z[0]))
+    out_came, out_own, ff_came, ff_x, ff_units, cot_z = tick(
+        out_came, out_own, ff_came, ff_x, ff_units, cot_z
+    )
+    residual = tok_own.astype(F32) + out_own + out_came.astype(F32)
+    normed_mlp = rms_scale(residual, gain_second).astype(BF)
+
+    row_z, row_y = [normed_mlp, hop(normed_mlp)], {0: swap(normed_mlp, "y")}
+    ff_came.update(sent_along(ff_units, 3))
+    ff_x.update({far: swap(piece, "x") for far, piece in joined(ff_came, far_of(1)).items()})
+    cot_y[1] = swap(cot_z[1], "y")
+    row_z, row_y, cot_z, cot_y, ff_came, ff_x = tick(row_z, row_y, cot_z, cot_y, ff_came, ff_x)
+    ff_x.update({far: swap(piece, "x") for far, piece in joined(ff_came, far_of(3)).items()})
+    row_z.append(hop(row_z[-1]))
+    cot_z.append(hop(cot_z[-1]))
+    row_y[1] = swap(row_z[1], "y")
+    row_z, row_y, cot_z, ff_x = tick(row_z, row_y, cot_z, ff_x)
+    ff_pieces = joined(ff_came, range(1, zn))
+    ff_pieces[0] = ff_units[0]
+    placed, plan = [], []
+    for k in every:
+        for across, part in enumerate((ff_pieces[k], ff_x[k])):
+            at = source(k, across, 0)
+            block = lambda i, at=at: at(i)[0] * 2 + at(i)[1]
+            n = len(placed)
+            placed.append(part)
+            plan.append((n, 0, 2 * fold, 0, rows_at(block, rows_ff)))
+            plan.append((n, 2 * fold, fold, 1, rows_at(block, rows_ff)))
+    w_gu, w_dt = place(plan, placed, [(width, 2 * fold), (width, fold)], "place_feed_forward")
+
+    def with_cores(pair):
+        return jnp.concatenate(list(pair) + [swap(part, "c") for part in pair])
+
+    def feed_forward(k):
+        rows, grads = with_cores((row_z[k], row_y[k])), with_cores((cot_z[k], cot_y[k]))
+        gu = product(rows, w_gu)
+        d_hidden = product(grads, w_dt)
+        hidden, pull = jax.vjp(gated_product, gu[:, :fold], gu[:, fold:])
+        d_gu = jnp.concatenate([item.astype(BF) for item in pull(d_hidden)], axis=1)
+        return rows, grads, hidden.astype(BF), d_gu, product_t(d_gu, w_gu).reshape(4, tok, width)
+
+    steps, d_parts, d_c, d_y, total = {}, {}, {}, {}, None
+    m_parts, m_c, m_y, m_total = {}, {}, {}, None
+
+    def core_give(parts):
+        return parts[2:].astype(BF)
+
+    def y_give(parts, came_c):
+        return (parts[1] + came_c[1].astype(F32)).astype(BF)
+
+    def own_sum(parts, came_c, came_y):
+        return parts[0] + came_c[0].astype(F32) + came_y.astype(F32)
+
+    where = jnp.stack([z, c, x]).astype(jnp.int32)
+    order = list(range(1, zn)) + [0]
+    for i in range(zn + 2):
+        if i < zn:
+            k = order[i]
+            steps[k] = feed_forward(k)
+            d_parts[k] = steps[k][-1]
+        if k + 2 < zn and i < zn - 1:
+            row_z.append(hop(row_z[-1]))
+        if k + 2 < zn and i < zn - 1:
+            cot_z.append(hop(cot_z[-1]))
+        if i < zn - 2:
+            row_y[k + 1] = swap(row_z[k + 1], "y")
+            cot_y[k + 1] = swap(cot_z[k + 1], "y")
+        if i < 2 or i == zn + 1:
+            for n in [k] if i < 2 else order[2:]:
+                m_parts[n] = product_t(steps[n][2], w_dt).reshape(4, tok, width)
+        if 1 <= i <= 2:
+            m_c[order[i - 1]] = swap(core_give(m_parts[order[i - 1]]), "c")
+        if 1 <= i <= zn:
+            d_c[order[i - 1]] = swap(core_give(d_parts[order[i - 1]]), "c")
+        if 2 <= i:
+            k = order[i - 2]
+            d_y[k] = swap(y_give(d_parts[k], d_c[k]), "y")
+        if 3 <= i:
+            k = order[i - 3]
+            term = own_sum(d_parts[k], d_c[k], d_y[k])
+            total = hop((term if total is None else total.astype(F32) + term).astype(BF))
+        if i in (2, 4):
+            k = order[i // 2 - 1]
+            m_y[k] = swap(y_give(m_parts[k], m_c[k]), "y")
+        if i == 4:
+            m_total = hop(own_sum(m_parts[1], m_c[1], m_y[1]).astype(BF))
+        if i == zn:
+            ff_keep, ff_give = tick(*ff_grads_call(
+                where, *([steps[k][n] for k in every] for n in range(4)), zn, rows_ff
+            ))
+            ff_give = {far: ff_give[far] for far in every}
+        if i == zn + 1:
+            break
+        steps, row_z, row_y, cot_z, cot_y, d_parts, d_c, d_y, total, m_parts, m_c, m_y, m_total = tick(
+            steps, row_z, row_y, cot_z, cot_y, d_parts, d_c, d_y, total, m_parts, m_c, m_y, m_total
+        )
+        steps = {k: step[:4] for k, step in steps.items()}
+
+    ff_sent, ff_home = {}, {}
+
+    def cut_block(block, part):
+        middle = 3 * fold // 2
+        return block if part is None else block[:, :middle] if part == 0 else block[:, middle:]
+
+    def give_across(turn):
+        for far, part in turn:
+            ff_sent[far, part] = swap(cut_block(ff_give[far], part), "x")
+
+    def own_and_sent(far, part):
+        return (cut_block(ff_keep[far], part) + ff_sent[far, part].astype(F32)).astype(BF)
+
+    def send_home(turn):
+        for far, part in turns[turn]:
+            ff_home[far, part] = shifted(own_and_sent(far, part), "z", far, zn, True)
+
+    give_across(turns[3] + turns[1])
+    total, d_y, ff_sent, ff_give, m_total, m_parts = tick(total, d_y, ff_sent, ff_give, m_total, m_parts)
+
+    d_normed_mlp = own_sum(d_parts[0], d_c[0], d_y[0]) + total.astype(F32)
+    unused, second_pull = jax.vjp(rms_scale, residual, gain_second)
+    d_res_norm, d_gain_mlp = second_pull(d_normed_mlp)
+    d_residual = cot.astype(F32) + d_res_norm
+    d_branch = d_residual.astype(BF)
+    d_other = swap(d_branch, "y")
+    send_home(3)
+    give_across(turns[2])
+    for k in order[2:]:
+        m_c[k] = swap(core_give(m_parts[k]), "c")
+    d_branch, d_other, ff_sent, ff_give, m_total, m_c = tick(d_branch, d_other, ff_sent, ff_give, m_total, m_c)
+
+    d_branch_pair = jnp.concatenate([d_branch, d_other])
+    d_mixed = product_t(d_branch_pair, full_out).reshape(2, tok, half)
+    d_branch_y, local_back, cum_back = back_scan_call(d_mixed, branch_y, states, decays)
+    leaving = decays[:, 0] * local_back[:, 0]
+    for k in order[2:]:
+        m_y[k] = swap(y_give(m_parts[k], m_c[k]), "y")
+    send_home(1)
+    give_across(turns[0])
+    d_flat_y = d_branch_y.reshape(2 * tok, half)
+    eight = 8 * share
+    z_at = lambda n, where, first: lax.rem(where[0] - n - first + 2 * zn, zn)
+    full_spec = pl.BlockSpec((2 * tok, half), lambda n, where: (0, 0))
+
+    def yo_terms(first, count):
+        specs = [
+            pl.BlockSpec((2 * tok, eight), lambda n, where: (0, z_at(n, where, first))),
+            pl.BlockSpec((2 * tok, eight), lambda n, where: (0, lax.rem(z_at(n, where, first), zh))),
+            full_spec,
+            pl.BlockSpec((2 * tok, half), lambda n, where: (0, z_at(n, where, first) // zh)),
+        ]
+        args = (normed, mixed, d_flat_y, d_branch_pair)
+        return term_call(yo_kernel, where, specs, args, first, count, share, 2 * half, "grad_w_y_w_out")
+
+    def x_terms(first, count):
+        specs = [
+            pl.BlockSpec((2 * tok, eight), lambda n, where: (0, z_at(n, where, first))),
+            pl.BlockSpec(
+                (1, eight, HD),
+                lambda n, where: (z_at(n, where, first) // zh, lax.rem(z_at(n, where, first), zh), 0),
+            ),
+            full_spec,
+        ]
+        args = (normed, d_gates, d_flat_x)
+        return term_call(xg_kernel, where, specs, args, first, count, share, half + HD, "grad_w_x")
+
+    yo_a = yo_terms(1, 2)
+    leaving, d_branch_y, yo_a, m_y, m_total, ff_home, ff_sent, ff_give = tick(
+        leaving, d_branch_y, yo_a, m_y, m_total, ff_home, ff_sent, ff_give
+    )
+
+    carry_back = carried(cum[:, -1], leaving, zn, x, -1)
+    ends = jnp.pad(jnp.stack([carry_back, state_in], axis=1), ((0, 0), (0, 6), (0, 0)))
+    yo_ac = swap(yo_a[1], "c")
+    ends, yo_a, yo_ac, d_flat_y, ff_sent, ff_give, m_y, m_total = tick(
+        ends, yo_a, yo_ac, d_flat_y, ff_sent, ff_give, m_y, m_total
+    )
+
+    yo, xg = {}, {}
+
+    def hold(terms, kept, came, first):
+        for n in range(came.shape[0]):
+            terms[(first + n) % zn] = (kept, came, n)
+
+    def at_x(term, which):
+        kept, came, n = term
+        part = lambda v: lax.dynamic_slice(
+            v.reshape((-1, 2, 2) + v.shape[2:]), (n, which, 0, 0, 0), (1, 1, 2) + v.shape[2:]
+        )[0, 0]
+        return part(kept) + part(came).astype(F32)
+
+    def x_give(term):
+        return at_x(term, 1 - x).astype(BF)
+
+    hold(yo, yo_a[0], yo_ac, 1)
+    yo_x = {1: swap(x_give(yo[1]), "x")}
+    send_home(2)
+    d_conv, d_gates, d_prm = tick(*backward_call(
+        branch_x, halo, prm, gates_t, local_back, cum_back, ends, states
+    ))
+    rim = shifted(d_conv[:, :8], zx, -1, seq_count)
+    yo_b = yo_terms(3, zn - 2)
+    rim, yo_x, yo_b, ff_home, ff_sent, ff_give, m_total, m_y = tick(
+        rim, yo_x, yo_b, ff_home, ff_sent, ff_give, m_total, m_y
+    )
+    yo_bc = swap(yo_b[1], "c")
+
+    d_ext = jnp.concatenate([d_conv, rim], axis=1)
+    d_branch_x = sum(prm[k] * d_ext[:, k : k + tok] for k in range(WIDTH)).astype(BF)
+    d_flat_x = d_branch_x.reshape(2 * tok, half)
+
+    def add(total, terms, came_x, k):
+        return total.astype(F32) + at_x(terms[k], x) + came_x[k].astype(F32)
+
+    def return_rows(sums):
+        mine = z // zh
+        return [
+            lax.ppermute(
+                lax.dynamic_index_in_dim(sums, mine if k == 0 else 1 - mine, 0, False).astype(BF),
+                zy, gathered_back[k],
+            )
+            for k in (0, 1)
+        ]
+
+    def returned_rows(came):
+        came = [item.astype(F32) for item in came]
+        return pick(y == 0, came[0], came[1]), pick(y == 0, came[1], came[0])
+
+    def return_columns(sums):
+        return swap(lax.dynamic_index_in_dim(sums, 1 - y, 0, False).astype(BF), "y")
+
+    def returned_columns(sums, came):
+        mine, across = lax.dynamic_index_in_dim(sums, y, 0, False), came.astype(F32)
+        return jnp.concatenate([pick(y == 0, mine, across), pick(y == 0, across, mine)], axis=1)
+
+    xg_x, xg_total = {}, None
+    zero = jnp.zeros((), F32)
+    yo_total = add(zero, yo, yo_x, 1)
+    for t in range(zn + 1):
+        if t < zn - 1:
+            if t == 0:
+                yo_total = hop(yo_total.astype(BF))
+            else:
+                k = order[t]
+                m_total = m_total.astype(F32) + own_sum(m_parts[k], m_c[k], m_y[k])
+                rows = 2 * share
+                both = jnp.concatenate([yo_total.astype(BF).reshape(rows, -1), m_total.astype(BF)])
+                both = hop(both)
+                yo_total, m_total = both[:rows].reshape(2, share, -1), both[rows:]
+            k = order[t + 1]
+            yo_x[k] = swap(x_give(yo[k]), "x")
+        if t >= 2:
+            xg_total = hop(xg_total.astype(BF))
+        if t in (1, 2):
+            pair = order[:2] if t == 1 else order[2:]
+            came = swap(jnp.stack([x_give(xg[k]) for k in pair]), "x")
+            xg_x.update({k: came[i] for i, k in enumerate(pair)})
+        if t == 0:
+            send_home(0)
+            xg_a = x_terms(1, zn)
+            xg_ac = swap(xg_a[1], "c")
+        elif t == 1:
+            d_normed = product_t(d_flat_x, full_x) + product_t(d_flat_y, full_y)
+            d_came = swap(d_normed[tok:].astype(BF), "y")
+        elif t == 2:
+            unused, first_pull = jax.vjp(rms_scale, tok_own.astype(F32), gain_first)
+            d_tok, d_gain_in = first_pull(d_normed[:tok] + d_came.astype(F32))
+            tokens_grad = (d_residual + d_tok)[None]
+            small = jnp.concatenate([d_prm, jnp.stack([d_gain_in, d_gain_mlp]).reshape(4, half)])
+            small = small + swap(small, "c")
+        elif t == 3:
+            small = small + swap(small, "x")
+            give_across([(0, None)])
+        if t == zn - 1:
+            out_came = return_rows(yo_total[:, :, half:])
+        if t == zn:
+            y_came = return_columns(yo_total[:, :, :half])
+        if t == zn:
+            small = small + sum(shifted(small, "z", by, zn, True) for by in range(1, zn))
+            ff_home = joined(ff_home, range(1, zn))
+            ff_home[0] = own_and_sent(0, None)
+            g_gate, g_up, g_down = place_feed_forward_grads(
+                [ff_home[far] for far in every], rows_ff, cols_ff, fold, zn,
+            )
+        if t == 0:
+            yo_x, yo_total, xg_a, xg_ac, yo_bc, d_flat_y = tick(
+                yo_x, yo_total, xg_a, xg_ac, yo_bc, d_flat_y
+            )
+            hold(yo, yo_b[0], yo_bc, 3)
+            hold(xg, xg_a[0], xg_ac, 1)
+        elif t == 1:
+            yo_x, yo_total, xg_x, d_normed, d_came, ff_home, m_total, xg_a, xg_ac, ff_give = tick(
+                yo_x, yo_total, xg_x, d_normed, d_came, ff_home, m_total, xg_a, xg_ac, ff_give
+            )
+            hold(xg, xg_a[0], xg_ac, 1)
+            xg_total = add(zero, xg, xg_x, 1)
+        elif t < zn:
+            if t == 2:
+                yo_x, yo_total, xg_x, xg_total, small, m_total = tick(
+                    yo_x, yo_total, xg_x, xg_total, small, m_total
+                )
+                m_term = own_sum(m_parts[0], m_c[0], m_y[0])
+                result = (residual + m_total.astype(F32) + m_term).astype(BF)[None]
+            else:
+                yo_total, xg_x, xg_total, small, out_came, ff_sent = tick(
+                    yo_total, xg_x, xg_total, small, out_came, ff_sent
+                )
+        else:
+            xg_x, xg_total, small, y_came, out_came, yo_total = tick(
+                xg_x, xg_total, small, y_came, out_came, yo_total
+            )
+        if t >= 2:
+            xg_total = add(xg_total, xg, xg_x, order[t - 1])
+        if t < zn - 1:
+            yo_total = add(yo_total, yo, yo_x, order[t + 1])
+    grad_w_x = returned_columns(xg_total[:, :, :half], return_columns(xg_total[:, :, :half]))
+    grad_gate_w = jnp.stack(returned_rows(return_rows(xg_total[:, :, half:]))).transpose(0, 2, 1)
+    grad_w_y = returned_columns(yo_total[:, :, :half], y_came)
+    grad_w_out = jnp.concatenate(returned_rows(out_came), axis=1)
+
+    beside = swap(small, "y")
+    both_halves = jnp.concatenate(
+        [pick(y == 0, small, beside)[:8], pick(y == 0, beside, small)[:8]], axis=1
+    )
+    gains = (small + beside)[8:].reshape(2, 2 * half)
+    at = ((z * 2 + x) * 4 + y * 2 + c) * share
+    own_small = lax.dynamic_slice_in_dim(both_halves, at, share, 1)
+    own_gain = lax.dynamic_slice_in_dim(gains, at, share, 1)
+    return (
+        result,
+        tokens_grad,
+        grad_w_x,
+        grad_w_y,
+        grad_w_out,
+        grad_gate_w,
+        own_gain[0],
+        own_gain[1],
+        own_small[:WIDTH],
+        own_small[WIDTH : WIDTH + 2],
+        own_small[WIDTH + 2],
+        g_gate,
+        g_up,
+        g_down.T,
+    )
+
+
 PRECISE = lax.Precision.HIGHEST
 
 
@@ -33,22 +994,6 @@
         return jax.tree.map(lambda new, old: jnp.where(position < mine, new, old), longer, total)
 
     return lax.fori_loop(0, count - 1, step, total)
-
-
-def product(left, right):
-    return jnp.dot(left, right, preferred_element_type=jnp.float32)
-
-
-def rms_scale(values, gain_scale):
-    return values * lax.rsqrt(jnp.mean(values * values, axis=-1, keepdims=True) + EPS) * gain_scale
-
-
-def gelu_tanh(values):
-    return jax.nn.gelu(values, approximate=True)
-
-
-def gated_product(left, right):
-    return gelu_tanh(left) * right
 
 
 def affine_pair(earlier, latter):
@@ -147,7 +1092,7 @@
     return tuple((merge_owner(item, dim) for item, dim in zip(summed, dims)))
 
 
-def per_device(
+def per_device_gathered(
     tokens,
     w_x,
     w_y,
@@ -283,42 +1228,41 @@
     )
 
 
+def by_mesh_axes(specs):
+    names = {("z", "x"): "seq", ("y", "c"): "fsdp", ("z", "x", "y", "c"): ("seq", "fsdp"), None: None}
+    return tuple(P(*(names[entry] for entry in spec)) for spec in specs)
+
+
 def solution(mesh):
+    seq_count, pair_count = mesh.shape["seq"], mesh.shape["fsdp"]
+    zn = seq_count // 2
+    grid = Mesh(mesh.devices.reshape(zn, 2, pair_count // 2, 2), ("z", "x", "y", "c"))
+    seq, fsdp, both = ("z", "x"), ("y", "c"), ("z", "x", "y", "c")
+    rows = P(fsdp, seq, None)
+    by_row = P(both, None)
+    by_col = P(None, both)
     placed = (
-        P("fsdp", "seq", None),
-        P(("seq", "fsdp"), None),
-        P(("seq", "fsdp"), None),
-        P(("seq", "fsdp"), None),
-        P(None, None, ("seq", "fsdp")),
-        P(("seq", "fsdp")),
-        P(("seq", "fsdp")),
-        P(None, ("seq", "fsdp")),
-        P(None, ("seq", "fsdp")),
-        P(("seq", "fsdp")),
-        P("seq", "fsdp"),
-        P("seq", "fsdp"),
-        P("fsdp", "seq"),
-        P("fsdp", "seq", None),
-    )
-    return jax.shard_map(
-        per_device,
-        mesh=mesh,
-        in_specs=placed,
-        out_specs=(
-            P("fsdp", "seq", None),
-            P("fsdp", "seq", None),
-            P(("seq", "fsdp"), None),
-            P(("seq", "fsdp"), None),
-            P(("seq", "fsdp"), None),
-            P(None, None, ("seq", "fsdp")),
-            P(("seq", "fsdp")),
-            P(("seq", "fsdp")),
-            P(None, ("seq", "fsdp")),
-            P(None, ("seq", "fsdp")),
-            P(("seq", "fsdp")),
-            P("seq", "fsdp"),
-            P("seq", "fsdp"),
-            P("fsdp", "seq"),
-        ),
-        check_vma=False,
-    )
+        rows, by_row, by_row, by_row, P(None, None, both), P(both), P(both), by_col, by_col, P(both),
+        P(seq, fsdp), P(seq, fsdp), P(fsdp, seq), rows,
+    )
+    out_specs = (
+        rows, rows, by_row, by_row, by_row, P(None, None, both), P(both), P(both), by_col, by_col,
+        P(both), P(seq, fsdp), P(seq, fsdp), P(fsdp, seq),
+    )
+
+    lanes = 128
+
+    def run(*args):
+        width = args[0].shape[2]
+        whole_tiles = width % (16 * mesh.size) == 0 and 2 * width % (lanes * seq_count) == 0
+        if whole_tiles and zn >= 4:
+            hidden_share = args[10].shape[1] // pair_count
+            fold = -(-hidden_share // (lanes * zn)) * lanes
+            program = functools.partial(per_device, zn, fold)
+            on, ins, outs = grid, placed, out_specs
+        else:
+            program, on = per_device_gathered, mesh
+            ins, outs = by_mesh_axes(placed), by_mesh_axes(out_specs)
+        return jax.shard_map(program, mesh=on, in_specs=ins, out_specs=outs, check_vma=False)(*args)
+
+    return run

time: 4660 us -> 858 us (0.18)
  waiting for transfers between devices: 3760 us -> 383 us
  blocking collectives: 294 us -> 0 us
  local copies, waits for them, and re-layouts: 287 us -> 55.8 us
  starting transfers between devices: 4.24 us -> 147 us
  matrix products: 214 us -> 77.3 us
  Pallas kernels: 0 us -> 94.4 us
    reduce_scatter x11 -> x0, waiting for transfers between devices: 1440 us -> none  [the longest x1 328 us: per_device(): lax.psum_scatter(grad_gate, 'seq', scatter_dimension=0, tiled=True)]
    unnamed x28 -> x0, waiting for transfers between devices: 1340 us -> none
    all_gather x15 -> x0, waiting for transfers between devices: 985 us -> none  [the longest x2 276 us: fetch_feedforward(): lax.all_gather(w_down, 'seq', axis=1, tiled=True)]
    ppermute x2 -> x144, waiting for transfers between devices: 0.01 us -> 383 us  [the longest x41 215 us: shifted(): return lax.ppermute(value, axes, pairs)]
    all_gather x6 -> x0, blocking collectives: 201 us -> none  [the longest x4 124 us: entering(): pieces = jax.tree.map(lambda part: lax.all_gather(part, axis), value)]
    ppermute x2 -> x144, starting transfers between devices: 3.17 us -> 147 us  [the longest x95 78.7 us: swap(): return lax.ppermute(value, axis, [(0, 1), (1, 0)])]
    dot_general x24 -> x22, matrix products: 214 us -> 77.3 us  [dot(): lax.dot_general(left, right, (dims, ((), ())), preferred_element_type=F32)]
    slice x98 -> x32, local copies, waits for them, and re-layouts: 128 us -> 15.2 us  [the longest x8 9.14 us: core_give(): return parts[2:].astype(BF)]
  transfers between devices with their start and end apart: 29 -> 144, of which waited for: 22 -> 50; matrix products, arithmetic and copies ran while one was open for 11% -> 22% of each run, Pallas kernels for 0% -> 9%
where the time goes in v2:
time: 858 us; the launch traced here: 849 us
  waiting for transfers between devices  383 us (45%)
  starting transfers between devices  147 us (17%)
  Pallas kernels  94.4 us (11%)
  other arithmetic  86.9 us (10%)
  matrix products  77.3 us (9%)
  local copies, waits for them, and re-layouts  55.8 us (7%)
    ppermute x41, waiting for transfers between devices, shifted(): return lax.ppermute(value, axes, pairs)  215 us
    ppermute x95, waiting for transfers between devices, swap(): return lax.ppermute(value, axis, [(0, 1), (1, 0)])  143 us
    ppermute x95, starting transfers between devices, swap(): return lax.ppermute(value, axis, [(0, 1), (1, 0)])  78.7 us
    dot_general x22, matrix products, dot(): lax.dot_general(left, right, (dims, ((), ())), preferred_element_type=F32)  77.3 us
    ppermute x41, starting transfers between devices, shifted(): return lax.ppermute(value, axes, pairs)  53.9 us
    unnamed x305, local copies, waits for them, and re-layouts  23.6 us
    pallas_call x1, Pallas kernels, ff_grads_call(): pl.pallas_call(functools.partial(ff_kernel, steps, fold), grid_spec=pltpu...  23.4 us
    pallas_call x3, Pallas kernels, place(): pl.pallas_call(functools.partial(place_kernel, plan, len(pieces)), in_spe...  20.3 us
  transfers between devices with their start and end apart: 144, of which 50 were waited for; matrix products, arithmetic and copies ran while one was open for 22% of the time, Pallas kernels for 9%

profile of v2, /device:TPU:0, one launch (start us, length us, event | category | flops | bytes accessed | tf_op | source)
XLA Modules:
  0.0 848.5 jit_solution(3911672604236370317)
XLA Ops:
  22.9 6.8 collective-permute-done.3.refs_4_
  45.4 4.4 collective-permute-start.11
  51.4 14.0 %collective-permute-done.11.refs_12_ = bf16[80,3328]{1,0:T(8,128)(2,1)S(1)} collective-permute-done((bf16[80,3328]{1,0:T(8,128)(2,1)S(1)}, bf16[80,3328]{1,0:T(8,128)(2,1)S(1)}, u32[]{:S(2)}, u32[]{:S(2)}) %collective-permute-start.11) | collective-permute-done | bytes 532512 | tf_op jit(solution)/shard_map/ppermute | solution.py:26
  70.4 9.5 %collective-permute-done.13.refs_14_ = bf16[80,3328]{1,0:T(8,128)(2,1)S(1)} collective-permute-done((bf16[80,3328]{1,0:T(8,128)(2,1)S(1)}, bf16[80,3328]{1,0:T(8,128)(2,1)S(1)}, u32[]{:S(2)}, u32[]{:S(2)}) %collective-permute-start.13) | collective-permute-done | bytes 532512 | tf_op jit(solution)/shard_map/ppermute | solution.py:21
  85.2 5.7 place_w_x.1
  94.4 5.2 convolution_convert_fusion
  99.7 4.7 collective-permute-done.22.refs_4_
  108.4 16.6 %collective-permute-done.23.halo_ref = bf16[2,16,1280]{2,1,0:T(8,128)(2,1)S(1)} collective-permute-done((bf16[2,16,1280]{2,1,0:T(8,128)(2,1)S(1)}, bf16[2,16,1280]{2,1,0:T(8,128)(2,1)S(1)}, u32[]{:S(2)}, u32[]{:S(2)}) %collective-permute-start.23) | collective-permute-done | bytes 81952 | tf_op jit(solution)/shard_map/ppermute | solution.py:26
  126.9 8.1 recurrence_forward.1
  150.0 6.2 collective-permute-done.28
  161.1 16.3 %collective-permute-done.34.refs_14_ = bf16[80,5120]{1,0:T(8,128)(2,1)S(1)} collective-permute-done((bf16[80,5120]{1,0:T(8,128)(2,1)S(1)}, bf16[80,5120]{1,0:T(8,128)(2,1)S(1)}, u32[]{:S(2)}, u32[]{:S(2)}) %collective-permute-start.34) | collective-permute-done | bytes 819232 | tf_op jit(solution)/shard_map/ppermute | solution.py:21
  177.4 5.4 collective-permute-done.35.refs_2_
  187.2 4.9 collective-permute-start.45
  193.1 9.5 %place_w_y_w_out.1 = (bf16[2560,1280]{1,0:T(8,128)(2,1)}, bf16[1280,2560]{1,0:T(8,128)(2,1)}) custom-call(bf16[80,5120]{1,0:T(8,128)(2,1)S(1)} %pad_maximum_fusion.15.refs_0_, bf16[80,5120]{1,0:T(8,128)(2,1)S(1)} %collective-permute-done.33.refs_1_, bf16[80,5120]{1,0:T(8,128)(2,1)} %collective-permute-done.25.refs_2_, ...), custom_call_target="tpu_custom_call" | custom-call | tf_op jit(solution)/shard_map/place_w_y_w_out/pallas_call | solution.py:263
  202.6 6.6 fusion.21
  217.6 34.8 %collective-permute-done.47 = bf16[320,768]{1,0:T(8,128)(2,1)S(1)} collective-permute-done((bf16[320,768]{1,0:T(8,128)(2,1)S(1)}, bf16[320,768]{1,0:T(8,128)(2,1)S(1)}, u32[]{:S(2)}, u32[]{:S(2)}) %collective-permute-start.47) | collective-permute-done | bytes 491552 | tf_op jit(solution)/shard_map/ppermute | solution.py:26
  260.8 28.9 %collective-permute-done.50 = bf16[128,2560]{1,0:T(8,128)(2,1)} collective-permute-done((bf16[128,2560]{1,0:T(8,128)(2,1)S(1)}, bf16[128,2560]{1,0:T(8,128)(2,1)}, u32[]{:S(2)}, u32[]{:S(2)}) %collective-permute-start.50) | collective-permute-done | bytes 655392 | tf_op jit(solution)/shard_map/ppermute | solution.py:26
  297.1 15.8 %collective-permute-done.55 = bf16[128,2560]{1,0:T(8,128)(2,1)} collective-permute-done((bf16[128,2560]{1,0:T(8,128)(2,1)}, bf16[128,2560]{1,0:T(8,128)(2,1)}, u32[]{:S(2)}, u32[]{:S(2)}) %collective-permute-start.55) | collective-permute-done | bytes 655392 | tf_op jit(solution)/shard_map/ppermute | solution.py:26
  312.9 11.4 %collective-permute-done.57 = bf16[128,2560]{1,0:T(8,128)(2,1)} collective-permute-done((bf16[128,2560]{1,0:T(8,128)(2,1)}, bf16[128,2560]{1,0:T(8,128)(2,1)}, u32[]{:S(2)}, u32[]{:S(2)}) %collective-permute-start.57) | collective-permute-done | bytes 655392 | tf_op jit(solution)/shard_map/ppermute | solution.py:26
  327.4 5.1 place_feed_forward.1
  351.5 9.0 %collective-permute-done.65 = bf16[128,2560]{1,0:T(8,128)(2,1)S(1)} collective-permute-done((bf16[128,2560]{1,0:T(8,128)(2,1)}, bf16[128,2560]{1,0:T(8,128)(2,1)S(1)}, u32[]{:S(2)}, u32[]{:S(2)}) %collective-permute-start.65) | collective-permute-done | bytes 655392 | tf_op jit(solution)/shard_map/ppermute | solution.py:26
  360.5 4.6 collective-permute-done.66
  381.9 6.9 fusion.127
  388.9 10.8 %collective-permute-done.72 = bf16[128,2560]{1,0:T(8,128)(2,1)} collective-permute-done((bf16[128,2560]{1,0:T(8,128)(2,1)S(1)}, bf16[128,2560]{1,0:T(8,128)(2,1)}, u32[]{:S(2)}, u32[]{:S(2)}) %collective-permute-start.72) | collective-permute-done | bytes 655392 | tf_op jit(solution)/shard_map/ppermute | solution.py:21
  411.0 4.8 fusion.138
  420.2 8.2 fusion.126
  428.4 11.5 %collective-permute-done.82 = bf16[128,2560]{1,0:T(8,128)(2,1)} collective-permute-done((bf16[128,2560]{1,0:T(8,128)(2,1)S(1)}, bf16[128,2560]{1,0:T(8,128)(2,1)}, u32[]{:S(2)}, u32[]{:S(2)}) %collective-permute-start.82) | collective-permute-done | bytes 655392 | tf_op jit(solution)/shard_map/ppermute | solution.py:21
  452.2 5.7 fusion.139
  461.1 5.0 fusion.125
  483.6 23.4 %feed_forward_grads.1 = (f32[4,320,1536]{2,1,0:T(8,128)}, bf16[4,320,1536]{2,1,0:T(8,128)(2,1)}) custom-call(s32[3]{0:T(128)S(1)} %pad_add_fusion.where_ref, bf16[512,2560]{1,0:T(8,128)(2,1)} %copy-done.55, bf16[512,2560]{1,0:T(8,128)(2,1)} %copy-done.54, bf16[512,2560]{1,0:T(8,128)(2,1)} %copy-done.59, bf16[512,2560]{1,0:T(8,128)(2,1)} %copy-done.57, ...), custom_call_target="tpu_custom_call" | custom-call | tf_op jit(solution)/shard_map/feed_forward_grads/pallas_call | solution.py:380
  525.0 19.5 %collective-permute-done.98 = bf16[320,1536]{1,0:T(8,128)(2,1)S(1)} collective-permute-done((bf16[320,1536]{1,0:T(8,128)(2,1)S(1)}, bf16[320,1536]{1,0:T(8,128)(2,1)S(1)}, u32[]{:S(2)}, u32[]{:S(2)}) %collective-permute-start.98) | collective-permute-done | bytes 983072 | tf_op jit(solution)/shard_map/ppermute | solution.py:21
  554.8 8.1 collective-permute-done.100
  575.1 7.1 recurrence_back_scan.1
  584.5 5.8 grad_w_y_w_out.2
  592.0 5.8 collective-permute-done.105
  618.9 13.9 %recurrence_backward.1 = (f32[2,128,1280]{2,1,0:T(8,128)S(1)}, f32[2,1280,256]{2,1,0:T(8,128)}, f32[8,1280]{1,0:T(8,128)S(1)}) custom-call(bf16[2,128,1280]{2,1,0:T(8,128)(2,1)S(1)} %bitcast.317, bf16[2,16,1280]{2,1,0:T(8,128)(2,1)S(1)} %copy-done.33, f32[8,1280]{1,0:T(8,128)S(1)} %copy-done.31, bf16[2,1280,256]{2,1,0:T(8,128)(2,1)S(1)} %copy-done.6, ...), custom_call_target="tpu_custom_call" | custom-call | tf_op jit(solution)/shard_map/recurrence_backward/pallas_call | solution.py:239
  634.4 5.9 grad_w_y_w_out.3
  642.5 6.4 grad_w_x.1
  662.7 8.1 collective-permute-done.116
  670.8 6.4 collective-permute-done.117
  688.5 4.9 fusion.143
  696.2 23.7 %collective-permute-done.123 = bf16[2,2,80,1536]{3,2,1,0:T(8,128)(2,1)S(1)} collective-permute-done((bf16[2,2,80,1536]{3,2,1,0:T(8,128)(2,1)}, bf16[2,2,80,1536]{3,2,1,0:T(8,128)(2,1)S(1)}, u32[]{:S(2)}, u32[]{:S(2)}) %collective-permute-start.123) | collective-permute-done | bytes 983072 | tf_op jit(solution)/shard_map/ppermute | solution.py:21
  721.5 7.2 collective-permute-done.122
  746.0 17.7 %collective-permute-done.127 = bf16[2,2,80,1536]{3,2,1,0:T(8,128)(2,1)} collective-permute-done((bf16[2,2,80,1536]{3,2,1,0:T(8,128)(2,1)}, bf16[2,2,80,1536]{3,2,1,0:T(8,128)(2,1)}, u32[]{:S(2)}, u32[]{:S(2)}) %collective-permute-start.127) | collective-permute-done | bytes 983072 | tf_op jit(solution)/shard_map/ppermute | solution.py:21
  765.0 8.4 collective-permute-done.126
  773.5 8.3 collective-permute-done.128
  794.9 19.0 %collective-permute-done.133 = bf16[80,1280]{1,0:T(8,128)(2,1)S(1)} collective-permute-done((bf16[80,1280]{1,0:T(8,128)(2,1)S(1)}, bf16[80,1280]{1,0:T(8,128)(2,1)S(1)}, u32[]{:S(2)}, u32[]{:S(2)}) %collective-permute-start.133) | collective-permute-done | bytes 204832 | tf_op jit(solution)/shard_map/ppermute | solution.py:844
  825.6 8.6 %collective-permute-done.137 = f32[12,1280]{1,0:T(8,128)S(1)} collective-permute-done((f32[12,1280]{1,0:T(8,128)S(1)}, f32[12,1280]{1,0:T(8,128)S(1)}, u32[]{:S(2)}, u32[]{:S(2)}) %collective-permute-start.137) | collective-permute-done | bytes 61472 | tf_op jit(solution)/shard_map/ppermute | solution.py:26
  (753 shorter events, 349.8 us)
Async XLA Ops:
  40.0 25.9 %collective-permute-start.14 = (bf16[80,3328]{1,0:T(8,128)(2,1)S(1)}, bf16[80,3328]{1,0:T(8,128)(2,1)S(1)}, u32[]{:S(2)}, u32[]{:S(2)}) collective-permute-start(bf16[80,3328]{1,0:T(8,128)(2,1)S(1)} %constant_dynamic-update-slice_fusion.refs_0_), channel_id=1, source_target_pairs={{0,1},{1,0},{2,3},{3,2},{4,5},{5,4},{6,7},{7,6},{8,9},{9,8},{10,11... | collective-permute-start | bytes 1597448 | tf_op jit(solution)/shard_map/ppermute | solution.py:21
  40.1 27.3 %collective-permute-start.15 = (bf16[80,3328]{1,0:T(8,128)(2,1)S(1)}, bf16[80,3328]{1,0:T(8,128)(2,1)S(1)}, u32[]{:S(2)}, u32[]{:S(2)}) collective-permute-start(bf16[80,3328]{1,0:T(8,128)(2,1)S(1)} %collective-permute-done.3.refs_4_), channel_id=1, source_target_pairs={{0,1},{1,0},{2,3},{3,2},{4,5},{5,4},{6,7},{7,6},{8,9},{9,8},{10,11... | collective-permute-start | bytes 1597448 | tf_op jit(solution)/shard_map/ppermute | solution.py:21
  83.0 42.0 %collective-permute-start.25 = (bf16[80,5120]{1,0:T(8,128)(2,1)S(1)}, bf16[80,5120]{1,0:T(8,128)(2,1)}, u32[]{:S(2)}, u32[]{:S(2)}) collective-permute-start(bf16[80,5120]{1,0:T(8,128)(2,1)S(1)} %pad_maximum_fusion.15.refs_0_), channel_id=1, source_target_pairs={{0,4},{4,0},{1,5},{5,1},{2,6},{6,2},{3,7},{7,3},{8,12},{12,8},{9,1... | collective-permute-start | bytes 2457608 | tf_op jit(solution)/shard_map/ppermute | solution.py:21
  211.3 41.2 %collective-permute-start.48 = (bf16[320,1536]{1,0:T(8,128)(2,1)S(1)}, bf16[320,1536]{1,0:T(8,128)(2,1)S(1)}, u32[]{:S(2)}, u32[]{:S(2)}) collective-permute-start(bf16[320,1536]{1,0:T(8,128)(2,1)S(1)} %collective-permute-done.35.refs_2_), channel_id=1, source_target_pairs={{0,4},{4,0},{1,5},{5,1},{2,6},{6,2},{3,7},{7,3},{8,12},{12,8},{9,1... | collective-permute-start | bytes 2949128 | tf_op jit(solution)/shard_map/ppermute | solution.py:21
  212.1 40.4 %collective-permute-start.46 = (bf16[128,2560]{1,0:T(8,128)(2,1)S(1)}, bf16[128,2560]{1,0:T(8,128)(2,1)S(1)}, u32[]{:S(2)}, u32[]{:S(2)}) collective-permute-start(bf16[128,2560]{1,0:T(8,128)(2,1)S(1)} %slice.916), channel_id=1, source_target_pairs={{0,2},{2,0},{1,3},{3,1},{4,6},{6,4},{5,7},{7,5},{8,10},{10,8},{9,1... | collective-permute-start | bytes 1966088 | tf_op jit(solution)/shard_map/ppermute | solution.py:21
  215.0 37.5 %collective-permute-start.49 = (bf16[128,2560]{1,0:T(8,128)(2,1)S(1)}, bf16[128,2560]{1,0:T(8,128)(2,1)}, u32[]{:S(2)}, u32[]{:S(2)}) collective-permute-start(bf16[128,2560]{1,0:T(8,128)(2,1)S(1)} %bitcast.362), channel_id=1, source_target_pairs={{0,8},{8,16},{16,24},{24,0},{1,9},{9,17},{17,25},{25,1},{2,10},{10... | collective-permute-start | bytes 1966088 | tf_op jit(solution)/shard_map/ppermute | solution.py:26
  215.7 36.7 %collective-permute-start.47 = (bf16[320,768]{1,0:T(8,128)(2,1)S(1)}, bf16[320,768]{1,0:T(8,128)(2,1)S(1)}, u32[]{:S(2)}, u32[]{:S(2)}) collective-permute-start(bf16[320,768]{1,0:T(8,128)(2,1)S(1)} %slice.456), channel_id=1, source_target_pairs={{0,16},{8,24},{16,0},{24,8},{1,17},{9,25},{17,1},{25,9},{2,18},{10... | collective-permute-start | bytes 1474568 | tf_op jit(solution)/shard_map/ppermute | solution.py:26
  253.5 37.1 %collective-permute-start.53 = (bf16[320,1536]{1,0:T(8,128)(2,1)S(1)}, bf16[320,1536]{1,0:T(8,128)(2,1)}, u32[]{:S(2)}, u32[]{:S(2)}) collective-permute-start(bf16[320,1536]{1,0:T(8,128)(2,1)S(1)} %copy-done.88), channel_id=1, source_target_pairs={{0,24},{8,0},{16,8},{24,16},{1,25},{9,1},{17,9},{25,17},{2,26},{10... | collective-permute-start | bytes 2949128 | tf_op jit(solution)/shard_map/ppermute | solution.py:26
  256.7 34.0 %collective-permute-start.54 = (bf16[320,1536]{1,0:T(8,128)(2,1)S(1)}, bf16[320,1536]{1,0:T(8,128)(2,1)S(1)}, u32[]{:S(2)}, u32[]{:S(2)}) collective-permute-start(bf16[320,1536]{1,0:T(8,128)(2,1)S(1)} %pad_maximum_fusion.10), channel_id=1, source_target_pairs={{0,4},{4,0},{1,5},{5,1},{2,6},{6,2},{3,7},{7,3},{8,12},{12,8},{9,1... | collective-permute-start | bytes 2949128 | tf_op jit(solution)/shard_map/ppermute | solution.py:21
  258.6 31.1 %collective-permute-start.50 = (bf16[128,2560]{1,0:T(8,128)(2,1)S(1)}, bf16[128,2560]{1,0:T(8,128)(2,1)}, u32[]{:S(2)}, u32[]{:S(2)}) collective-permute-start(bf16[128,2560]{1,0:T(8,128)(2,1)S(1)} %multiply_convert_fusion.2), channel_id=1, source_target_pairs={{0,8},{8,16},{16,24},{24,0},{1,9},{9,17},{17,25},{25,1},{2,10},{10... | collective-permute-start | bytes 1966088 | tf_op jit(solution)/shard_map/ppermute | solution.py:26
  258.7 31.0 %collective-permute-start.51 = (bf16[128,2560]{1,0:T(8,128)(2,1)S(1)}, bf16[128,2560]{1,0:T(8,128)(2,1)S(1)}, u32[]{:S(2)}, u32[]{:S(2)}) collective-permute-start(bf16[128,2560]{1,0:T(8,128)(2,1)S(1)} %multiply_convert_fusion.2), channel_id=1, source_target_pairs={{0,2},{2,0},{1,3},{3,1},{4,6},{6,4},{5,7},{7,5},{8,10},{10,8},{9,1... | collective-permute-start | bytes 1966088 | tf_op jit(solution)/shard_map/ppermute | solution.py:21
  259.0 30.7 %collective-permute-start.52 = (bf16[128,2560]{1,0:T(8,128)(2,1)}, bf16[128,2560]{1,0:T(8,128)(2,1)S(1)}, u32[]{:S(2)}, u32[]{:S(2)}) collective-permute-start(bf16[128,2560]{1,0:T(8,128)(2,1)} %collective-permute-done.49), channel_id=1, source_target_pairs={{0,2},{2,0},{1,3},{3,1},{4,6},{6,4},{5,7},{7,5},{8,10},{10,8},{9,1... | collective-permute-start | bytes 1966088 | tf_op jit(solution)/shard_map/ppermute | solution.py:21
  291.7 32.6 %collective-permute-start.58 = (bf16[320,1536]{1,0:T(8,128)(2,1)}, bf16[320,1536]{1,0:T(8,128)(2,1)}, u32[]{:S(2)}, u32[]{:S(2)}) collective-permute-start(bf16[320,1536]{1,0:T(8,128)(2,1)} %collective-permute-done.53.refs_6_), channel_id=1, source_target_pairs={{0,4},{4,0},{1,5},{5,1},{2,6},{6,2},{3,7},{7,3},{8,12},{12,8},{9,1... | collective-permute-start | bytes 2949128 | tf_op jit(solution)/shard_map/ppermute | solution.py:21
  294.2 30.1 %collective-permute-start.57 = (bf16[128,2560]{1,0:T(8,128)(2,1)}, bf16[128,2560]{1,0:T(8,128)(2,1)}, u32[]{:S(2)}, u32[]{:S(2)}) collective-permute-start(bf16[128,2560]{1,0:T(8,128)(2,1)} %collective-permute-done.49), channel_id=1, source_target_pairs={{0,8},{8,16},{16,24},{24,0},{1,9},{9,17},{17,25},{25,1},{2,10},{10... | collective-permute-start | bytes 1966088 | tf_op jit(solution)/shard_map/ppermute | solution.py:26
  295.6 45.1 %collective-permute-start.62 = (bf16[128,2560]{1,0:T(8,128)(2,1)}, bf16[128,2560]{1,0:T(8,128)(2,1)}, u32[]{:S(2)}, u32[]{:S(2)}) collective-permute-start(bf16[128,2560]{1,0:T(8,128)(2,1)} %copy-done.101), channel_id=1, source_target_pairs={{0,1},{1,0},{2,3},{3,2},{4,5},{5,4},{6,7},{7,6},{8,9},{9,8},{10,11... | collective-permute-start | bytes 1966088 | tf_op jit(solution)/shard_map/ppermute | solution.py:21
  334.4 26.1 %collective-permute-start.65 = (bf16[128,2560]{1,0:T(8,128)(2,1)}, bf16[128,2560]{1,0:T(8,128)(2,1)S(1)}, u32[]{:S(2)}, u32[]{:S(2)}) collective-permute-start(bf16[128,2560]{1,0:T(8,128)(2,1)} %collective-permute-done.57), channel_id=1, source_target_pairs={{0,8},{8,16},{16,24},{24,0},{1,9},{9,17},{17,25},{25,1},{2,10},{10... | collective-permute-start | bytes 1966088 | tf_op jit(solution)/shard_map/ppermute | solution.py:26
  336.1 29.0 %collective-permute-start.66 = (bf16[128,2560]{1,0:T(8,128)(2,1)}, bf16[128,2560]{1,0:T(8,128)(2,1)S(1)}, u32[]{:S(2)}, u32[]{:S(2)}) collective-permute-start(bf16[128,2560]{1,0:T(8,128)(2,1)} %collective-permute-done.57), channel_id=1, source_target_pairs={{0,2},{2,0},{1,3},{3,1},{4,6},{6,4},{5,7},{7,5},{8,10},{10,8},{9,1... | collective-permute-start | bytes 1966088 | tf_op jit(solution)/shard_map/ppermute | solution.py:21
  371.7 28.0 %collective-permute-start.72 = (bf16[128,2560]{1,0:T(8,128)(2,1)S(1)}, bf16[128,2560]{1,0:T(8,128)(2,1)}, u32[]{:S(2)}, u32[]{:S(2)}) collective-permute-start(bf16[128,2560]{1,0:T(8,128)(2,1)S(1)} %collective-permute-done.65), channel_id=1, source_target_pairs={{0,2},{2,0},{1,3},{3,1},{4,6},{6,4},{5,7},{7,5},{8,10},{10,8},{9,1... | collective-permute-start | bytes 1966088 | tf_op jit(solution)/shard_map/ppermute | solution.py:21
  373.3 26.4 %collective-permute-start.73 = (bf16[2,128,2560]{2,1,0:T(8,128)(2,1)}, bf16[2,128,2560]{2,1,0:T(8,128)(2,1)S(1)}, u32[]{:S(2)}, u32[]{:S(2)}) collective-permute-start(bf16[2,128,2560]{2,1,0:T(8,128)(2,1)} %slice.914), channel_id=1, source_target_pairs={{0,1},{1,0},{2,3},{3,2},{4,5},{5,4},{6,7},{7,6},{8,9},{9,8},{10,11... | collective-permute-start | bytes 3932168 | tf_op jit(solution)/shard_map/ppermute | solution.py:21
  373.4 26.3 %collective-permute-start.74 = (bf16[2,128,2560]{2,1,0:T(8,128)(2,1)}, bf16[2,128,2560]{2,1,0:T(8,128)(2,1)S(1)}, u32[]{:S(2)}, u32[]{:S(2)}) collective-permute-start(bf16[2,128,2560]{2,1,0:T(8,128)(2,1)} %slice.913), channel_id=1, source_target_pairs={{0,1},{1,0},{2,3},{3,2},{4,5},{5,4},{6,7},{7,6},{8,9},{9,8},{10,11... | collective-permute-start | bytes 3932168 | tf_op jit(solution)/shard_map/ppermute | solution.py:21
  403.8 36.2 %collective-permute-start.79 = (bf16[2,128,2560]{2,1,0:T(8,128)(2,1)}, bf16[2,128,2560]{2,1,0:T(8,128)(2,1)}, u32[]{:S(2)}, u32[]{:S(2)}) collective-permute-start(bf16[2,128,2560]{2,1,0:T(8,128)(2,1)} %slice.912), channel_id=1, source_target_pairs={{0,1},{1,0},{2,3},{3,2},{4,5},{5,4},{6,7},{7,6},{8,9},{9,8},{10,11... | collective-permute-start | bytes 3932168 | tf_op jit(solution)/shard_map/ppermute | solution.py:21
  409.1 30.8 %collective-permute-start.81 = (bf16[2,128,2560]{2,1,0:T(8,128)(2,1)}, bf16[2,128,2560]{2,1,0:T(8,128)(2,1)S(1)}, u32[]{:S(2)}, u32[]{:S(2)}) collective-permute-start(bf16[2,128,2560]{2,1,0:T(8,128)(2,1)} %slice.911), channel_id=1, source_target_pairs={{0,1},{1,0},{2,3},{3,2},{4,5},{5,4},{6,7},{7,6},{8,9},{9,8},{10,11... | collective-permute-start | bytes 3932168 | tf_op jit(solution)/shard_map/ppermute | solution.py:21
  409.4 30.5 %collective-permute-start.82 = (bf16[128,2560]{1,0:T(8,128)(2,1)S(1)}, bf16[128,2560]{1,0:T(8,128)(2,1)}, u32[]{:S(2)}, u32[]{:S(2)}) collective-permute-start(bf16[128,2560]{1,0:T(8,128)(2,1)S(1)} %fusion.90), channel_id=1, source_target_pairs={{0,2},{2,0},{1,3},{3,1},{4,6},{6,4},{5,7},{7,5},{8,10},{10,8},{9,1... | collective-permute-start | bytes 1966088 | tf_op jit(solution)/shard_map/ppermute | solution.py:21
  444.1 25.6 %collective-permute-start.87 = (bf16[2,128,2560]{2,1,0:T(8,128)(2,1)}, bf16[2,128,2560]{2,1,0:T(8,128)(2,1)}, u32[]{:S(2)}, u32[]{:S(2)}) collective-permute-start(bf16[2,128,2560]{2,1,0:T(8,128)(2,1)} %slice.910), channel_id=1, source_target_pairs={{0,1},{1,0},{2,3},{3,2},{4,5},{5,4},{6,7},{7,6},{8,9},{9,8},{10,11... | collective-permute-start | bytes 3932168 | tf_op jit(solution)/shard_map/ppermute | solution.py:21
  470.9 42.0 %collective-permute-start.90 = (bf16[2,128,2560]{2,1,0:T(8,128)(2,1)}, bf16[2,128,2560]{2,1,0:T(8,128)(2,1)}, u32[]{:S(2)}, u32[]{:S(2)}) collective-permute-start(bf16[2,128,2560]{2,1,0:T(8,128)(2,1)} %slice.909), channel_id=1, source_target_pairs={{0,1},{1,0},{2,3},{3,2},{4,5},{5,4},{6,7},{7,6},{8,9},{9,8},{10,11... | collective-permute-start | bytes 3932168 | tf_op jit(solution)/shard_map/ppermute | solution.py:21
  473.3 37.4 %collective-permute-start.91 = (bf16[128,2560]{1,0:T(8,128)(2,1)}, bf16[128,2560]{1,0:T(8,128)(2,1)}, u32[]{:S(2)}, u32[]{:S(2)}) collective-permute-start(bf16[128,2560]{1,0:T(8,128)(2,1)} %fusion.92), channel_id=1, source_target_pairs={{0,2},{2,0},{1,3},{3,1},{4,6},{6,4},{5,7},{7,5},{8,10},{10,8},{9,1... | collective-permute-start | bytes 1966088 | tf_op jit(solution)/shard_map/ppermute | solution.py:21
  477.2 34.1 %collective-permute-start.92 = (bf16[128,2560]{1,0:T(8,128)(2,1)}, bf16[128,2560]{1,0:T(8,128)(2,1)}, u32[]{:S(2)}, u32[]{:S(2)}) collective-permute-start(bf16[128,2560]{1,0:T(8,128)(2,1)} %fusion.45), channel_id=1, source_target_pairs={{0,8},{8,16},{16,24},{24,0},{1,9},{9,17},{17,25},{25,1},{2,10},{10... | collective-permute-start | bytes 1966088 | tf_op jit(solution)/shard_map/ppermute | solution.py:26
  478.2 34.6 %collective-permute-start.93 = (bf16[128,2560]{1,0:T(8,128)(2,1)}, bf16[128,2560]{1,0:T(8,128)(2,1)S(1)}, u32[]{:S(2)}, u32[]{:S(2)}) collective-permute-start(bf16[128,2560]{1,0:T(8,128)(2,1)} %fusion.93), channel_id=1, source_target_pairs={{0,2},{2,0},{1,3},{3,1},{4,6},{6,4},{5,7},{7,5},{8,10},{10,8},{9,1... | collective-permute-start | bytes 1966088 | tf_op jit(solution)/shard_map/ppermute | solution.py:21
  480.1 32.7 %collective-permute-start.94 = (bf16[128,2560]{1,0:T(8,128)(2,1)S(1)}, bf16[128,2560]{1,0:T(8,128)(2,1)S(1)}, u32[]{:S(2)}, u32[]{:S(2)}) collective-permute-start(bf16[128,2560]{1,0:T(8,128)(2,1)S(1)} %fusion.43), channel_id=1, source_target_pairs={{0,8},{8,16},{16,24},{24,0},{1,9},{9,17},{17,25},{25,1},{2,10},{10... | collective-permute-start | bytes 1966088 | tf_op jit(solution)/shard_map/ppermute | solution.py:26
  511.3 33.2 %collective-permute-start.98 = (bf16[320,1536]{1,0:T(8,128)(2,1)S(1)}, bf16[320,1536]{1,0:T(8,128)(2,1)S(1)}, u32[]{:S(2)}, u32[]{:S(2)}) collective-permute-start(bf16[320,1536]{1,0:T(8,128)(2,1)S(1)} %get-tuple-element.767), channel_id=1, source_target_pairs={{0,4},{4,0},{1,5},{5,1},{2,6},{6,2},{3,7},{7,3},{8,12},{12,8},{9,1... | collective-permute-start | bytes 2949128 | tf_op jit(solution)/shard_map/ppermute | solution.py:21
  515.5 29.0 %collective-permute-start.95 = (bf16[128,2560]{1,0:T(8,128)(2,1)S(1)}, bf16[128,2560]{1,0:T(8,128)(2,1)S(1)}, u32[]{:S(2)}, u32[]{:S(2)}) collective-permute-start(bf16[128,2560]{1,0:T(8,128)(2,1)S(1)} %fusion.41), channel_id=1, source_target_pairs={{0,8},{8,16},{16,24},{24,0},{1,9},{9,17},{17,25},{25,1},{2,10},{10... | collective-permute-start | bytes 1966088 | tf_op jit(solution)/shard_map/ppermute | solution.py:26
  551.9 39.1 %collective-permute-start.106 = (bf16[320,1536]{1,0:T(8,128)(2,1)}, bf16[320,1536]{1,0:T(8,128)(2,1)S(1)}, u32[]{:S(2)}, u32[]{:S(2)}) collective-permute-start(bf16[320,1536]{1,0:T(8,128)(2,1)} %fusion.6), channel_id=1, source_target_pairs={{0,24},{8,0},{16,8},{24,16},{1,25},{9,1},{17,9},{25,17},{2,26},{10... | collective-permute-start | bytes 2949128 | tf_op jit(solution)/shard_map/ppermute | solution.py:26
  566.1 31.6 %collective-permute-start.103 = (bf16[128,2560]{1,0:T(8,128)(2,1)}, bf16[128,2560]{1,0:T(8,128)(2,1)}, u32[]{:S(2)}, u32[]{:S(2)}) collective-permute-start(bf16[128,2560]{1,0:T(8,128)(2,1)} %fusion.95), channel_id=1, source_target_pairs={{0,2},{2,0},{1,3},{3,1},{4,6},{6,4},{5,7},{7,5},{8,10},{10,8},{9,1... | collective-permute-start | bytes 1966088 | tf_op jit(solution)/shard_map/ppermute | solution.py:21
  568.5 29.3 %collective-permute-start.104 = (bf16[128,2560]{1,0:T(8,128)(2,1)}, bf16[128,2560]{1,0:T(8,128)(2,1)}, u32[]{:S(2)}, u32[]{:S(2)}) collective-permute-start(bf16[128,2560]{1,0:T(8,128)(2,1)} %fusion.96), channel_id=1, source_target_pairs={{0,2},{2,0},{1,3},{3,1},{4,6},{6,4},{5,7},{7,5},{8,10},{10,8},{9,1... | collective-permute-start | bytes 1966088 | tf_op jit(solution)/shard_map/ppermute | solution.py:21
  569.3 28.4 %collective-permute-start.105 = (bf16[320,768]{1,0:T(8,128)(2,1)S(1)}, bf16[320,768]{1,0:T(8,128)(2,1)}, u32[]{:S(2)}, u32[]{:S(2)}) collective-permute-start(bf16[320,768]{1,0:T(8,128)(2,1)S(1)} %fusion.78), channel_id=1, source_target_pairs={{0,16},{8,24},{16,0},{24,8},{1,17},{9,25},{17,1},{25,9},{2,18},{10... | collective-permute-start | bytes 1474568 | tf_op jit(solution)/shard_map/ppermute | solution.py:26
  648.9 28.4 %collective-permute-start.118 = (bf16[4,4,80,1536]{3,2,1,0:T(8,128)(2,1)}, bf16[4,4,80,1536]{3,2,1,0:T(8,128)(2,1)}, u32[]{:S(2)}, u32[]{:S(2)}) collective-permute-start(bf16[4,4,80,1536]{3,2,1,0:T(8,128)(2,1)} %get-tuple-element.682), channel_id=1, source_target_pairs={{0,1},{1,0},{2,3},{3,2},{4,5},{5,4},{6,7},{7,6},{8,9},{9,8},{10,11... | collective-permute-start | bytes 11796488 | tf_op jit(solution)/shard_map/ppermute | solution.py:21
  648.9 28.4 %collective-permute-start.119 = (bf16[2,4,80,2560]{3,2,1,0:T(8,128)(2,1)}, bf16[2,4,80,2560]{3,2,1,0:T(8,128)(2,1)}, u32[]{:S(2)}, u32[]{:S(2)}) collective-permute-start(bf16[2,4,80,2560]{3,2,1,0:T(8,128)(2,1)} %get-tuple-element.683), channel_id=1, source_target_pairs={{0,1},{1,0},{2,3},{3,2},{4,5},{5,4},{6,7},{7,6},{8,9},{9,8},{10,11... | collective-permute-start | bytes 9830408 | tf_op jit(solution)/shard_map/ppermute | solution.py:21
  658.0 73.0 %collective-permute-start.125 = (bf16[320,1536]{1,0:T(8,128)(2,1)}, bf16[320,1536]{1,0:T(8,128)(2,1)S(1)}, u32[]{:S(2)}, u32[]{:S(2)}) collective-permute-start(bf16[320,1536]{1,0:T(8,128)(2,1)} %fusion.5), channel_id=1, source_target_pairs={{0,8},{8,16},{16,24},{24,0},{1,9},{9,17},{17,25},{25,1},{2,10},{10... | collective-permute-start | bytes 2949128 | tf_op jit(solution)/shard_map/ppermute | solution.py:26
  680.5 50.6 %collective-permute-start.121 = (bf16[2,80,2560]{2,1,0:T(8,128)(2,1)}, bf16[2,80,2560]{2,1,0:T(8,128)(2,1)}, u32[]{:S(2)}, u32[]{:S(2)}) collective-permute-start(bf16[2,80,2560]{2,1,0:T(8,128)(2,1)} %get-tuple-element.761), channel_id=1, source_target_pairs={{0,4},{4,0},{1,5},{5,1},{2,6},{6,2},{3,7},{7,3},{8,12},{12,8},{9,1... | collective-permute-start | bytes 2457608 | tf_op jit(solution)/shard_map/ppermute | solution.py:21
  684.4 44.3 %collective-permute-start.122 = (bf16[288,2560]{1,0:T(8,128)(2,1)}, bf16[288,2560]{1,0:T(8,128)(2,1)}, u32[]{:S(2)}, u32[]{:S(2)}) collective-permute-start(bf16[288,2560]{1,0:T(8,128)(2,1)} %pad_maximum_fusion), channel_id=1, source_target_pairs={{0,8},{8,16},{16,24},{24,0},{1,9},{9,17},{17,25},{25,1},{2,10},{10... | collective-permute-start | bytes 4423688 | tf_op jit(solution)/shard_map/ppermute | solution.py:26
  687.2 32.6 %collective-permute-start.123 = (bf16[2,2,80,1536]{3,2,1,0:T(8,128)(2,1)}, bf16[2,2,80,1536]{3,2,1,0:T(8,128)(2,1)S(1)}, u32[]{:S(2)}, u32[]{:S(2)}) collective-permute-start(bf16[2,2,80,1536]{3,2,1,0:T(8,128)(2,1)} %pad_maximum_fusion.12), channel_id=1, source_target_pairs={{0,4},{4,0},{1,5},{5,1},{2,6},{6,2},{3,7},{7,3},{8,12},{12,8},{9,1... | collective-permute-start | bytes 2949128 | tf_op jit(solution)/shard_map/ppermute | solution.py:21
  695.4 35.6 %collective-permute-start.124 = (bf16[128,2560]{1,0:T(8,128)(2,1)S(1)}, bf16[128,2560]{1,0:T(8,128)(2,1)S(1)}, u32[]{:S(2)}, u32[]{:S(2)}) collective-permute-start(bf16[128,2560]{1,0:T(8,128)(2,1)S(1)} %slice.915), channel_id=1, source_target_pairs={{0,2},{2,0},{1,3},{3,1},{4,6},{6,4},{5,7},{7,5},{8,10},{10,8},{9,1... | collective-permute-start | bytes 1966088 | tf_op jit(solution)/shard_map/ppermute | solution.py:21
  719.8 53.6 %collective-permute-start.120 = (bf16[2,80,2560]{2,1,0:T(8,128)(2,1)}, bf16[2,80,2560]{2,1,0:T(8,128)(2,1)}, u32[]{:S(2)}, u32[]{:S(2)}) collective-permute-start(bf16[2,80,2560]{2,1,0:T(8,128)(2,1)} %get-tuple-element.762), channel_id=1, source_target_pairs={{0,4},{4,0},{1,5},{5,1},{2,6},{6,2},{3,7},{7,3},{8,12},{12,8},{9,1... | collective-permute-start | bytes 2457608 | tf_op jit(solution)/shard_map/ppermute | solution.py:21
  736.2 37.2 %collective-permute-start.126 = (bf16[288,2560]{1,0:T(8,128)(2,1)}, bf16[288,2560]{1,0:T(8,128)(2,1)S(1)}, u32[]{:S(2)}, u32[]{:S(2)}) collective-permute-start(bf16[288,2560]{1,0:T(8,128)(2,1)} %pad_maximum_fusion.1), channel_id=1, source_target_pairs={{0,8},{8,16},{16,24},{24,0},{1,9},{9,17},{17,25},{25,1},{2,10},{10... | collective-permute-start | bytes 4423688 | tf_op jit(solution)/shard_map/ppermute | solution.py:26
  743.1 38.7 %collective-permute-start.128 = (bf16[2,80,1536]{2,1,0:T(8,128)(2,1)S(1)}, bf16[2,80,1536]{2,1,0:T(8,128)(2,1)S(1)}, u32[]{:S(2)}, u32[]{:S(2)}) collective-permute-start(bf16[2,80,1536]{2,1,0:T(8,128)(2,1)S(1)} %fusion.84), channel_id=1, source_target_pairs={{0,8},{8,16},{16,24},{24,0},{1,9},{9,17},{17,25},{25,1},{2,10},{10... | collective-permute-start | bytes 1474568 | tf_op jit(solution)/shard_map/ppermute | solution.py:26
  744.3 50.7 %collective-permute-start.134 = (bf16[320,1536]{1,0:T(8,128)(2,1)S(1)}, bf16[320,1536]{1,0:T(8,128)(2,1)S(1)}, u32[]{:S(2)}, u32[]{:S(2)}) collective-permute-start(bf16[320,1536]{1,0:T(8,128)(2,1)S(1)} %copy-done.87), channel_id=1, source_target_pairs={{0,4},{4,0},{1,5},{5,1},{2,6},{6,2},{3,7},{7,3},{8,12},{12,8},{9,1... | collective-permute-start | bytes 2949128 | tf_op jit(solution)/shard_map/ppermute | solution.py:21
  783.5 30.5 %collective-permute-start.130 = (bf16[2,80,1536]{2,1,0:T(8,128)(2,1)S(1)}, bf16[2,80,1536]{2,1,0:T(8,128)(2,1)S(1)}, u32[]{:S(2)}, u32[]{:S(2)}) collective-permute-start(bf16[2,80,1536]{2,1,0:T(8,128)(2,1)S(1)} %fusion.83), channel_id=1, source_target_pairs={{0,8},{8,16},{16,24},{24,0},{1,9},{9,17},{17,25},{25,1},{2,10},{10... | collective-permute-start | bytes 1474568 | tf_op jit(solution)/shard_map/ppermute | solution.py:26
  788.0 25.9 %collective-permute-start.133 = (bf16[80,1280]{1,0:T(8,128)(2,1)S(1)}, bf16[80,1280]{1,0:T(8,128)(2,1)S(1)}, u32[]{:S(2)}, u32[]{:S(2)}) collective-permute-start(bf16[80,1280]{1,0:T(8,128)(2,1)S(1)} %get-tuple-element.806), channel_id=1, source_target_pairs={{16,0},{0,2},{24,8},{8,10},{18,16},{2,18},{26,24},{10,26},{17,1},{... | collective-permute-start | bytes 614408 | tf_op jit(solution)/shard_map/ppermute | solution.py:844
  (235 other events, 3282.7 us)

commit v3 on v2

--- a/solution.py
+++ b/solution.py
@@ -502,8 +502,8 @@
             a_xc.append(swap(a_x[k - 2], "c"))
         if k == 1:
             tok_other = swap(tok_own, "y")
-            a_z, a_x, w_y, w_out, tok_own = tick(a_z, a_x, w_y, w_out, tok_own)
             y_other = swap(other_half(w_y), "y")
+            a_z, a_x, w_out = tick(a_z, a_x, w_out)
             out_halves = [w_out[:, :half], w_out[:, half:]]
             out_parts = [
                 lax.ppermute(pick(y == 0, out_halves[i], out_halves[1 - i]), zy, spread[i])
@@ -706,10 +706,9 @@
             k = order[i - 3]
             term = own_sum(d_parts[k], d_c[k], d_y[k])
             total = hop((term if total is None else total.astype(F32) + term).astype(BF))
-        if i in (2, 4):
-            k = order[i // 2 - 1]
-            m_y[k] = swap(y_give(m_parts[k], m_c[k]), "y")
         if i == 4:
+            m_y[1] = swap(y_give(m_parts[1], m_c[1]), "y")
+        if i == 5:
             m_total = hop(own_sum(m_parts[1], m_c[1], m_y[1]).astype(BF))
         if i == zn:
             ff_keep, ff_give = tick(*ff_grads_call(
@@ -759,8 +758,7 @@
     d_mixed = product_t(d_branch_pair, full_out).reshape(2, tok, half)
     d_branch_y, local_back, cum_back = back_scan_call(d_mixed, branch_y, states, decays)
     leaving = decays[:, 0] * local_back[:, 0]
-    for k in order[2:]:
-        m_y[k] = swap(y_give(m_parts[k], m_c[k]), "y")
+    m_y[2] = swap(y_give(m_parts[2], m_c[2]), "y")
     send_home(1)
     give_across(turns[0])
     d_flat_y = d_branch_y.reshape(2 * tok, half)
@@ -821,6 +819,8 @@
     hold(yo, yo_a[0], yo_ac, 1)
     yo_x = {1: swap(x_give(yo[1]), "x")}
     send_home(2)
+    for k in order[2:]:
+        m_y[k] = swap(y_give(m_parts[k], m_c[k]), "y")
     d_conv, d_gates, d_prm = tick(*backward_call(
         branch_x, halo, prm, gates_t, local_back, cum_back, ends, states
     ))

time: 858 us -> 843 us (0.983)
  waiting for transfers between devices: 383 us -> 373 us
    unnamed x305 -> x327, local copies, waits for them, and re-layouts: 23.6 us -> 25.7 us
  transfers between devices with their start and end apart: 144 -> 144, of which waited for: 50 -> 46; matrix products, arithmetic and copies ran while one was open for 22% -> 23% of each run, Pallas kernels for 9% -> 10%
where the time goes in v3:
time: 843 us; the launch traced here: 833 us
  waiting for transfers between devices  373 us (44%)
  starting transfers between devices  141 us (17%)
  Pallas kernels  94.4 us (11%)
  other arithmetic  86.1 us (10%)
  matrix products  77.8 us (9%)
  local copies, waits for them, and re-layouts  56.8 us (7%)
    ppermute x41, waiting for transfers between devices, shifted(): return lax.ppermute(value, axes, pairs)  212 us
    ppermute x95, waiting for transfers between devices, swap(): return lax.ppermute(value, axis, [(0, 1), (1, 0)])  136 us
    ppermute x95, starting transfers between devices, swap(): return lax.ppermute(value, axis, [(0, 1), (1, 0)])  78.2 us
    dot_general x22, matrix products, dot(): lax.dot_general(left, right, (dims, ((), ())), preferred_element_type=F32)  77.8 us
    ppermute x41, starting transfers between devices, shifted(): return lax.ppermute(value, axes, pairs)  49.9 us
    unnamed x327, local copies, waits for them, and re-layouts  25.7 us
    pallas_call x1, Pallas kernels, ff_grads_call(): pl.pallas_call(functools.partial(ff_kernel, steps, fold), grid_spec=pltpu...  23.5 us
    pallas_call x3, Pallas kernels, place(): pl.pallas_call(functools.partial(place_kernel, plan, len(pieces)), in_spe...  20.3 us
  transfers between devices with their start and end apart: 144, of which 46 were waited for; matrix products, arithmetic and copies ran while one was open for 23% of the time, Pallas kernels for 10%

profile of v3, /device:TPU:0, one launch (start us, length us, event | category | flops | bytes accessed | tf_op | source)
XLA Modules:
  0.0 833.3 jit_solution(9307099224286245098)
XLA Ops:
  23.0 6.7 collective-permute-done.3.refs_4_
  32.6 6.0 collective-permute-done.8
  45.4 4.4 collective-permute-start.11
  51.4 14.0 %collective-permute-done.11.refs_12_ = bf16[80,3328]{1,0:T(8,128)(2,1)S(1)} collective-permute-done((bf16[80,3328]{1,0:T(8,128)(2,1)S(1)}, bf16[80,3328]{1,0:T(8,128)(2,1)S(1)}, u32[]{:S(2)}, u32[]{:S(2)}) %collective-permute-start.11) | collective-permute-done | bytes 532512 | tf_op jit(solution)/shard_map/ppermute | solution.py:26
  70.4 9.6 %collective-permute-done.13.refs_14_ = bf16[80,3328]{1,0:T(8,128)(2,1)S(1)} collective-permute-done((bf16[80,3328]{1,0:T(8,128)(2,1)S(1)}, bf16[80,3328]{1,0:T(8,128)(2,1)S(1)}, u32[]{:S(2)}, u32[]{:S(2)}) %collective-permute-start.13) | collective-permute-done | bytes 532512 | tf_op jit(solution)/shard_map/ppermute | solution.py:21
  85.2 5.7 place_w_x.1
  94.4 5.2 convolution_convert_fusion
  99.7 4.7 collective-permute-done.22.refs_4_
  108.4 16.6 %collective-permute-done.23.halo_ref = bf16[2,16,1280]{2,1,0:T(8,128)(2,1)S(1)} collective-permute-done((bf16[2,16,1280]{2,1,0:T(8,128)(2,1)S(1)}, bf16[2,16,1280]{2,1,0:T(8,128)(2,1)S(1)}, u32[]{:S(2)}, u32[]{:S(2)}) %collective-permute-start.23) | collective-permute-done | bytes 81952 | tf_op jit(solution)/shard_map/ppermute | solution.py:26
  126.9 8.1 recurrence_forward.1
  150.0 6.2 collective-permute-done.28
  161.1 16.3 %collective-permute-done.34.refs_14_ = bf16[80,5120]{1,0:T(8,128)(2,1)S(1)} collective-permute-done((bf16[80,5120]{1,0:T(8,128)(2,1)S(1)}, bf16[80,5120]{1,0:T(8,128)(2,1)S(1)}, u32[]{:S(2)}, u32[]{:S(2)}) %collective-permute-start.34) | collective-permute-done | bytes 819232 | tf_op jit(solution)/shard_map/ppermute | solution.py:21
  177.4 5.4 collective-permute-done.35.refs_2_
  187.2 4.9 collective-permute-start.45
  193.1 9.5 %place_w_y_w_out.1 = (bf16[2560,1280]{1,0:T(8,128)(2,1)}, bf16[1280,2560]{1,0:T(8,128)(2,1)}) custom-call(bf16[80,5120]{1,0:T(8,128)(2,1)S(1)} %pad_maximum_fusion.15.refs_0_, bf16[80,5120]{1,0:T(8,128)(2,1)S(1)} %collective-permute-done.33.refs_1_, bf16[80,5120]{1,0:T(8,128)(2,1)} %collective-permute-done.25.refs_2_, ...), custom_call_target="tpu_custom_call" | custom-call | tf_op jit(solution)/shard_map/place_w_y_w_out/pallas_call | solution.py:263
  202.6 6.6 fusion.21
  217.6 34.8 %collective-permute-done.47 = bf16[320,768]{1,0:T(8,128)(2,1)S(1)} collective-permute-done((bf16[320,768]{1,0:T(8,128)(2,1)S(1)}, bf16[320,768]{1,0:T(8,128)(2,1)S(1)}, u32[]{:S(2)}, u32[]{:S(2)}) %collective-permute-start.47) | collective-permute-done | bytes 491552 | tf_op jit(solution)/shard_map/ppermute | solution.py:26
  260.8 28.9 %collective-permute-done.50 = bf16[128,2560]{1,0:T(8,128)(2,1)} collective-permute-done((bf16[128,2560]{1,0:T(8,128)(2,1)S(1)}, bf16[128,2560]{1,0:T(8,128)(2,1)}, u32[]{:S(2)}, u32[]{:S(2)}) %collective-permute-start.50) | collective-permute-done | bytes 655392 | tf_op jit(solution)/shard_map/ppermute | solution.py:26
  297.1 15.8 %collective-permute-done.55 = bf16[128,2560]{1,0:T(8,128)(2,1)} collective-permute-done((bf16[128,2560]{1,0:T(8,128)(2,1)}, bf16[128,2560]{1,0:T(8,128)(2,1)}, u32[]{:S(2)}, u32[]{:S(2)}) %collective-permute-start.55) | collective-permute-done | bytes 655392 | tf_op jit(solution)/shard_map/ppermute | solution.py:26
  312.9 11.4 %collective-permute-done.57 = bf16[128,2560]{1,0:T(8,128)(2,1)} collective-permute-done((bf16[128,2560]{1,0:T(8,128)(2,1)}, bf16[128,2560]{1,0:T(8,128)(2,1)}, u32[]{:S(2)}, u32[]{:S(2)}) %collective-permute-start.57) | collective-permute-done | bytes 655392 | tf_op jit(solution)/shard_map/ppermute | solution.py:26
  327.3 5.1 place_feed_forward.1
  351.5 9.0 %collective-permute-done.65 = bf16[128,2560]{1,0:T(8,128)(2,1)S(1)} collective-permute-done((bf16[128,2560]{1,0:T(8,128)(2,1)}, bf16[128,2560]{1,0:T(8,128)(2,1)S(1)}, u32[]{:S(2)}, u32[]{:S(2)}) %collective-permute-start.65) | collective-permute-done | bytes 655392 | tf_op jit(solution)/shard_map/ppermute | solution.py:26
  360.5 4.6 collective-permute-done.66
  381.9 6.9 fusion.127
  388.9 10.8 %collective-permute-done.72 = bf16[128,2560]{1,0:T(8,128)(2,1)} collective-permute-done((bf16[128,2560]{1,0:T(8,128)(2,1)S(1)}, bf16[128,2560]{1,0:T(8,128)(2,1)}, u32[]{:S(2)}, u32[]{:S(2)}) %collective-permute-start.72) | collective-permute-done | bytes 655392 | tf_op jit(solution)/shard_map/ppermute | solution.py:21
  407.5 5.7 fusion.138
  416.6 7.3 fusion.126
  437.6 5.7 fusion.139
  446.6 5.2 fusion.125
  465.8 23.5 %feed_forward_grads.1 = (f32[4,320,1536]{2,1,0:T(8,128)}, bf16[4,320,1536]{2,1,0:T(8,128)(2,1)}) custom-call(s32[3]{0:T(128)S(1)} %pad_add_fusion.where_ref, bf16[512,2560]{1,0:T(8,128)(2,1)} %copy-done.56, bf16[512,2560]{1,0:T(8,128)(2,1)} %copy-done.55, bf16[512,2560]{1,0:T(8,128)(2,1)} %copy-done.60, bf16[512,2560]{1,0:T(8,128)(2,1)} %copy-done.58, ...), custom_call_target="tpu_custom_call" | custom-call | tf_op jit(solution)/shard_map/feed_forward_grads/pallas_call | solution.py:380
  507.2 20.0 %collective-permute-done.96 = bf16[320,1536]{1,0:T(8,128)(2,1)S(1)} collective-permute-done((bf16[320,1536]{1,0:T(8,128)(2,1)S(1)}, bf16[320,1536]{1,0:T(8,128)(2,1)S(1)}, u32[]{:S(2)}, u32[]{:S(2)}) %collective-permute-start.96) | collective-permute-done | bytes 983072 | tf_op jit(solution)/shard_map/ppermute | solution.py:21
  537.0 9.7 %collective-permute-done.99 = bf16[320,768]{1,0:T(8,128)(2,1)S(1)} collective-permute-done((bf16[320,768]{1,0:T(8,128)(2,1)S(1)}, bf16[320,768]{1,0:T(8,128)(2,1)S(1)}, u32[]{:S(2)}, u32[]{:S(2)}) %collective-permute-start.99) | collective-permute-done | bytes 491552 | tf_op jit(solution)/shard_map/ppermute | solution.py:21
  555.8 7.1 recurrence_back_scan.1
  565.3 5.8 grad_w_y_w_out.2
  572.8 4.8 collective-permute-done.103
  603.5 13.9 %recurrence_backward.1 = (f32[2,128,1280]{2,1,0:T(8,128)S(1)}, f32[2,1280,256]{2,1,0:T(8,128)}, f32[8,1280]{1,0:T(8,128)S(1)}) custom-call(bf16[2,128,1280]{2,1,0:T(8,128)(2,1)S(1)} %bitcast.317, bf16[2,16,1280]{2,1,0:T(8,128)(2,1)S(1)} %copy-done.33, f32[8,1280]{1,0:T(8,128)S(1)} %copy-done.31, bf16[2,1280,256]{2,1,0:T(8,128)(2,1)S(1)} %copy-done.6, ...), custom_call_target="tpu_custom_call" | custom-call | tf_op jit(solution)/shard_map/recurrence_backward/pallas_call | solution.py:239
  618.9 5.9 grad_w_y_w_out.3
  627.6 6.3 grad_w_x.1
  647.7 8.0 collective-permute-done.116
  655.7 6.4 collective-permute-done.117
  673.5 5.2 fusion.143
  681.6 22.8 %collective-permute-done.123 = bf16[2,2,80,1536]{3,2,1,0:T(8,128)(2,1)S(1)} collective-permute-done((bf16[2,2,80,1536]{3,2,1,0:T(8,128)(2,1)}, bf16[2,2,80,1536]{3,2,1,0:T(8,128)(2,1)S(1)}, u32[]{:S(2)}, u32[]{:S(2)}) %collective-permute-start.123) | collective-permute-done | bytes 983072 | tf_op jit(solution)/shard_map/ppermute | solution.py:21
  706.9 6.7 collective-permute-done.122
  729.9 18.6 %collective-permute-done.127 = bf16[2,2,80,1536]{3,2,1,0:T(8,128)(2,1)} collective-permute-done((bf16[2,2,80,1536]{3,2,1,0:T(8,128)(2,1)}, bf16[2,2,80,1536]{3,2,1,0:T(8,128)(2,1)}, u32[]{:S(2)}, u32[]{:S(2)}) %collective-permute-start.127) | collective-permute-done | bytes 983072 | tf_op jit(solution)/shard_map/ppermute | solution.py:21
  749.7 8.4 %collective-permute-done.126 = bf16[288,2560]{1,0:T(8,128)(2,1)S(1)} collective-permute-done((bf16[288,2560]{1,0:T(8,128)(2,1)}, bf16[288,2560]{1,0:T(8,128)(2,1)S(1)}, u32[]{:S(2)}, u32[]{:S(2)}) %collective-permute-start.126) | collective-permute-done | bytes 1474592 | tf_op jit(solution)/shard_map/ppermute | solution.py:26
  758.2 8.3 collective-permute-done.128
  779.9 18.7 %collective-permute-done.133 = bf16[80,1280]{1,0:T(8,128)(2,1)S(1)} collective-permute-done((bf16[80,1280]{1,0:T(8,128)(2,1)S(1)}, bf16[80,1280]{1,0:T(8,128)(2,1)S(1)}, u32[]{:S(2)}, u32[]{:S(2)}) %collective-permute-start.133) | collective-permute-done | bytes 204832 | tf_op jit(solution)/shard_map/ppermute | solution.py:844
  810.3 8.6 %collective-permute-done.137 = f32[12,1280]{1,0:T(8,128)S(1)} collective-permute-done((f32[12,1280]{1,0:T(8,128)S(1)}, f32[12,1280]{1,0:T(8,128)S(1)}, u32[]{:S(2)}, u32[]{:S(2)}) %collective-permute-start.137) | collective-permute-done | bytes 61472 | tf_op jit(solution)/shard_map/ppermute | solution.py:26
  (776 shorter events, 339.3 us)
Async XLA Ops:
  41.0 26.4 %collective-permute-start.15 = (bf16[80,3328]{1,0:T(8,128)(2,1)S(1)}, bf16[80,3328]{1,0:T(8,128)(2,1)S(1)}, u32[]{:S(2)}, u32[]{:S(2)}) collective-permute-start(bf16[80,3328]{1,0:T(8,128)(2,1)S(1)} %collective-permute-done.3.refs_4_), channel_id=1, source_target_pairs={{0,1},{1,0},{2,3},{3,2},{4,5},{5,4},{6,7},{7,6},{8,9},{9,8},{10,11... | collective-permute-start | bytes 1597448 | tf_op jit(solution)/shard_map/ppermute | solution.py:21
  83.0 42.0 %collective-permute-start.25 = (bf16[80,5120]{1,0:T(8,128)(2,1)S(1)}, bf16[80,5120]{1,0:T(8,128)(2,1)}, u32[]{:S(2)}, u32[]{:S(2)}) collective-permute-start(bf16[80,5120]{1,0:T(8,128)(2,1)S(1)} %pad_maximum_fusion.15.refs_0_), channel_id=1, source_target_pairs={{0,4},{4,0},{1,5},{5,1},{2,6},{6,2},{3,7},{7,3},{8,12},{12,8},{9,1... | collective-permute-start | bytes 2457608 | tf_op jit(solution)/shard_map/ppermute | solution.py:21
  185.8 25.4 %collective-permute-start.43 = (bf16[320,768]{1,0:T(8,128)(2,1)}, bf16[320,768]{1,0:T(8,128)(2,1)}, u32[]{:S(2)}, u32[]{:S(2)}) collective-permute-start(bf16[320,768]{1,0:T(8,128)(2,1)} %slice.455), channel_id=1, source_target_pairs={{0,16},{8,24},{16,0},{24,8},{1,17},{9,25},{17,1},{25,9},{2,18},{10... | collective-permute-start | bytes 1474568 | tf_op jit(solution)/shard_map/ppermute | solution.py:26
  185.9 25.3 %collective-permute-start.44 = (bf16[320,1536]{1,0:T(8,128)(2,1)S(1)}, bf16[320,1536]{1,0:T(8,128)(2,1)S(1)}, u32[]{:S(2)}, u32[]{:S(2)}) collective-permute-start(bf16[320,1536]{1,0:T(8,128)(2,1)S(1)} %pad_maximum_fusion.6.refs_0_), channel_id=1, source_target_pairs={{0,4},{4,0},{1,5},{5,1},{2,6},{6,2},{3,7},{7,3},{8,12},{12,8},{9,1... | collective-permute-start | bytes 2949128 | tf_op jit(solution)/shard_map/ppermute | solution.py:21
  211.3 41.2 %collective-permute-start.48 = (bf16[320,1536]{1,0:T(8,128)(2,1)S(1)}, bf16[320,1536]{1,0:T(8,128)(2,1)S(1)}, u32[]{:S(2)}, u32[]{:S(2)}) collective-permute-start(bf16[320,1536]{1,0:T(8,128)(2,1)S(1)} %collective-permute-done.35.refs_2_), channel_id=1, source_target_pairs={{0,4},{4,0},{1,5},{5,1},{2,6},{6,2},{3,7},{7,3},{8,12},{12,8},{9,1... | collective-permute-start | bytes 2949128 | tf_op jit(solution)/shard_map/ppermute | solution.py:21
  212.1 40.4 %collective-permute-start.46 = (bf16[128,2560]{1,0:T(8,128)(2,1)S(1)}, bf16[128,2560]{1,0:T(8,128)(2,1)S(1)}, u32[]{:S(2)}, u32[]{:S(2)}) collective-permute-start(bf16[128,2560]{1,0:T(8,128)(2,1)S(1)} %slice.916), channel_id=1, source_target_pairs={{0,2},{2,0},{1,3},{3,1},{4,6},{6,4},{5,7},{7,5},{8,10},{10,8},{9,1... | collective-permute-start | bytes 1966088 | tf_op jit(solution)/shard_map/ppermute | solution.py:21
  215.0 37.5 %collective-permute-start.49 = (bf16[128,2560]{1,0:T(8,128)(2,1)S(1)}, bf16[128,2560]{1,0:T(8,128)(2,1)}, u32[]{:S(2)}, u32[]{:S(2)}) collective-permute-start(bf16[128,2560]{1,0:T(8,128)(2,1)S(1)} %bitcast.362), channel_id=1, source_target_pairs={{0,8},{8,16},{16,24},{24,0},{1,9},{9,17},{17,25},{25,1},{2,10},{10... | collective-permute-start | bytes 1966088 | tf_op jit(solution)/shard_map/ppermute | solution.py:26
  215.8 36.7 %collective-permute-start.47 = (bf16[320,768]{1,0:T(8,128)(2,1)S(1)}, bf16[320,768]{1,0:T(8,128)(2,1)S(1)}, u32[]{:S(2)}, u32[]{:S(2)}) collective-permute-start(bf16[320,768]{1,0:T(8,128)(2,1)S(1)} %slice.456), channel_id=1, source_target_pairs={{0,16},{8,24},{16,0},{24,8},{1,17},{9,25},{17,1},{25,9},{2,18},{10... | collective-permute-start | bytes 1474568 | tf_op jit(solution)/shard_map/ppermute | solution.py:26
  253.6 37.2 %collective-permute-start.53 = (bf16[320,1536]{1,0:T(8,128)(2,1)S(1)}, bf16[320,1536]{1,0:T(8,128)(2,1)}, u32[]{:S(2)}, u32[]{:S(2)}) collective-permute-start(bf16[320,1536]{1,0:T(8,128)(2,1)S(1)} %copy-done.91), channel_id=1, source_target_pairs={{0,24},{8,0},{16,8},{24,16},{1,25},{9,1},{17,9},{25,17},{2,26},{10... | collective-permute-start | bytes 2949128 | tf_op jit(solution)/shard_map/ppermute | solution.py:26
  256.7 34.0 %collective-permute-start.54 = (bf16[320,1536]{1,0:T(8,128)(2,1)S(1)}, bf16[320,1536]{1,0:T(8,128)(2,1)S(1)}, u32[]{:S(2)}, u32[]{:S(2)}) collective-permute-start(bf16[320,1536]{1,0:T(8,128)(2,1)S(1)} %pad_maximum_fusion.10), channel_id=1, source_target_pairs={{0,4},{4,0},{1,5},{5,1},{2,6},{6,2},{3,7},{7,3},{8,12},{12,8},{9,1... | collective-permute-start | bytes 2949128 | tf_op jit(solution)/shard_map/ppermute | solution.py:21
  258.6 31.1 %collective-permute-start.50 = (bf16[128,2560]{1,0:T(8,128)(2,1)S(1)}, bf16[128,2560]{1,0:T(8,128)(2,1)}, u32[]{:S(2)}, u32[]{:S(2)}) collective-permute-start(bf16[128,2560]{1,0:T(8,128)(2,1)S(1)} %multiply_convert_fusion.2), channel_id=1, source_target_pairs={{0,8},{8,16},{16,24},{24,0},{1,9},{9,17},{17,25},{25,1},{2,10},{10... | collective-permute-start | bytes 1966088 | tf_op jit(solution)/shard_map/ppermute | solution.py:26
  258.7 31.0 %collective-permute-start.51 = (bf16[128,2560]{1,0:T(8,128)(2,1)S(1)}, bf16[128,2560]{1,0:T(8,128)(2,1)S(1)}, u32[]{:S(2)}, u32[]{:S(2)}) collective-permute-start(bf16[128,2560]{1,0:T(8,128)(2,1)S(1)} %multiply_convert_fusion.2), channel_id=1, source_target_pairs={{0,2},{2,0},{1,3},{3,1},{4,6},{6,4},{5,7},{7,5},{8,10},{10,8},{9,1... | collective-permute-start | bytes 1966088 | tf_op jit(solution)/shard_map/ppermute | solution.py:21
  259.1 30.7 %collective-permute-start.52 = (bf16[128,2560]{1,0:T(8,128)(2,1)}, bf16[128,2560]{1,0:T(8,128)(2,1)S(1)}, u32[]{:S(2)}, u32[]{:S(2)}) collective-permute-start(bf16[128,2560]{1,0:T(8,128)(2,1)} %collective-permute-done.49), channel_id=1, source_target_pairs={{0,2},{2,0},{1,3},{3,1},{4,6},{6,4},{5,7},{7,5},{8,10},{10,8},{9,1... | collective-permute-start | bytes 1966088 | tf_op jit(solution)/shard_map/ppermute | solution.py:21
  291.7 32.6 %collective-permute-start.58 = (bf16[320,1536]{1,0:T(8,128)(2,1)}, bf16[320,1536]{1,0:T(8,128)(2,1)}, u32[]{:S(2)}, u32[]{:S(2)}) collective-permute-start(bf16[320,1536]{1,0:T(8,128)(2,1)} %collective-permute-done.53.refs_6_), channel_id=1, source_target_pairs={{0,4},{4,0},{1,5},{5,1},{2,6},{6,2},{3,7},{7,3},{8,12},{12,8},{9,1... | collective-permute-start | bytes 2949128 | tf_op jit(solution)/shard_map/ppermute | solution.py:21
  294.2 30.1 %collective-permute-start.57 = (bf16[128,2560]{1,0:T(8,128)(2,1)}, bf16[128,2560]{1,0:T(8,128)(2,1)}, u32[]{:S(2)}, u32[]{:S(2)}) collective-permute-start(bf16[128,2560]{1,0:T(8,128)(2,1)} %collective-permute-done.49), channel_id=1, source_target_pairs={{0,8},{8,16},{16,24},{24,0},{1,9},{9,17},{17,25},{25,1},{2,10},{10... | collective-permute-start | bytes 1966088 | tf_op jit(solution)/shard_map/ppermute | solution.py:26
  295.6 45.1 %collective-permute-start.62 = (bf16[128,2560]{1,0:T(8,128)(2,1)}, bf16[128,2560]{1,0:T(8,128)(2,1)}, u32[]{:S(2)}, u32[]{:S(2)}) collective-permute-start(bf16[128,2560]{1,0:T(8,128)(2,1)} %copy-done.104), channel_id=1, source_target_pairs={{0,1},{1,0},{2,3},{3,2},{4,5},{5,4},{6,7},{7,6},{8,9},{9,8},{10,11... | collective-permute-start | bytes 1966088 | tf_op jit(solution)/shard_map/ppermute | solution.py:21
  334.4 26.1 %collective-permute-start.65 = (bf16[128,2560]{1,0:T(8,128)(2,1)}, bf16[128,2560]{1,0:T(8,128)(2,1)S(1)}, u32[]{:S(2)}, u32[]{:S(2)}) collective-permute-start(bf16[128,2560]{1,0:T(8,128)(2,1)} %collective-permute-done.57), channel_id=1, source_target_pairs={{0,8},{8,16},{16,24},{24,0},{1,9},{9,17},{17,25},{25,1},{2,10},{10... | collective-permute-start | bytes 1966088 | tf_op jit(solution)/shard_map/ppermute | solution.py:26
  336.1 29.0 %collective-permute-start.66 = (bf16[128,2560]{1,0:T(8,128)(2,1)}, bf16[128,2560]{1,0:T(8,128)(2,1)S(1)}, u32[]{:S(2)}, u32[]{:S(2)}) collective-permute-start(bf16[128,2560]{1,0:T(8,128)(2,1)} %collective-permute-done.57), channel_id=1, source_target_pairs={{0,2},{2,0},{1,3},{3,1},{4,6},{6,4},{5,7},{7,5},{8,10},{10,8},{9,1... | collective-permute-start | bytes 1966088 | tf_op jit(solution)/shard_map/ppermute | solution.py:21
  371.7 28.0 %collective-permute-start.72 = (bf16[128,2560]{1,0:T(8,128)(2,1)S(1)}, bf16[128,2560]{1,0:T(8,128)(2,1)}, u32[]{:S(2)}, u32[]{:S(2)}) collective-permute-start(bf16[128,2560]{1,0:T(8,128)(2,1)S(1)} %collective-permute-done.65), channel_id=1, source_target_pairs={{0,2},{2,0},{1,3},{3,1},{4,6},{6,4},{5,7},{7,5},{8,10},{10,8},{9,1... | collective-permute-start | bytes 1966088 | tf_op jit(solution)/shard_map/ppermute | solution.py:21
  373.3 26.4 %collective-permute-start.73 = (bf16[2,128,2560]{2,1,0:T(8,128)(2,1)}, bf16[2,128,2560]{2,1,0:T(8,128)(2,1)S(1)}, u32[]{:S(2)}, u32[]{:S(2)}) collective-permute-start(bf16[2,128,2560]{2,1,0:T(8,128)(2,1)} %slice.914), channel_id=1, source_target_pairs={{0,1},{1,0},{2,3},{3,2},{4,5},{5,4},{6,7},{7,6},{8,9},{9,8},{10,11... | collective-permute-start | bytes 3932168 | tf_op jit(solution)/shard_map/ppermute | solution.py:21
  373.4 26.3 %collective-permute-start.74 = (bf16[2,128,2560]{2,1,0:T(8,128)(2,1)}, bf16[2,128,2560]{2,1,0:T(8,128)(2,1)S(1)}, u32[]{:S(2)}, u32[]{:S(2)}) collective-permute-start(bf16[2,128,2560]{2,1,0:T(8,128)(2,1)} %slice.913), channel_id=1, source_target_pairs={{0,1},{1,0},{2,3},{3,2},{4,5},{5,4},{6,7},{7,6},{8,9},{9,8},{10,11... | collective-permute-start | bytes 3932168 | tf_op jit(solution)/shard_map/ppermute | solution.py:21
  429.4 25.4 %collective-permute-start.86 = (bf16[2,128,2560]{2,1,0:T(8,128)(2,1)}, bf16[2,128,2560]{2,1,0:T(8,128)(2,1)}, u32[]{:S(2)}, u32[]{:S(2)}) collective-permute-start(bf16[2,128,2560]{2,1,0:T(8,128)(2,1)} %slice.910), channel_id=1, source_target_pairs={{0,1},{1,0},{2,3},{3,2},{4,5},{5,4},{6,7},{7,6},{8,9},{9,8},{10,11... | collective-permute-start | bytes 3932168 | tf_op jit(solution)/shard_map/ppermute | solution.py:21
  456.0 39.0 %collective-permute-start.89 = (bf16[2,128,2560]{2,1,0:T(8,128)(2,1)}, bf16[2,128,2560]{2,1,0:T(8,128)(2,1)}, u32[]{:S(2)}, u32[]{:S(2)}) collective-permute-start(bf16[2,128,2560]{2,1,0:T(8,128)(2,1)} %slice.909), channel_id=1, source_target_pairs={{0,1},{1,0},{2,3},{3,2},{4,5},{5,4},{6,7},{7,6},{8,9},{9,8},{10,11... | collective-permute-start | bytes 3932168 | tf_op jit(solution)/shard_map/ppermute | solution.py:21
  458.1 35.4 %collective-permute-start.90 = (bf16[128,2560]{1,0:T(8,128)(2,1)}, bf16[128,2560]{1,0:T(8,128)(2,1)}, u32[]{:S(2)}, u32[]{:S(2)}) collective-permute-start(bf16[128,2560]{1,0:T(8,128)(2,1)} %fusion.91), channel_id=1, source_target_pairs={{0,2},{2,0},{1,3},{3,1},{4,6},{6,4},{5,7},{7,5},{8,10},{10,8},{9,1... | collective-permute-start | bytes 1966088 | tf_op jit(solution)/shard_map/ppermute | solution.py:21
  461.2 33.9 %collective-permute-start.91 = (bf16[128,2560]{1,0:T(8,128)(2,1)}, bf16[128,2560]{1,0:T(8,128)(2,1)}, u32[]{:S(2)}, u32[]{:S(2)}) collective-permute-start(bf16[128,2560]{1,0:T(8,128)(2,1)} %fusion.45), channel_id=1, source_target_pairs={{0,8},{8,16},{16,24},{24,0},{1,9},{9,17},{17,25},{25,1},{2,10},{10... | collective-permute-start | bytes 1966088 | tf_op jit(solution)/shard_map/ppermute | solution.py:26
  462.2 32.9 %collective-permute-start.92 = (bf16[128,2560]{1,0:T(8,128)(2,1)}, bf16[128,2560]{1,0:T(8,128)(2,1)}, u32[]{:S(2)}, u32[]{:S(2)}) collective-permute-start(bf16[128,2560]{1,0:T(8,128)(2,1)} %fusion.92), channel_id=1, source_target_pairs={{0,2},{2,0},{1,3},{3,1},{4,6},{6,4},{5,7},{7,5},{8,10},{10,8},{9,1... | collective-permute-start | bytes 1966088 | tf_op jit(solution)/shard_map/ppermute | solution.py:21
  493.6 33.6 %collective-permute-start.96 = (bf16[320,1536]{1,0:T(8,128)(2,1)S(1)}, bf16[320,1536]{1,0:T(8,128)(2,1)S(1)}, u32[]{:S(2)}, u32[]{:S(2)}) collective-permute-start(bf16[320,1536]{1,0:T(8,128)(2,1)S(1)} %get-tuple-element.753), channel_id=1, source_target_pairs={{0,4},{4,0},{1,5},{5,1},{2,6},{6,2},{3,7},{7,3},{8,12},{12,8},{9,1... | collective-permute-start | bytes 2949128 | tf_op jit(solution)/shard_map/ppermute | solution.py:21
  496.9 30.3 %collective-permute-start.93 = (bf16[128,2560]{1,0:T(8,128)(2,1)S(1)}, bf16[128,2560]{1,0:T(8,128)(2,1)S(1)}, u32[]{:S(2)}, u32[]{:S(2)}) collective-permute-start(bf16[128,2560]{1,0:T(8,128)(2,1)S(1)} %fusion.42), channel_id=1, source_target_pairs={{0,8},{8,16},{16,24},{24,0},{1,9},{9,17},{17,25},{25,1},{2,10},{10... | collective-permute-start | bytes 1966088 | tf_op jit(solution)/shard_map/ppermute | solution.py:26
  499.8 27.4 %collective-permute-start.94 = (bf16[128,2560]{1,0:T(8,128)(2,1)S(1)}, bf16[128,2560]{1,0:T(8,128)(2,1)S(1)}, u32[]{:S(2)}, u32[]{:S(2)}) collective-permute-start(bf16[128,2560]{1,0:T(8,128)(2,1)S(1)} %fusion.93), channel_id=1, source_target_pairs={{0,2},{2,0},{1,3},{3,1},{4,6},{6,4},{5,7},{7,5},{8,10},{10,8},{9,1... | collective-permute-start | bytes 1966088 | tf_op jit(solution)/shard_map/ppermute | solution.py:21
  502.2 26.6 %collective-permute-start.97 = (bf16[128,2560]{1,0:T(8,128)(2,1)S(1)}, bf16[128,2560]{1,0:T(8,128)(2,1)S(1)}, u32[]{:S(2)}, u32[]{:S(2)}) collective-permute-start(bf16[128,2560]{1,0:T(8,128)(2,1)S(1)} %fusion.40), channel_id=1, source_target_pairs={{0,8},{8,16},{16,24},{24,0},{1,9},{9,17},{17,25},{25,1},{2,10},{10... | collective-permute-start | bytes 1966088 | tf_op jit(solution)/shard_map/ppermute | solution.py:26
  535.0 36.7 %collective-permute-start.104 = (bf16[320,1536]{1,0:T(8,128)(2,1)S(1)}, bf16[320,1536]{1,0:T(8,128)(2,1)S(1)}, u32[]{:S(2)}, u32[]{:S(2)}) collective-permute-start(bf16[320,1536]{1,0:T(8,128)(2,1)S(1)} %fusion.6), channel_id=1, source_target_pairs={{0,24},{8,0},{16,8},{24,16},{1,25},{9,1},{17,9},{25,17},{2,26},{10... | collective-permute-start | bytes 2949128 | tf_op jit(solution)/shard_map/ppermute | solution.py:26
  552.0 25.6 %collective-permute-start.102 = (bf16[128,2560]{1,0:T(8,128)(2,1)S(1)}, bf16[128,2560]{1,0:T(8,128)(2,1)S(1)}, u32[]{:S(2)}, u32[]{:S(2)}) collective-permute-start(bf16[128,2560]{1,0:T(8,128)(2,1)S(1)} %fusion.94), channel_id=1, source_target_pairs={{0,2},{2,0},{1,3},{3,1},{4,6},{6,4},{5,7},{7,5},{8,10},{10,8},{9,1... | collective-permute-start | bytes 1966088 | tf_op jit(solution)/shard_map/ppermute | solution.py:21
  553.3 25.1 %collective-permute-start.105 = (bf16[320,1536]{1,0:T(8,128)(2,1)}, bf16[320,1536]{1,0:T(8,128)(2,1)}, u32[]{:S(2)}, u32[]{:S(2)}) collective-permute-start(bf16[320,1536]{1,0:T(8,128)(2,1)} %get-tuple-element.638), channel_id=1, source_target_pairs={{0,4},{4,0},{1,5},{5,1},{2,6},{6,2},{3,7},{7,3},{8,12},{12,8},{9,1... | collective-permute-start | bytes 2949128 | tf_op jit(solution)/shard_map/ppermute | solution.py:21
  588.3 36.6 %collective-permute-start.114 = (bf16[128,2560]{1,0:T(8,128)(2,1)S(1)}, bf16[128,2560]{1,0:T(8,128)(2,1)S(1)}, u32[]{:S(2)}, u32[]{:S(2)}) collective-permute-start(bf16[128,2560]{1,0:T(8,128)(2,1)S(1)} %fusion.95), channel_id=1, source_target_pairs={{0,2},{2,0},{1,3},{3,1},{4,6},{6,4},{5,7},{7,5},{8,10},{10,8},{9,1... | collective-permute-start | bytes 1966088 | tf_op jit(solution)/shard_map/ppermute | solution.py:21
  598.0 26.9 %collective-permute-start.112 = (bf16[2,80,2560]{2,1,0:T(8,128)(2,1)S(1)}, bf16[2,80,2560]{2,1,0:T(8,128)(2,1)S(1)}, u32[]{:S(2)}, u32[]{:S(2)}) collective-permute-start(bf16[2,80,2560]{2,1,0:T(8,128)(2,1)S(1)} %get-tuple-element.750), channel_id=1, source_target_pairs={{0,4},{4,0},{1,5},{5,1},{2,6},{6,2},{3,7},{7,3},{8,12},{12,8},{9,1... | collective-permute-start | bytes 2457608 | tf_op jit(solution)/shard_map/ppermute | solution.py:21
  633.9 28.3 %collective-permute-start.118 = (bf16[4,4,80,1536]{3,2,1,0:T(8,128)(2,1)}, bf16[4,4,80,1536]{3,2,1,0:T(8,128)(2,1)}, u32[]{:S(2)}, u32[]{:S(2)}) collective-permute-start(bf16[4,4,80,1536]{3,2,1,0:T(8,128)(2,1)} %get-tuple-element.670), channel_id=1, source_target_pairs={{0,1},{1,0},{2,3},{3,2},{4,5},{5,4},{6,7},{7,6},{8,9},{9,8},{10,11... | collective-permute-start | bytes 11796488 | tf_op jit(solution)/shard_map/ppermute | solution.py:21
  633.9 28.3 %collective-permute-start.119 = (bf16[2,4,80,2560]{3,2,1,0:T(8,128)(2,1)}, bf16[2,4,80,2560]{3,2,1,0:T(8,128)(2,1)}, u32[]{:S(2)}, u32[]{:S(2)}) collective-permute-start(bf16[2,4,80,2560]{3,2,1,0:T(8,128)(2,1)} %get-tuple-element.671), channel_id=1, source_target_pairs={{0,1},{1,0},{2,3},{3,2},{4,5},{5,4},{6,7},{7,6},{8,9},{9,8},{10,11... | collective-permute-start | bytes 9830408 | tf_op jit(solution)/shard_map/ppermute | solution.py:21
  643.7 72.3 %collective-permute-start.125 = (bf16[320,1536]{1,0:T(8,128)(2,1)}, bf16[320,1536]{1,0:T(8,128)(2,1)S(1)}, u32[]{:S(2)}, u32[]{:S(2)}) collective-permute-start(bf16[320,1536]{1,0:T(8,128)(2,1)} %fusion.5), channel_id=1, source_target_pairs={{0,8},{8,16},{16,24},{24,0},{1,9},{9,17},{17,25},{25,1},{2,10},{10... | collective-permute-start | bytes 2949128 | tf_op jit(solution)/shard_map/ppermute | solution.py:26
  665.4 50.6 %collective-permute-start.121 = (bf16[2,80,2560]{2,1,0:T(8,128)(2,1)}, bf16[2,80,2560]{2,1,0:T(8,128)(2,1)}, u32[]{:S(2)}, u32[]{:S(2)}) collective-permute-start(bf16[2,80,2560]{2,1,0:T(8,128)(2,1)} %get-tuple-element.747), channel_id=1, source_target_pairs={{0,4},{4,0},{1,5},{5,1},{2,6},{6,2},{3,7},{7,3},{8,12},{12,8},{9,1... | collective-permute-start | bytes 2457608 | tf_op jit(solution)/shard_map/ppermute | solution.py:21
  669.7 43.9 %collective-permute-start.122 = (bf16[288,2560]{1,0:T(8,128)(2,1)}, bf16[288,2560]{1,0:T(8,128)(2,1)}, u32[]{:S(2)}, u32[]{:S(2)}) collective-permute-start(bf16[288,2560]{1,0:T(8,128)(2,1)} %pad_maximum_fusion), channel_id=1, source_target_pairs={{0,8},{8,16},{16,24},{24,0},{1,9},{9,17},{17,25},{25,1},{2,10},{10... | collective-permute-start | bytes 4423688 | tf_op jit(solution)/shard_map/ppermute | solution.py:26
  672.5 31.8 %collective-permute-start.123 = (bf16[2,2,80,1536]{3,2,1,0:T(8,128)(2,1)}, bf16[2,2,80,1536]{3,2,1,0:T(8,128)(2,1)S(1)}, u32[]{:S(2)}, u32[]{:S(2)}) collective-permute-start(bf16[2,2,80,1536]{3,2,1,0:T(8,128)(2,1)} %pad_maximum_fusion.12), channel_id=1, source_target_pairs={{0,4},{4,0},{1,5},{5,1},{2,6},{6,2},{3,7},{7,3},{8,12},{12,8},{9,1... | collective-permute-start | bytes 2949128 | tf_op jit(solution)/shard_map/ppermute | solution.py:21
  680.7 35.2 %collective-permute-start.124 = (bf16[128,2560]{1,0:T(8,128)(2,1)S(1)}, bf16[128,2560]{1,0:T(8,128)(2,1)S(1)}, u32[]{:S(2)}, u32[]{:S(2)}) collective-permute-start(bf16[128,2560]{1,0:T(8,128)(2,1)S(1)} %slice.915), channel_id=1, source_target_pairs={{0,2},{2,0},{1,3},{3,1},{4,6},{6,4},{5,7},{7,5},{8,10},{10,8},{9,1... | collective-permute-start | bytes 1966088 | tf_op jit(solution)/shard_map/ppermute | solution.py:21
  704.3 53.8 %collective-permute-start.120 = (bf16[2,80,2560]{2,1,0:T(8,128)(2,1)}, bf16[2,80,2560]{2,1,0:T(8,128)(2,1)}, u32[]{:S(2)}, u32[]{:S(2)}) collective-permute-start(bf16[2,80,2560]{2,1,0:T(8,128)(2,1)} %get-tuple-element.748), channel_id=1, source_target_pairs={{0,4},{4,0},{1,5},{5,1},{2,6},{6,2},{3,7},{7,3},{8,12},{12,8},{9,1... | collective-permute-start | bytes 2457608 | tf_op jit(solution)/shard_map/ppermute | solution.py:21
  720.9 37.2 %collective-permute-start.126 = (bf16[288,2560]{1,0:T(8,128)(2,1)}, bf16[288,2560]{1,0:T(8,128)(2,1)S(1)}, u32[]{:S(2)}, u32[]{:S(2)}) collective-permute-start(bf16[288,2560]{1,0:T(8,128)(2,1)} %pad_maximum_fusion.1), channel_id=1, source_target_pairs={{0,8},{8,16},{16,24},{24,0},{1,9},{9,17},{17,25},{25,1},{2,10},{10... | collective-permute-start | bytes 4423688 | tf_op jit(solution)/shard_map/ppermute | solution.py:26
  727.2 39.2 %collective-permute-start.128 = (bf16[2,80,1536]{2,1,0:T(8,128)(2,1)S(1)}, bf16[2,80,1536]{2,1,0:T(8,128)(2,1)S(1)}, u32[]{:S(2)}, u32[]{:S(2)}) collective-permute-start(bf16[2,80,1536]{2,1,0:T(8,128)(2,1)S(1)} %fusion.84), channel_id=1, source_target_pairs={{0,8},{8,16},{16,24},{24,0},{1,9},{9,17},{17,25},{25,1},{2,10},{10... | collective-permute-start | bytes 1474568 | tf_op jit(solution)/shard_map/ppermute | solution.py:26
  728.1 51.8 %collective-permute-start.134 = (bf16[320,1536]{1,0:T(8,128)(2,1)S(1)}, bf16[320,1536]{1,0:T(8,128)(2,1)S(1)}, u32[]{:S(2)}, u32[]{:S(2)}) collective-permute-start(bf16[320,1536]{1,0:T(8,128)(2,1)S(1)} %copy-done.90), channel_id=1, source_target_pairs={{0,4},{4,0},{1,5},{5,1},{2,6},{6,2},{3,7},{7,3},{8,12},{12,8},{9,1... | collective-permute-start | bytes 2949128 | tf_op jit(solution)/shard_map/ppermute | solution.py:21
  768.2 30.4 %collective-permute-start.130 = (bf16[2,80,1536]{2,1,0:T(8,128)(2,1)S(1)}, bf16[2,80,1536]{2,1,0:T(8,128)(2,1)S(1)}, u32[]{:S(2)}, u32[]{:S(2)}) collective-permute-start(bf16[2,80,1536]{2,1,0:T(8,128)(2,1)S(1)} %fusion.83), channel_id=1, source_target_pairs={{0,8},{8,16},{16,24},{24,0},{1,9},{9,17},{17,25},{25,1},{2,10},{10... | collective-permute-start | bytes 1474568 | tf_op jit(solution)/shard_map/ppermute | solution.py:26
  773.2 25.5 %collective-permute-start.133 = (bf16[80,1280]{1,0:T(8,128)(2,1)S(1)}, bf16[80,1280]{1,0:T(8,128)(2,1)S(1)}, u32[]{:S(2)}, u32[]{:S(2)}) collective-permute-start(bf16[80,1280]{1,0:T(8,128)(2,1)S(1)} %get-tuple-element.792), channel_id=1, source_target_pairs={{16,0},{0,2},{24,8},{8,10},{18,16},{2,18},{26,24},{10,26},{17,1},{... | collective-permute-start | bytes 614408 | tf_op jit(solution)/shard_map/ppermute | solution.py:844
  (246 other events, 3321.7 us)

commit v4 on v3

--- a/solution.py
+++ b/solution.py
@@ -796,9 +796,6 @@
     carry_back = carried(cum[:, -1], leaving, zn, x, -1)
     ends = jnp.pad(jnp.stack([carry_back, state_in], axis=1), ((0, 0), (0, 6), (0, 0)))
     yo_ac = swap(yo_a[1], "c")
-    ends, yo_a, yo_ac, d_flat_y, ff_sent, ff_give, m_y, m_total = tick(
-        ends, yo_a, yo_ac, d_flat_y, ff_sent, ff_give, m_y, m_total
-    )
 
     yo, xg = {}, {}
 
@@ -817,7 +814,12 @@
         return at_x(term, 1 - x).astype(BF)
 
     hold(yo, yo_a[0], yo_ac, 1)
-    yo_x = {1: swap(x_give(yo[1]), "x")}
+    yo_first = x_give(yo[1])
+    ends, yo_a, yo_ac, yo_first, d_flat_y, ff_sent, ff_give, m_y, m_total = tick(
+        ends, yo_a, yo_ac, yo_first, d_flat_y, ff_sent, ff_give, m_y, m_total
+    )
+    hold(yo, yo_a[0], yo_ac, 1)
+    yo_x = {1: swap(yo_first, "x")}
     send_home(2)
     for k in order[2:]:
         m_y[k] = swap(y_give(m_parts[k], m_c[k]), "y")
@@ -897,12 +899,13 @@
         elif t == 3:
             small = small + swap(small, "x")
             give_across([(0, None)])
-        if t == zn - 1:
+        if t == zn:
             out_came = return_rows(yo_total[:, :, half:])
-        if t == zn:
             y_came = return_columns(yo_total[:, :, :half])
         if t == zn:
-            small = small + sum(shifted(small, "z", by, zn, True) for by in range(1, zn))
+            doubling = zn & (zn - 1) == 0
+            if doubling:
+                small = small + shifted(small, "z", 1, zn, True)
             ff_home = joined(ff_home, range(1, zn))
             ff_home[0] = own_and_sent(0, None)
             g_gate, g_up, g_down = place_feed_forward_grads(
@@ -928,8 +931,8 @@
                 m_term = own_sum(m_parts[0], m_c[0], m_y[0])
                 result = (residual + m_total.astype(F32) + m_term).astype(BF)[None]
             else:
-                yo_total, xg_x, xg_total, small, out_came, ff_sent = tick(
-                    yo_total, xg_x, xg_total, small, out_came, ff_sent
+                yo_total, xg_x, xg_total, small, ff_sent = tick(
+                    yo_total, xg_x, xg_total, small, ff_sent
                 )
         else:
             xg_x, xg_total, small, y_came, out_came, yo_total = tick(
@@ -944,6 +947,13 @@
     grad_w_y = returned_columns(yo_total[:, :, :half], y_came)
     grad_w_out = jnp.concatenate(returned_rows(out_came), axis=1)
 
+    if doubling:
+        by = 2
+        while by < zn:
+            small = small + shifted(small, "z", by, zn, True)
+            by *= 2
+    else:
+        small = small + sum(shifted(small, "z", by, zn, True) for by in range(1, zn))
     beside = swap(small, "y")
     both_halves = jnp.concatenate(
         [pick(y == 0, small, beside)[:8], pick(y == 0, beside, small)[:8]], axis=1

time: 843 us -> 843 us (level)
    ppermute x41 -> x40, waiting for transfers between devices: 212 us -> 212 us  [shifted(): return lax.ppermute(value, axes, pairs)]
    ppermute x41 -> x40, starting transfers between devices: 49.9 us -> 49.4 us  [shifted(): return lax.ppermute(value, axes, pairs)]
    unnamed x327 -> x331, local copies, waits for them, and re-layouts: 25.7 us -> 25.8 us
  transfers between devices with their start and end apart: 144 -> 143, of which waited for: 46 -> 49; matrix products, arithmetic and copies ran while one was open for 23% -> 23% of each run, Pallas kernels for 10% -> 10%
where the time goes in v4:
time: 843 us; the launch traced here: 834 us
  waiting for transfers between devices  370 us (44%)
  starting transfers between devices  144 us (17%)
  Pallas kernels  94.5 us (11%)
  other arithmetic  85.5 us (10%)
  matrix products  77.9 us (9%)
  local copies, waits for them, and re-layouts  57 us (7%)
    ppermute x40, waiting for transfers between devices, shifted(): return lax.ppermute(value, axes, pairs)  212 us
    ppermute x95, waiting for transfers between devices, swap(): return lax.ppermute(value, axis, [(0, 1), (1, 0)])  138 us
    ppermute x95, starting transfers between devices, swap(): return lax.ppermute(value, axis, [(0, 1), (1, 0)])  78 us
    dot_general x22, matrix products, dot(): lax.dot_general(left, right, (dims, ((), ())), preferred_element_type=F32)  77.9 us
    ppermute x40, starting transfers between devices, shifted(): return lax.ppermute(value, axes, pairs)  49.4 us
    unnamed x331, local copies, waits for them, and re-layouts  25.8 us
    pallas_call x1, Pallas kernels, ff_grads_call(): pl.pallas_call(functools.partial(ff_kernel, steps, fold), grid_spec=pltpu...  23.5 us
    pallas_call x3, Pallas kernels, place(): pl.pallas_call(functools.partial(place_kernel, plan, len(pieces)), in_spe...  20.3 us
  transfers between devices with their start and end apart: 143, of which 49 were waited for; matrix products, arithmetic and copies ran while one was open for 23% of the time, Pallas kernels for 10%

profile of v4, /device:TPU:0, one launch (start us, length us, event | category | flops | bytes accessed | tf_op | source)
XLA Modules:
  0.0 833.8 jit_solution(18073491388217154882)
XLA Ops:
  23.0 6.7 collective-permute-done.3.refs_4_
  32.6 6.0 collective-permute-done.8
  51.4 14.0 %collective-permute-done.11.refs_12_ = bf16[80,3328]{1,0:T(8,128)(2,1)S(1)} collective-permute-done((bf16[80,3328]{1,0:T(8,128)(2,1)S(1)}, bf16[80,3328]{1,0:T(8,128)(2,1)S(1)}, u32[]{:S(2)}, u32[]{:S(2)}) %collective-permute-start.11) | collective-permute-done | bytes 532512 | tf_op jit(solution)/shard_map/ppermute | solution.py:26
  70.4 9.6 %collective-permute-done.13.refs_14_ = bf16[80,3328]{1,0:T(8,128)(2,1)S(1)} collective-permute-done((bf16[80,3328]{1,0:T(8,128)(2,1)S(1)}, bf16[80,3328]{1,0:T(8,128)(2,1)S(1)}, u32[]{:S(2)}, u32[]{:S(2)}) %collective-permute-start.13) | collective-permute-done | bytes 532512 | tf_op jit(solution)/shard_map/ppermute | solution.py:21
  85.2 5.7 place_w_x.1
  94.4 5.2 convolution_convert_fusion
  99.7 4.7 collective-permute-done.22.refs_4_
  108.4 16.6 %collective-permute-done.23.halo_ref = bf16[2,16,1280]{2,1,0:T(8,128)(2,1)S(1)} collective-permute-done((bf16[2,16,1280]{2,1,0:T(8,128)(2,1)S(1)}, bf16[2,16,1280]{2,1,0:T(8,128)(2,1)S(1)}, u32[]{:S(2)}, u32[]{:S(2)}) %collective-permute-start.23) | collective-permute-done | bytes 81952 | tf_op jit(solution)/shard_map/ppermute | solution.py:26
  126.9 8.1 recurrence_forward.1
  150.0 6.2 collective-permute-done.28
  161.1 16.3 %collective-permute-done.34.refs_14_ = bf16[80,5120]{1,0:T(8,128)(2,1)S(1)} collective-permute-done((bf16[80,5120]{1,0:T(8,128)(2,1)S(1)}, bf16[80,5120]{1,0:T(8,128)(2,1)S(1)}, u32[]{:S(2)}, u32[]{:S(2)}) %collective-permute-start.34) | collective-permute-done | bytes 819232 | tf_op jit(solution)/shard_map/ppermute | solution.py:21
  177.4 5.4 collective-permute-done.35.refs_2_
  187.2 4.9 collective-permute-start.45
  193.1 9.5 %place_w_y_w_out.1 = (bf16[2560,1280]{1,0:T(8,128)(2,1)}, bf16[1280,2560]{1,0:T(8,128)(2,1)}) custom-call(bf16[80,5120]{1,0:T(8,128)(2,1)S(1)} %pad_maximum_fusion.15.refs_0_, bf16[80,5120]{1,0:T(8,128)(2,1)S(1)} %collective-permute-done.33.refs_1_, bf16[80,5120]{1,0:T(8,128)(2,1)} %collective-permute-done.25.refs_2_, ...), custom_call_target="tpu_custom_call" | custom-call | tf_op jit(solution)/shard_map/place_w_y_w_out/pallas_call | solution.py:263
  202.6 6.6 fusion.21
  217.6 34.8 %collective-permute-done.47 = bf16[320,768]{1,0:T(8,128)(2,1)S(1)} collective-permute-done((bf16[320,768]{1,0:T(8,128)(2,1)S(1)}, bf16[320,768]{1,0:T(8,128)(2,1)S(1)}, u32[]{:S(2)}, u32[]{:S(2)}) %collective-permute-start.47) | collective-permute-done | bytes 491552 | tf_op jit(solution)/shard_map/ppermute | solution.py:26
  260.8 28.9 %collective-permute-done.50 = bf16[128,2560]{1,0:T(8,128)(2,1)} collective-permute-done((bf16[128,2560]{1,0:T(8,128)(2,1)S(1)}, bf16[128,2560]{1,0:T(8,128)(2,1)}, u32[]{:S(2)}, u32[]{:S(2)}) %collective-permute-start.50) | collective-permute-done | bytes 655392 | tf_op jit(solution)/shard_map/ppermute | solution.py:26
  297.2 15.8 %collective-permute-done.55 = bf16[128,2560]{1,0:T(8,128)(2,1)} collective-permute-done((bf16[128,2560]{1,0:T(8,128)(2,1)}, bf16[128,2560]{1,0:T(8,128)(2,1)}, u32[]{:S(2)}, u32[]{:S(2)}) %collective-permute-start.55) | collective-permute-done | bytes 655392 | tf_op jit(solution)/shard_map/ppermute | solution.py:26
  313.0 11.4 %collective-permute-done.57 = bf16[128,2560]{1,0:T(8,128)(2,1)} collective-permute-done((bf16[128,2560]{1,0:T(8,128)(2,1)}, bf16[128,2560]{1,0:T(8,128)(2,1)}, u32[]{:S(2)}, u32[]{:S(2)}) %collective-permute-start.57) | collective-permute-done | bytes 655392 | tf_op jit(solution)/shard_map/ppermute | solution.py:26
  327.4 5.1 place_feed_forward.1
  351.5 9.0 %collective-permute-done.65 = bf16[128,2560]{1,0:T(8,128)(2,1)S(1)} collective-permute-done((bf16[128,2560]{1,0:T(8,128)(2,1)}, bf16[128,2560]{1,0:T(8,128)(2,1)S(1)}, u32[]{:S(2)}, u32[]{:S(2)}) %collective-permute-start.65) | collective-permute-done | bytes 655392 | tf_op jit(solution)/shard_map/ppermute | solution.py:26
  360.5 4.6 collective-permute-done.66
  382.0 6.9 fusion.127
  388.9 10.8 %collective-permute-done.72 = bf16[128,2560]{1,0:T(8,128)(2,1)} collective-permute-done((bf16[128,2560]{1,0:T(8,128)(2,1)S(1)}, bf16[128,2560]{1,0:T(8,128)(2,1)}, u32[]{:S(2)}, u32[]{:S(2)}) %collective-permute-start.72) | collective-permute-done | bytes 655392 | tf_op jit(solution)/shard_map/ppermute | solution.py:21
  407.5 5.7 fusion.139
  416.7 7.3 fusion.126
  437.6 5.7 fusion.140
  446.6 5.2 fusion.125
  465.9 23.5 %feed_forward_grads.1 = (f32[4,320,1536]{2,1,0:T(8,128)}, bf16[4,320,1536]{2,1,0:T(8,128)(2,1)}) custom-call(s32[3]{0:T(128)S(1)} %pad_add_fusion.where_ref, bf16[512,2560]{1,0:T(8,128)(2,1)} %copy-done.56, bf16[512,2560]{1,0:T(8,128)(2,1)} %copy-done.55, bf16[512,2560]{1,0:T(8,128)(2,1)} %copy-done.60, bf16[512,2560]{1,0:T(8,128)(2,1)} %copy-done.58, ...), custom_call_target="tpu_custom_call" | custom-call | tf_op jit(solution)/shard_map/feed_forward_grads/pallas_call | solution.py:380
  507.2 19.9 %collective-permute-done.96 = bf16[320,1536]{1,0:T(8,128)(2,1)S(1)} collective-permute-done((bf16[320,1536]{1,0:T(8,128)(2,1)S(1)}, bf16[320,1536]{1,0:T(8,128)(2,1)S(1)}, u32[]{:S(2)}, u32[]{:S(2)}) %collective-permute-start.96) | collective-permute-done | bytes 983072 | tf_op jit(solution)/shard_map/ppermute | solution.py:21
  537.0 9.7 %collective-permute-done.99 = bf16[320,768]{1,0:T(8,128)(2,1)S(1)} collective-permute-done((bf16[320,768]{1,0:T(8,128)(2,1)S(1)}, bf16[320,768]{1,0:T(8,128)(2,1)S(1)}, u32[]{:S(2)}, u32[]{:S(2)}) %collective-permute-start.99) | collective-permute-done | bytes 491552 | tf_op jit(solution)/shard_map/ppermute | solution.py:21
  555.8 7.1 recurrence_back_scan.1
  565.3 5.8 grad_w_y_w_out.2
  572.8 4.8 collective-permute-done.103
  601.7 13.9 %recurrence_backward.1 = (f32[2,128,1280]{2,1,0:T(8,128)S(1)}, f32[2,1280,256]{2,1,0:T(8,128)}, f32[8,1280]{1,0:T(8,128)S(1)}) custom-call(bf16[2,128,1280]{2,1,0:T(8,128)(2,1)S(1)} %bitcast.319, bf16[2,16,1280]{2,1,0:T(8,128)(2,1)S(1)} %copy-done.33, f32[8,1280]{1,0:T(8,128)S(1)} %copy-done.31, bf16[2,1280,256]{2,1,0:T(8,128)(2,1)S(1)} %copy-done.6, ...), custom_call_target="tpu_custom_call" | custom-call | tf_op jit(solution)/shard_map/recurrence_backward/pallas_call | solution.py:239
  617.1 5.9 grad_w_y_w_out.3
  625.8 6.3 grad_w_x.1
  647.5 8.1 collective-permute-done.116
  655.6 6.7 collective-permute-done.117
  673.6 5.2 fusion.144
  681.6 22.9 %collective-permute-done.123 = bf16[2,2,80,1536]{3,2,1,0:T(8,128)(2,1)S(1)} collective-permute-done((bf16[2,2,80,1536]{3,2,1,0:T(8,128)(2,1)}, bf16[2,2,80,1536]{3,2,1,0:T(8,128)(2,1)S(1)}, u32[]{:S(2)}, u32[]{:S(2)}) %collective-permute-start.123) | collective-permute-done | bytes 983072 | tf_op jit(solution)/shard_map/ppermute | solution.py:21
  706.9 6.8 collective-permute-done.122
  730.0 18.6 %collective-permute-done.127 = bf16[2,2,80,1536]{3,2,1,0:T(8,128)(2,1)} collective-permute-done((bf16[2,2,80,1536]{3,2,1,0:T(8,128)(2,1)}, bf16[2,2,80,1536]{3,2,1,0:T(8,128)(2,1)}, u32[]{:S(2)}, u32[]{:S(2)}) %collective-permute-start.127) | collective-permute-done | bytes 983072 | tf_op jit(solution)/shard_map/ppermute | solution.py:21
  749.9 8.3 collective-permute-done.126
  758.3 8.2 collective-permute-done.128
  775.9 5.2 collective-permute-done.130
  785.0 7.1 collective-permute-start.137
  800.5 13.8 %collective-permute-done.137 = bf16[80,1280]{1,0:T(8,128)(2,1)S(1)} collective-permute-done((bf16[80,1280]{1,0:T(8,128)(2,1)S(1)}, bf16[80,1280]{1,0:T(8,128)(2,1)S(1)}, u32[]{:S(2)}, u32[]{:S(2)}) %collective-permute-start.137) | collective-permute-done | bytes 204832 | tf_op jit(solution)/shard_map/ppermute | solution.py:846
  (779 shorter events, 345.1 us)
Async XLA Ops:
  41.0 26.4 %collective-permute-start.15 = (bf16[80,3328]{1,0:T(8,128)(2,1)S(1)}, bf16[80,3328]{1,0:T(8,128)(2,1)S(1)}, u32[]{:S(2)}, u32[]{:S(2)}) collective-permute-start(bf16[80,3328]{1,0:T(8,128)(2,1)S(1)} %collective-permute-done.3.refs_4_), channel_id=1, source_target_pairs={{0,1},{1,0},{2,3},{3,2},{4,5},{5,4},{6,7},{7,6},{8,9},{9,8},{10,11... | collective-permute-start | bytes 1597448 | tf_op jit(solution)/shard_map/ppermute | solution.py:21
  82.9 42.0 %collective-permute-start.25 = (bf16[80,5120]{1,0:T(8,128)(2,1)S(1)}, bf16[80,5120]{1,0:T(8,128)(2,1)}, u32[]{:S(2)}, u32[]{:S(2)}) collective-permute-start(bf16[80,5120]{1,0:T(8,128)(2,1)S(1)} %pad_maximum_fusion.15.refs_0_), channel_id=1, source_target_pairs={{0,4},{4,0},{1,5},{5,1},{2,6},{6,2},{3,7},{7,3},{8,12},{12,8},{9,1... | collective-permute-start | bytes 2457608 | tf_op jit(solution)/shard_map/ppermute | solution.py:21
  185.8 25.5 %collective-permute-start.43 = (bf16[320,768]{1,0:T(8,128)(2,1)}, bf16[320,768]{1,0:T(8,128)(2,1)}, u32[]{:S(2)}, u32[]{:S(2)}) collective-permute-start(bf16[320,768]{1,0:T(8,128)(2,1)} %slice.455), channel_id=1, source_target_pairs={{0,16},{8,24},{16,0},{24,8},{1,17},{9,25},{17,1},{25,9},{2,18},{10... | collective-permute-start | bytes 1474568 | tf_op jit(solution)/shard_map/ppermute | solution.py:26
  185.9 25.4 %collective-permute-start.44 = (bf16[320,1536]{1,0:T(8,128)(2,1)S(1)}, bf16[320,1536]{1,0:T(8,128)(2,1)S(1)}, u32[]{:S(2)}, u32[]{:S(2)}) collective-permute-start(bf16[320,1536]{1,0:T(8,128)(2,1)S(1)} %pad_maximum_fusion.6.refs_0_), channel_id=1, source_target_pairs={{0,4},{4,0},{1,5},{5,1},{2,6},{6,2},{3,7},{7,3},{8,12},{12,8},{9,1... | collective-permute-start | bytes 2949128 | tf_op jit(solution)/shard_map/ppermute | solution.py:21
  211.3 41.2 %collective-permute-start.48 = (bf16[320,1536]{1,0:T(8,128)(2,1)S(1)}, bf16[320,1536]{1,0:T(8,128)(2,1)S(1)}, u32[]{:S(2)}, u32[]{:S(2)}) collective-permute-start(bf16[320,1536]{1,0:T(8,128)(2,1)S(1)} %collective-permute-done.35.refs_2_), channel_id=1, source_target_pairs={{0,4},{4,0},{1,5},{5,1},{2,6},{6,2},{3,7},{7,3},{8,12},{12,8},{9,1... | collective-permute-start | bytes 2949128 | tf_op jit(solution)/shard_map/ppermute | solution.py:21
  212.2 40.3 %collective-permute-start.46 = (bf16[128,2560]{1,0:T(8,128)(2,1)S(1)}, bf16[128,2560]{1,0:T(8,128)(2,1)S(1)}, u32[]{:S(2)}, u32[]{:S(2)}) collective-permute-start(bf16[128,2560]{1,0:T(8,128)(2,1)S(1)} %slice.915), channel_id=1, source_target_pairs={{0,2},{2,0},{1,3},{3,1},{4,6},{6,4},{5,7},{7,5},{8,10},{10,8},{9,1... | collective-permute-start | bytes 1966088 | tf_op jit(solution)/shard_map/ppermute | solution.py:21
  215.0 37.5 %collective-permute-start.49 = (bf16[128,2560]{1,0:T(8,128)(2,1)S(1)}, bf16[128,2560]{1,0:T(8,128)(2,1)}, u32[]{:S(2)}, u32[]{:S(2)}) collective-permute-start(bf16[128,2560]{1,0:T(8,128)(2,1)S(1)} %bitcast.365), channel_id=1, source_target_pairs={{0,8},{8,16},{16,24},{24,0},{1,9},{9,17},{17,25},{25,1},{2,10},{10... | collective-permute-start | bytes 1966088 | tf_op jit(solution)/shard_map/ppermute | solution.py:26
  215.7 36.7 %collective-permute-start.47 = (bf16[320,768]{1,0:T(8,128)(2,1)S(1)}, bf16[320,768]{1,0:T(8,128)(2,1)S(1)}, u32[]{:S(2)}, u32[]{:S(2)}) collective-permute-start(bf16[320,768]{1,0:T(8,128)(2,1)S(1)} %slice.456), channel_id=1, source_target_pairs={{0,16},{8,24},{16,0},{24,8},{1,17},{9,25},{17,1},{25,9},{2,18},{10... | collective-permute-start | bytes 1474568 | tf_op jit(solution)/shard_map/ppermute | solution.py:26
  253.6 37.1 %collective-permute-start.53 = (bf16[320,1536]{1,0:T(8,128)(2,1)S(1)}, bf16[320,1536]{1,0:T(8,128)(2,1)}, u32[]{:S(2)}, u32[]{:S(2)}) collective-permute-start(bf16[320,1536]{1,0:T(8,128)(2,1)S(1)} %copy-done.91), channel_id=1, source_target_pairs={{0,24},{8,0},{16,8},{24,16},{1,25},{9,1},{17,9},{25,17},{2,26},{10... | collective-permute-start | bytes 2949128 | tf_op jit(solution)/shard_map/ppermute | solution.py:26
  256.7 34.0 %collective-permute-start.54 = (bf16[320,1536]{1,0:T(8,128)(2,1)S(1)}, bf16[320,1536]{1,0:T(8,128)(2,1)S(1)}, u32[]{:S(2)}, u32[]{:S(2)}) collective-permute-start(bf16[320,1536]{1,0:T(8,128)(2,1)S(1)} %pad_maximum_fusion.10), channel_id=1, source_target_pairs={{0,4},{4,0},{1,5},{5,1},{2,6},{6,2},{3,7},{7,3},{8,12},{12,8},{9,1... | collective-permute-start | bytes 2949128 | tf_op jit(solution)/shard_map/ppermute | solution.py:21
  258.7 31.0 %collective-permute-start.50 = (bf16[128,2560]{1,0:T(8,128)(2,1)S(1)}, bf16[128,2560]{1,0:T(8,128)(2,1)}, u32[]{:S(2)}, u32[]{:S(2)}) collective-permute-start(bf16[128,2560]{1,0:T(8,128)(2,1)S(1)} %multiply_convert_fusion.2), channel_id=1, source_target_pairs={{0,8},{8,16},{16,24},{24,0},{1,9},{9,17},{17,25},{25,1},{2,10},{10... | collective-permute-start | bytes 1966088 | tf_op jit(solution)/shard_map/ppermute | solution.py:26
  258.7 31.0 %collective-permute-start.51 = (bf16[128,2560]{1,0:T(8,128)(2,1)S(1)}, bf16[128,2560]{1,0:T(8,128)(2,1)S(1)}, u32[]{:S(2)}, u32[]{:S(2)}) collective-permute-start(bf16[128,2560]{1,0:T(8,128)(2,1)S(1)} %multiply_convert_fusion.2), channel_id=1, source_target_pairs={{0,2},{2,0},{1,3},{3,1},{4,6},{6,4},{5,7},{7,5},{8,10},{10,8},{9,1... | collective-permute-start | bytes 1966088 | tf_op jit(solution)/shard_map/ppermute | solution.py:21
  259.1 30.6 %collective-permute-start.52 = (bf16[128,2560]{1,0:T(8,128)(2,1)}, bf16[128,2560]{1,0:T(8,128)(2,1)S(1)}, u32[]{:S(2)}, u32[]{:S(2)}) collective-permute-start(bf16[128,2560]{1,0:T(8,128)(2,1)} %collective-permute-done.49), channel_id=1, source_target_pairs={{0,2},{2,0},{1,3},{3,1},{4,6},{6,4},{5,7},{7,5},{8,10},{10,8},{9,1... | collective-permute-start | bytes 1966088 | tf_op jit(solution)/shard_map/ppermute | solution.py:21
  291.7 32.7 %collective-permute-start.58 = (bf16[320,1536]{1,0:T(8,128)(2,1)}, bf16[320,1536]{1,0:T(8,128)(2,1)}, u32[]{:S(2)}, u32[]{:S(2)}) collective-permute-start(bf16[320,1536]{1,0:T(8,128)(2,1)} %collective-permute-done.53.refs_6_), channel_id=1, source_target_pairs={{0,4},{4,0},{1,5},{5,1},{2,6},{6,2},{3,7},{7,3},{8,12},{12,8},{9,1... | collective-permute-start | bytes 2949128 | tf_op jit(solution)/shard_map/ppermute | solution.py:21
  294.2 30.1 %collective-permute-start.57 = (bf16[128,2560]{1,0:T(8,128)(2,1)}, bf16[128,2560]{1,0:T(8,128)(2,1)}, u32[]{:S(2)}, u32[]{:S(2)}) collective-permute-start(bf16[128,2560]{1,0:T(8,128)(2,1)} %collective-permute-done.49), channel_id=1, source_target_pairs={{0,8},{8,16},{16,24},{24,0},{1,9},{9,17},{17,25},{25,1},{2,10},{10... | collective-permute-start | bytes 1966088 | tf_op jit(solution)/shard_map/ppermute | solution.py:26
  295.7 45.1 %collective-permute-start.62 = (bf16[128,2560]{1,0:T(8,128)(2,1)}, bf16[128,2560]{1,0:T(8,128)(2,1)}, u32[]{:S(2)}, u32[]{:S(2)}) collective-permute-start(bf16[128,2560]{1,0:T(8,128)(2,1)} %copy-done.104), channel_id=1, source_target_pairs={{0,1},{1,0},{2,3},{3,2},{4,5},{5,4},{6,7},{7,6},{8,9},{9,8},{10,11... | collective-permute-start | bytes 1966088 | tf_op jit(solution)/shard_map/ppermute | solution.py:21
  334.4 26.1 %collective-permute-start.65 = (bf16[128,2560]{1,0:T(8,128)(2,1)}, bf16[128,2560]{1,0:T(8,128)(2,1)S(1)}, u32[]{:S(2)}, u32[]{:S(2)}) collective-permute-start(bf16[128,2560]{1,0:T(8,128)(2,1)} %collective-permute-done.57), channel_id=1, source_target_pairs={{0,8},{8,16},{16,24},{24,0},{1,9},{9,17},{17,25},{25,1},{2,10},{10... | collective-permute-start | bytes 1966088 | tf_op jit(solution)/shard_map/ppermute | solution.py:26
  336.2 29.0 %collective-permute-start.66 = (bf16[128,2560]{1,0:T(8,128)(2,1)}, bf16[128,2560]{1,0:T(8,128)(2,1)S(1)}, u32[]{:S(2)}, u32[]{:S(2)}) collective-permute-start(bf16[128,2560]{1,0:T(8,128)(2,1)} %collective-permute-done.57), channel_id=1, source_target_pairs={{0,2},{2,0},{1,3},{3,1},{4,6},{6,4},{5,7},{7,5},{8,10},{10,8},{9,1... | collective-permute-start | bytes 1966088 | tf_op jit(solution)/shard_map/ppermute | solution.py:21
  371.8 28.0 %collective-permute-start.72 = (bf16[128,2560]{1,0:T(8,128)(2,1)S(1)}, bf16[128,2560]{1,0:T(8,128)(2,1)}, u32[]{:S(2)}, u32[]{:S(2)}) collective-permute-start(bf16[128,2560]{1,0:T(8,128)(2,1)S(1)} %collective-permute-done.65), channel_id=1, source_target_pairs={{0,2},{2,0},{1,3},{3,1},{4,6},{6,4},{5,7},{7,5},{8,10},{10,8},{9,1... | collective-permute-start | bytes 1966088 | tf_op jit(solution)/shard_map/ppermute | solution.py:21
  373.3 26.4 %collective-permute-start.73 = (bf16[2,128,2560]{2,1,0:T(8,128)(2,1)}, bf16[2,128,2560]{2,1,0:T(8,128)(2,1)S(1)}, u32[]{:S(2)}, u32[]{:S(2)}) collective-permute-start(bf16[2,128,2560]{2,1,0:T(8,128)(2,1)} %slice.913), channel_id=1, source_target_pairs={{0,1},{1,0},{2,3},{3,2},{4,5},{5,4},{6,7},{7,6},{8,9},{9,8},{10,11... | collective-permute-start | bytes 3932168 | tf_op jit(solution)/shard_map/ppermute | solution.py:21
  373.5 26.3 %collective-permute-start.74 = (bf16[2,128,2560]{2,1,0:T(8,128)(2,1)}, bf16[2,128,2560]{2,1,0:T(8,128)(2,1)S(1)}, u32[]{:S(2)}, u32[]{:S(2)}) collective-permute-start(bf16[2,128,2560]{2,1,0:T(8,128)(2,1)} %slice.912), channel_id=1, source_target_pairs={{0,1},{1,0},{2,3},{3,2},{4,5},{5,4},{6,7},{7,6},{8,9},{9,8},{10,11... | collective-permute-start | bytes 3932168 | tf_op jit(solution)/shard_map/ppermute | solution.py:21
  429.5 25.4 %collective-permute-start.86 = (bf16[2,128,2560]{2,1,0:T(8,128)(2,1)}, bf16[2,128,2560]{2,1,0:T(8,128)(2,1)}, u32[]{:S(2)}, u32[]{:S(2)}) collective-permute-start(bf16[2,128,2560]{2,1,0:T(8,128)(2,1)} %slice.909), channel_id=1, source_target_pairs={{0,1},{1,0},{2,3},{3,2},{4,5},{5,4},{6,7},{7,6},{8,9},{9,8},{10,11... | collective-permute-start | bytes 3932168 | tf_op jit(solution)/shard_map/ppermute | solution.py:21
  456.1 39.0 %collective-permute-start.89 = (bf16[2,128,2560]{2,1,0:T(8,128)(2,1)}, bf16[2,128,2560]{2,1,0:T(8,128)(2,1)}, u32[]{:S(2)}, u32[]{:S(2)}) collective-permute-start(bf16[2,128,2560]{2,1,0:T(8,128)(2,1)} %slice.908), channel_id=1, source_target_pairs={{0,1},{1,0},{2,3},{3,2},{4,5},{5,4},{6,7},{7,6},{8,9},{9,8},{10,11... | collective-permute-start | bytes 3932168 | tf_op jit(solution)/shard_map/ppermute | solution.py:21
  458.2 35.3 %collective-permute-start.90 = (bf16[128,2560]{1,0:T(8,128)(2,1)}, bf16[128,2560]{1,0:T(8,128)(2,1)}, u32[]{:S(2)}, u32[]{:S(2)}) collective-permute-start(bf16[128,2560]{1,0:T(8,128)(2,1)} %fusion.91), channel_id=1, source_target_pairs={{0,2},{2,0},{1,3},{3,1},{4,6},{6,4},{5,7},{7,5},{8,10},{10,8},{9,1... | collective-permute-start | bytes 1966088 | tf_op jit(solution)/shard_map/ppermute | solution.py:21
  461.2 33.9 %collective-permute-start.91 = (bf16[128,2560]{1,0:T(8,128)(2,1)}, bf16[128,2560]{1,0:T(8,128)(2,1)}, u32[]{:S(2)}, u32[]{:S(2)}) collective-permute-start(bf16[128,2560]{1,0:T(8,128)(2,1)} %fusion.45), channel_id=1, source_target_pairs={{0,8},{8,16},{16,24},{24,0},{1,9},{9,17},{17,25},{25,1},{2,10},{10... | collective-permute-start | bytes 1966088 | tf_op jit(solution)/shard_map/ppermute | solution.py:26
  462.2 32.9 %collective-permute-start.92 = (bf16[128,2560]{1,0:T(8,128)(2,1)}, bf16[128,2560]{1,0:T(8,128)(2,1)}, u32[]{:S(2)}, u32[]{:S(2)}) collective-permute-start(bf16[128,2560]{1,0:T(8,128)(2,1)} %fusion.92), channel_id=1, source_target_pairs={{0,2},{2,0},{1,3},{3,1},{4,6},{6,4},{5,7},{7,5},{8,10},{10,8},{9,1... | collective-permute-start | bytes 1966088 | tf_op jit(solution)/shard_map/ppermute | solution.py:21
  493.5 33.7 %collective-permute-start.96 = (bf16[320,1536]{1,0:T(8,128)(2,1)S(1)}, bf16[320,1536]{1,0:T(8,128)(2,1)S(1)}, u32[]{:S(2)}, u32[]{:S(2)}) collective-permute-start(bf16[320,1536]{1,0:T(8,128)(2,1)S(1)} %get-tuple-element.749), channel_id=1, source_target_pairs={{0,4},{4,0},{1,5},{5,1},{2,6},{6,2},{3,7},{7,3},{8,12},{12,8},{9,1... | collective-permute-start | bytes 2949128 | tf_op jit(solution)/shard_map/ppermute | solution.py:21
  496.9 30.3 %collective-permute-start.93 = (bf16[128,2560]{1,0:T(8,128)(2,1)S(1)}, bf16[128,2560]{1,0:T(8,128)(2,1)S(1)}, u32[]{:S(2)}, u32[]{:S(2)}) collective-permute-start(bf16[128,2560]{1,0:T(8,128)(2,1)S(1)} %fusion.42), channel_id=1, source_target_pairs={{0,8},{8,16},{16,24},{24,0},{1,9},{9,17},{17,25},{25,1},{2,10},{10... | collective-permute-start | bytes 1966088 | tf_op jit(solution)/shard_map/ppermute | solution.py:26
  499.8 27.3 %collective-permute-start.94 = (bf16[128,2560]{1,0:T(8,128)(2,1)S(1)}, bf16[128,2560]{1,0:T(8,128)(2,1)S(1)}, u32[]{:S(2)}, u32[]{:S(2)}) collective-permute-start(bf16[128,2560]{1,0:T(8,128)(2,1)S(1)} %fusion.93), channel_id=1, source_target_pairs={{0,2},{2,0},{1,3},{3,1},{4,6},{6,4},{5,7},{7,5},{8,10},{10,8},{9,1... | collective-permute-start | bytes 1966088 | tf_op jit(solution)/shard_map/ppermute | solution.py:21
  502.2 26.6 %collective-permute-start.97 = (bf16[128,2560]{1,0:T(8,128)(2,1)S(1)}, bf16[128,2560]{1,0:T(8,128)(2,1)S(1)}, u32[]{:S(2)}, u32[]{:S(2)}) collective-permute-start(bf16[128,2560]{1,0:T(8,128)(2,1)S(1)} %fusion.40), channel_id=1, source_target_pairs={{0,8},{8,16},{16,24},{24,0},{1,9},{9,17},{17,25},{25,1},{2,10},{10... | collective-permute-start | bytes 1966088 | tf_op jit(solution)/shard_map/ppermute | solution.py:26
  535.0 36.8 %collective-permute-start.104 = (bf16[320,1536]{1,0:T(8,128)(2,1)S(1)}, bf16[320,1536]{1,0:T(8,128)(2,1)S(1)}, u32[]{:S(2)}, u32[]{:S(2)}) collective-permute-start(bf16[320,1536]{1,0:T(8,128)(2,1)S(1)} %fusion.6), channel_id=1, source_target_pairs={{0,24},{8,0},{16,8},{24,16},{1,25},{9,1},{17,9},{25,17},{2,26},{10... | collective-permute-start | bytes 2949128 | tf_op jit(solution)/shard_map/ppermute | solution.py:26
  552.0 25.6 %collective-permute-start.102 = (bf16[128,2560]{1,0:T(8,128)(2,1)S(1)}, bf16[128,2560]{1,0:T(8,128)(2,1)S(1)}, u32[]{:S(2)}, u32[]{:S(2)}) collective-permute-start(bf16[128,2560]{1,0:T(8,128)(2,1)S(1)} %fusion.94), channel_id=1, source_target_pairs={{0,2},{2,0},{1,3},{3,1},{4,6},{6,4},{5,7},{7,5},{8,10},{10,8},{9,1... | collective-permute-start | bytes 1966088 | tf_op jit(solution)/shard_map/ppermute | solution.py:21
  553.3 25.1 %collective-permute-start.105 = (bf16[320,1536]{1,0:T(8,128)(2,1)}, bf16[320,1536]{1,0:T(8,128)(2,1)}, u32[]{:S(2)}, u32[]{:S(2)}) collective-permute-start(bf16[320,1536]{1,0:T(8,128)(2,1)} %get-tuple-element.637), channel_id=1, source_target_pairs={{0,4},{4,0},{1,5},{5,1},{2,6},{6,2},{3,7},{7,3},{8,12},{12,8},{9,1... | collective-permute-start | bytes 2949128 | tf_op jit(solution)/shard_map/ppermute | solution.py:21
  588.4 34.7 %collective-permute-start.114 = (bf16[128,2560]{1,0:T(8,128)(2,1)S(1)}, bf16[128,2560]{1,0:T(8,128)(2,1)S(1)}, u32[]{:S(2)}, u32[]{:S(2)}) collective-permute-start(bf16[128,2560]{1,0:T(8,128)(2,1)S(1)} %fusion.95), channel_id=1, source_target_pairs={{0,2},{2,0},{1,3},{3,1},{4,6},{6,4},{5,7},{7,5},{8,10},{10,8},{9,1... | collective-permute-start | bytes 1966088 | tf_op jit(solution)/shard_map/ppermute | solution.py:21
  596.1 27.0 %collective-permute-start.112 = (bf16[2,80,2560]{2,1,0:T(8,128)(2,1)S(1)}, bf16[2,80,2560]{2,1,0:T(8,128)(2,1)S(1)}, u32[]{:S(2)}, u32[]{:S(2)}) collective-permute-start(bf16[2,80,2560]{2,1,0:T(8,128)(2,1)S(1)} %fusion.85), channel_id=1, source_target_pairs={{0,4},{4,0},{1,5},{5,1},{2,6},{6,2},{3,7},{7,3},{8,12},{12,8},{9,1... | collective-permute-start | bytes 2457608 | tf_op jit(solution)/shard_map/ppermute | solution.py:21
  632.1 30.2 %collective-permute-start.118 = (bf16[4,4,80,1536]{3,2,1,0:T(8,128)(2,1)}, bf16[4,4,80,1536]{3,2,1,0:T(8,128)(2,1)}, u32[]{:S(2)}, u32[]{:S(2)}) collective-permute-start(bf16[4,4,80,1536]{3,2,1,0:T(8,128)(2,1)} %get-tuple-element.670), channel_id=1, source_target_pairs={{0,1},{1,0},{2,3},{3,2},{4,5},{5,4},{6,7},{7,6},{8,9},{9,8},{10,11... | collective-permute-start | bytes 11796488 | tf_op jit(solution)/shard_map/ppermute | solution.py:21
  632.1 30.2 %collective-permute-start.119 = (bf16[2,4,80,2560]{3,2,1,0:T(8,128)(2,1)}, bf16[2,4,80,2560]{3,2,1,0:T(8,128)(2,1)}, u32[]{:S(2)}, u32[]{:S(2)}) collective-permute-start(bf16[2,4,80,2560]{3,2,1,0:T(8,128)(2,1)} %get-tuple-element.671), channel_id=1, source_target_pairs={{0,1},{1,0},{2,3},{3,2},{4,5},{5,4},{6,7},{7,6},{8,9},{9,8},{10,11... | collective-permute-start | bytes 9830408 | tf_op jit(solution)/shard_map/ppermute | solution.py:21
  643.9 72.2 %collective-permute-start.125 = (bf16[320,1536]{1,0:T(8,128)(2,1)}, bf16[320,1536]{1,0:T(8,128)(2,1)S(1)}, u32[]{:S(2)}, u32[]{:S(2)}) collective-permute-start(bf16[320,1536]{1,0:T(8,128)(2,1)} %fusion.5), channel_id=1, source_target_pairs={{0,8},{8,16},{16,24},{24,0},{1,9},{9,17},{17,25},{25,1},{2,10},{10... | collective-permute-start | bytes 2949128 | tf_op jit(solution)/shard_map/ppermute | solution.py:26
  665.5 50.6 %collective-permute-start.121 = (bf16[2,80,2560]{2,1,0:T(8,128)(2,1)}, bf16[2,80,2560]{2,1,0:T(8,128)(2,1)}, u32[]{:S(2)}, u32[]{:S(2)}) collective-permute-start(bf16[2,80,2560]{2,1,0:T(8,128)(2,1)} %get-tuple-element.745), channel_id=1, source_target_pairs={{0,4},{4,0},{1,5},{5,1},{2,6},{6,2},{3,7},{7,3},{8,12},{12,8},{9,1... | collective-permute-start | bytes 2457608 | tf_op jit(solution)/shard_map/ppermute | solution.py:21
  669.8 43.9 %collective-permute-start.122 = (bf16[288,2560]{1,0:T(8,128)(2,1)}, bf16[288,2560]{1,0:T(8,128)(2,1)}, u32[]{:S(2)}, u32[]{:S(2)}) collective-permute-start(bf16[288,2560]{1,0:T(8,128)(2,1)} %pad_maximum_fusion), channel_id=1, source_target_pairs={{0,8},{8,16},{16,24},{24,0},{1,9},{9,17},{17,25},{25,1},{2,10},{10... | collective-permute-start | bytes 4423688 | tf_op jit(solution)/shard_map/ppermute | solution.py:26
  672.6 31.9 %collective-permute-start.123 = (bf16[2,2,80,1536]{3,2,1,0:T(8,128)(2,1)}, bf16[2,2,80,1536]{3,2,1,0:T(8,128)(2,1)S(1)}, u32[]{:S(2)}, u32[]{:S(2)}) collective-permute-start(bf16[2,2,80,1536]{3,2,1,0:T(8,128)(2,1)} %pad_maximum_fusion.12), channel_id=1, source_target_pairs={{0,4},{4,0},{1,5},{5,1},{2,6},{6,2},{3,7},{7,3},{8,12},{12,8},{9,1... | collective-permute-start | bytes 2949128 | tf_op jit(solution)/shard_map/ppermute | solution.py:21
  680.8 35.2 %collective-permute-start.124 = (bf16[128,2560]{1,0:T(8,128)(2,1)S(1)}, bf16[128,2560]{1,0:T(8,128)(2,1)S(1)}, u32[]{:S(2)}, u32[]{:S(2)}) collective-permute-start(bf16[128,2560]{1,0:T(8,128)(2,1)S(1)} %slice.914), channel_id=1, source_target_pairs={{0,2},{2,0},{1,3},{3,1},{4,6},{6,4},{5,7},{7,5},{8,10},{10,8},{9,1... | collective-permute-start | bytes 1966088 | tf_op jit(solution)/shard_map/ppermute | solution.py:21
  704.5 53.8 %collective-permute-start.120 = (bf16[2,80,2560]{2,1,0:T(8,128)(2,1)}, bf16[2,80,2560]{2,1,0:T(8,128)(2,1)}, u32[]{:S(2)}, u32[]{:S(2)}) collective-permute-start(bf16[2,80,2560]{2,1,0:T(8,128)(2,1)} %get-tuple-element.746), channel_id=1, source_target_pairs={{0,4},{4,0},{1,5},{5,1},{2,6},{6,2},{3,7},{7,3},{8,12},{12,8},{9,1... | collective-permute-start | bytes 2457608 | tf_op jit(solution)/shard_map/ppermute | solution.py:21
  721.0 37.2 %collective-permute-start.126 = (bf16[288,2560]{1,0:T(8,128)(2,1)}, bf16[288,2560]{1,0:T(8,128)(2,1)S(1)}, u32[]{:S(2)}, u32[]{:S(2)}) collective-permute-start(bf16[288,2560]{1,0:T(8,128)(2,1)} %pad_maximum_fusion.1), channel_id=1, source_target_pairs={{0,8},{8,16},{16,24},{24,0},{1,9},{9,17},{17,25},{25,1},{2,10},{10... | collective-permute-start | bytes 4423688 | tf_op jit(solution)/shard_map/ppermute | solution.py:26
  727.3 39.3 %collective-permute-start.128 = (bf16[2,80,1536]{2,1,0:T(8,128)(2,1)S(1)}, bf16[2,80,1536]{2,1,0:T(8,128)(2,1)S(1)}, u32[]{:S(2)}, u32[]{:S(2)}) collective-permute-start(bf16[2,80,1536]{2,1,0:T(8,128)(2,1)S(1)} %fusion.84), channel_id=1, source_target_pairs={{0,8},{8,16},{16,24},{24,0},{1,9},{9,17},{17,25},{25,1},{2,10},{10... | collective-permute-start | bytes 1474568 | tf_op jit(solution)/shard_map/ppermute | solution.py:26
  728.2 47.6 %collective-permute-start.132 = (bf16[320,1536]{1,0:T(8,128)(2,1)S(1)}, bf16[320,1536]{1,0:T(8,128)(2,1)S(1)}, u32[]{:S(2)}, u32[]{:S(2)}) collective-permute-start(bf16[320,1536]{1,0:T(8,128)(2,1)S(1)} %copy-done.90), channel_id=1, source_target_pairs={{0,4},{4,0},{1,5},{5,1},{2,6},{6,2},{3,7},{7,3},{8,12},{12,8},{9,1... | collective-permute-start | bytes 2949128 | tf_op jit(solution)/shard_map/ppermute | solution.py:21
  782.6 31.7 %collective-permute-start.133 = (bf16[2,80,1536]{2,1,0:T(8,128)(2,1)S(1)}, bf16[2,80,1536]{2,1,0:T(8,128)(2,1)S(1)}, u32[]{:S(2)}, u32[]{:S(2)}) collective-permute-start(bf16[2,80,1536]{2,1,0:T(8,128)(2,1)S(1)} %fusion.81), channel_id=1, source_target_pairs={{0,8},{8,16},{16,24},{24,0},{1,9},{9,17},{17,25},{25,1},{2,10},{10... | collective-permute-start | bytes 1474568 | tf_op jit(solution)/shard_map/ppermute | solution.py:26
  785.0 29.4 %collective-permute-start.137 = (bf16[80,1280]{1,0:T(8,128)(2,1)S(1)}, bf16[80,1280]{1,0:T(8,128)(2,1)S(1)}, u32[]{:S(2)}, u32[]{:S(2)}) collective-permute-start(bf16[80,1280]{1,0:T(8,128)(2,1)S(1)} %get-tuple-element.790), channel_id=1, source_target_pairs={{16,0},{0,2},{24,8},{8,10},{18,16},{2,18},{26,24},{10,26},{17,1},{... | collective-permute-start | bytes 614408 | tf_op jit(solution)/shard_map/ppermute | solution.py:846
  (247 other events, 3433.9 us)
